TPU v7x, 32 devices: a whole 2x2x4 slice. The times are simulated.
32 devices in a mesh: dp: 4 (over y, x), expert: 8 (over z, core).
Axes of the slice: x: 2, y: 2, z: 4, core: 2. Of those that a mesh axis runs over, the one named last changes fastest.
Arguments:
- tokens: bfloat16 [4096, 2048], P(('dp', 'expert')), may hold values from -6 to 6
- expert_ids: int32 [4096, 8], P(('dp', 'expert')), may hold values from 0 to 15, all different within a row
- bucket_codes: int32 [4096, 8], P(('dp', 'expert')), may hold values from 0 to 65535
- route_weights: float32 [4096, 8], P(('dp', 'expert')), may hold values from 0.1 to 1
- cotangent: bfloat16 [4096, 2048], P(('dp', 'expert')), may hold values from -2 to 2
- counts: int32 [16], replicated, may hold values from 4 to 16, as said below
- comp_scale: bfloat16 [16, 2048], replicated, may hold values from -3 to 3
- w_gate: bfloat16 [16, 2048, 768], P('expert'), may hold values from -0.125 to 0.125
- w_up: bfloat16 [16, 2048, 768], P('expert'), may hold values from -0.125 to 0.125
- w_down: bfloat16 [16, 768, 2048], P('expert'), may hold values from -0.21875 to 0.21875
Outputs:
- layer_output: bfloat16 [4096, 2048], P(('dp', 'expert'))
- grad_tokens: bfloat16 [4096, 2048], P(('dp', 'expert'))
- grad_down: bfloat16 [16, 768, 2048], P('expert', None, 'dp')
Inputs may be any that keep to these rules, and one draw needn't show every extreme that they name: `counts`: experts 2i and 2i+1 (those of index i of the expert axis) have 20 buckets together; some expert has exactly 16. `expert_ids`: the 8 experts of one token differ.
All inputs are finite; a program needn't handle non-finite values.
Results may differ from a plain program's by a relative error of at most 0.013.
Values may be sent and summed in bfloat16 or wider, within the bound.
No kernel may reach another device: no remote copies, remote signals or barrier semaphores. Data moves between devices by JAX's collectives and lax.ppermute only.
A program may use at most 192 MiB of HBM per device.

v0:
```python
import jax
import jax.numpy as jnp
from jax import lax
from jax.sharding import PartitionSpec as P

NB = 16


def expert_forward(arrived, w_gate, w_up, w_down):
    gate_act = jnp.einsum("qjbd,jdf->jqbf", arrived, w_gate, preferred_element_type=jnp.float32)
    up_act = jnp.einsum("qjbd,jdf->jqbf", arrived, w_up, preferred_element_type=jnp.float32)
    hidden = (gate_act * jax.nn.sigmoid(gate_act) * up_act).astype(jnp.bfloat16)
    expert_out = jnp.einsum(
        "jqbf,jfd->qjbd", hidden, w_down, preferred_element_type=jnp.float32
    ).astype(jnp.bfloat16)
    return (gate_act, up_act, hidden, expert_out)


def expert_backward(pull_rows, gate_act, up_act, hidden, w_gate, w_up, w_down):
    d_hidden = jnp.einsum("qjbd,jfd->jqbf", pull_rows, w_down, preferred_element_type=jnp.float32)
    gate_sigmoid = jax.nn.sigmoid(gate_act)
    d_gate = (d_hidden * up_act * gate_sigmoid * (1.0 + gate_act * (1.0 - gate_sigmoid))).astype(
        jnp.bfloat16
    )
    d_up = (d_hidden * gate_act * gate_sigmoid).astype(jnp.bfloat16)
    back_rows = (
        jnp.einsum("jqbf,jdf->qjbd", d_gate, w_gate, preferred_element_type=jnp.float32)
        + jnp.einsum("jqbf,jdf->qjbd", d_up, w_up, preferred_element_type=jnp.float32)
    ).astype(jnp.bfloat16)
    reduced = lax.psum_scatter(
        jnp.einsum("jqbf,qjbd->djf", hidden, pull_rows, preferred_element_type=jnp.float32).astype(
            jnp.bfloat16
        ),
        "dp",
        scatter_dimension=0,
        tiled=True,
    ).astype(jnp.float32)
    grad_down = jnp.transpose(reduced, (1, 2, 0)).astype(jnp.bfloat16)
    return (back_rows, grad_down)


def on_device(
    tokens,
    expert_ids,
    bucket_codes,
    route_weights,
    cotangent,
    counts,
    comp_scale,
    w_gate,
    w_up,
    w_down,
):
    model_width = tokens.shape[1]
    tok_count = tokens.shape[0]
    pick_count = expert_ids.shape[1]
    expert_total = counts.shape[0]
    local_count = w_gate.shape[0]
    group_count = lax.axis_size("expert")
    slot_total = expert_total * NB
    expert_hit = (expert_ids[:, :, None] == jnp.arange(expert_total, dtype=jnp.int32)).astype(
        jnp.int32
    )
    pair_count = jnp.sum(expert_hit * counts[None, None, :], axis=2)
    slot_id = expert_ids * NB + bucket_codes % pair_count
    slot_hit = (slot_id[:, :, None] == jnp.arange(slot_total, dtype=jnp.int32)).astype(jnp.float32)
    member = jnp.sum(slot_hit, axis=1).T
    occupancy = jnp.sum(member, axis=1)
    divisor = jnp.maximum(occupancy, 1.0)[:, None]
    bucket_sums = jnp.dot(member.astype(jnp.bfloat16), tokens, preferred_element_type=jnp.float32)
    centroid = (bucket_sums / divisor).astype(jnp.bfloat16)
    flat_slots = slot_id.reshape(tok_count * pick_count)
    pair_pull = (route_weights[:, :, None] * cotangent.astype(jnp.float32)[:, None, :]).reshape(
        tok_count * pick_count, model_width
    )
    pull_sum = jax.ops.segment_sum(pair_pull, flat_slots, num_segments=slot_total).astype(
        jnp.bfloat16
    )
    gain_mix = jnp.sum(expert_hit.astype(jnp.float32) * route_weights[:, :, None], axis=1)
    gain_token = jnp.dot(gain_mix, comp_scale.astype(jnp.float32), precision=lax.Precision.HIGHEST)

    def source_out(values):
        return values.reshape(group_count, local_count * NB, model_width)

    def owner_in(received):
        return received.reshape(group_count, local_count, NB, model_width)

    def owner_out(values):
        return values.reshape(group_count, local_count * NB, model_width)

    def source_in(received):
        return received.reshape(slot_total, model_width)

    arrived = owner_in(
        lax.all_to_all(source_out(centroid), "expert", split_axis=0, concat_axis=0, tiled=True)
    )
    gate_act, up_act, hidden, expert_out = expert_forward(arrived, w_gate, w_up, w_down)
    got_out = lax.all_to_all(
        owner_out(expert_out), "expert", split_axis=0, concat_axis=0, tiled=True
    )
    pull_rows = owner_in(
        lax.all_to_all(source_out(pull_sum), "expert", split_axis=0, concat_axis=0, tiled=True)
    )
    back_rows, grad_down = expert_backward(
        pull_rows, gate_act, up_act, hidden, w_gate, w_up, w_down
    )
    got_back = lax.all_to_all(
        owner_out(back_rows), "expert", split_axis=0, concat_axis=0, tiled=True
    )
    slot_out = source_in(got_out)
    slot_back = source_in(got_back)
    scale_slot = jnp.repeat(comp_scale.astype(jnp.float32), NB, axis=0)
    combined = slot_out.astype(jnp.float32) - scale_slot * centroid.astype(jnp.float32)
    layer_pairs = route_weights[:, :, None] * combined[slot_id]
    layer_output = (jnp.sum(layer_pairs, axis=1) + gain_token * tokens.astype(jnp.float32)).astype(
        jnp.bfloat16
    )
    correction = (
        slot_back.astype(jnp.float32) - scale_slot * pull_sum.astype(jnp.float32)
    ) / divisor
    grad_tokens = (
        jnp.sum(correction[slot_id], axis=1) + gain_token * cotangent.astype(jnp.float32)
    ).astype(jnp.bfloat16)
    return (layer_output, grad_tokens, grad_down)


def solution(mesh):
    in_specs = (
        P(("dp", "expert"), None),
        P(("dp", "expert"), None),
        P(("dp", "expert"), None),
        P(("dp", "expert"), None),
        P(("dp", "expert"), None),
        P(),
        P(),
        P("expert", None, None),
        P("expert", None, None),
        P("expert", None, None),
    )
    out_specs = (P(("dp", "expert"), None), P(("dp", "expert"), None), P("expert", None, "dp"))
    return jax.shard_map(
        on_device, mesh=mesh, in_specs=in_specs, out_specs=out_specs, check_vma=False
    )
```

profile of v0, /device:TPU:0, one launch (start us, length us, event | category | flops | bytes accessed | tf_op | source)
XLA Modules:
  0.0 197.7 jit_solution(18289397907189265137)
XLA Ops:
  7.2 0.8 select_reduce_fusion
  8.0 0.8 compare_select_fusion
  9.0 0.4 convert_reduce_fusion.1
  9.4 2.5 %fusion.20 = bf16[256,2048]{1,0:T(8,128)(2,1)} fusion(bf16[128,2048]{1,0:T(8,128)(2,1)} %param.10, f32[256]{0:T(256)S(1)} %broadcast_maximum_fusion, bf16[128,256]{1,0:T(8,128)(2,1)S(1)} %get-tuple-element.12), kind=kOutput, calls=%fused_computation.28 | convolution fusion | flops 135266304 | bytes 1639424 | tf_op jit(solution)/shard_map/dot_general | solution.py:70
  11.9 6.3 %all-to-all-start = ((bf16[8,32,2048]{2,1,0:T(8,128)(2,1)}), bf16[8,32,2048]{2,1,0:T(8,128)(2,1)S(1)}, u32[]{:S(2)}, u32[]{:S(2)}) async-start(bf16[8,32,2048]{2,1,0:T(8,128)(2,1)} %bitcast), calls=%async_computation | async-start | bytes 2097152 | tf_op jit(solution)/shard_map/all_to_all | solution.py:95
  18.5 0.5 copy-done.7
  19.1 1.1 convert_element_type.100
  20.1 14.9 %scatter_custom_fusion = f32[256,2048]{1,0:T(8,128)S(1)} fusion(s32[1024]{0:T(1024)S(1)} %reshape.71, f32[128,2048]{1,0:T(8,128)} %convert_element_type.100, f32[1024]{0:T(1024)S(1)} %mul.96, f32[]{:T(128)} %constant.9.clone.1), kind=kCustom, calls=%fused_computation.6 | custom fusion | flops 4194304 | bytes 3149828 | tf_op jit(solution)/shard_map/scatter-add | solution.py:76
  35.0 1.2 convert_element_type.101
  36.3 8.6 %all-to-all-done = bf16[8,32,2048]{2,1,0:T(8,128)(2,1)S(1)} async-done(((bf16[8,32,2048]{2,1,0:T(8,128)(2,1)}), bf16[8,32,2048]{2,1,0:T(8,128)(2,1)S(1)}, u32[]{:S(2)}, u32[]{:S(2)}) %all-to-all-start) | async-done | bytes 1048608 | tf_op jit(solution)/shard_map/all_to_all | solution.py:95
  44.8 4.2 %all-to-all-start.2 = ((bf16[8,32,2048]{2,1,0:T(8,128)(2,1)}), bf16[8,32,2048]{2,1,0:T(8,128)(2,1)}, u32[]{:S(2)}, u32[]{:S(2)}) async-start(bf16[8,32,2048]{2,1,0:T(8,128)(2,1)} %bitcast.84), calls=%async_computation.2 | async-start | bytes 2097152 | tf_op jit(solution)/shard_map/all_to_all | solution.py:102
  49.3 3.8 %fusion.9 = f32[2,8,16,768]{3,2,1,0:T(8,128)S(1)} fusion(bf16[2,2048,768]{2,1,0:T(8,128)(2,1)} %param.17, bf16[8,2,16,2048]{3,2,1,0:T(8,128)(2,1)S(1)} %bitcast.82), kind=kOutput, calls=%fused_computation.16 | convolution fusion | flops 805306368 | bytes 8126464 | tf_op jit(solution)/shard_map/qjbd,jdf->jqbf/dot_general | solution.py:10
  53.1 0.9 copy-done.1
  54.0 4.8 %multiply_convert_fusion.2 = (bf16[2,8,16,768]{3,2,1,0:T(8,128)(2,1)S(1)}, f32[2,8,16,768]{3,2,1,0:T(8,128)}) fusion(f32[2,8,16,768]{3,2,1,0:T(8,128)S(1)} %fusion.9, bf16[2,2048,768]{2,1,0:T(8,128)(2,1)} %param.18, bf16[8,2,16,2048]{3,2,1,0:T(8,128)(2,1)S(1)} %bitcast.83), kind=kOutput, calls=%fused_computation.47 | convolution fusion | flops 806486016 | bytes 9306112 | tf_op jit(solution)/shard_map/qjbd,jdf->jqbf/dot_general | solution.py:11
  58.8 16.9 %all-to-all-done.2 = bf16[8,32,2048]{2,1,0:T(8,128)(2,1)} async-done(((bf16[8,32,2048]{2,1,0:T(8,128)(2,1)}), bf16[8,32,2048]{2,1,0:T(8,128)(2,1)}, u32[]{:S(2)}, u32[]{:S(2)}) %all-to-all-start.2) | async-done | bytes 1048608 | tf_op jit(solution)/shard_map/all_to_all | solution.py:102
  75.7 5.7 %fusion.2 = bf16[2048,2,768]{2,0,1:T(8,128)(2,1)} fusion(bf16[8,2,16,2048]{3,2,1,0:T(8,128)(2,1)} %bitcast.15, bf16[2,8,16,768]{3,2,1,0:T(8,128)(2,1)S(1)} %get-tuple-element.20), kind=kOutput, calls=%fused_computation.9 | convolution fusion | flops 808452096 | bytes 7733248 | tf_op jit(solution)/shard_map/jqbf,qjbd->djf/dot_general | solution.py:31
  81.4 5.5 %fusion.11 = f32[2,8,16,768]{3,2,1,0:T(8,128)S(1)} fusion(bf16[2,768,2048]{2,1,0:T(8,128)(2,1)} %param.19, bf16[8,2,16,2048]{3,2,1,0:T(8,128)(2,1)} %bitcast.15), kind=kOutput, calls=%fused_computation.18 | convolution fusion | flops 805306368 | bytes 8126464 | tf_op jit(solution)/shard_map/qjbd,jfd->jqbf/dot_general | solution.py:20
  86.9 5.4 %fusion.3 = f32[2,8,16,2048]{3,2,1,0:T(8,128)S(1)} fusion(bf16[2,2048,768]{2,1,0:T(8,128)(2,1)} %param.18, f32[2,8,16,768]{3,2,1,0:T(8,128)S(1)} %fusion.11, f32[2,8,16,768]{3,2,1,0:T(8,128)S(1)} %copy-done.2), kind=kOutput, calls=%fused_computation.10 | convolution fusion | flops 806486016 | bytes 9961472 | tf_op jit(solution)/shard_map/jqbf,jdf->qjbd/dot_general | solution.py:28
  92.3 2.2 %fusion.30 = bf16[8,2,16,2048]{3,2,0,1:T(8,128)(2,1)S(1)} fusion(f32[2,8,16,2048]{3,2,1,0:T(8,128)S(1)} %fusion.3, bf16[2,2048,768]{2,1,0:T(8,128)(2,1)S(1)} %bitcast.81, f32[2,8,16,768]{3,2,1,0:T(8,128)S(1)} %copy-done.2, f32[2,8,16,768]{3,2,1,0:T(8,128)S(1)} %fusion.11, f32[2,8,16,768]{3,2,1,0:T(8,128)S(1)} %copy-done.6), kind=kOutput, calls=%fused_computation.32 | convolution fusion | flops 808321024 | bytes 11796480 | tf_op jit(solution)/shard_map/jqbf,jdf->qjbd/dot_general | solution.py:27
  94.5 1.0 copy.41
  95.5 3.6 %all-to-all-start.3 = ((bf16[8,32,2048]{2,1,0:T(8,128)(2,1)}), bf16[8,32,2048]{2,1,0:T(8,128)(2,1)S(1)}, u32[]{:S(2)}, u32[]{:S(2)}) async-start(bf16[8,32,2048]{2,1,0:T(8,128)(2,1)} %bitcast.20), calls=%async_computation.3 | async-start | bytes 2097152 | tf_op jit(solution)/shard_map/all_to_all | solution.py:107
  99.1 4.0 %fusion.27 = bf16[8,2,16,2048]{3,2,0,1:T(8,128)(2,1)S(1)} fusion(bf16[2,8,16,768]{3,2,1,0:T(8,128)(2,1)S(1)} %get-tuple-element.20, bf16[2,768,2048]{2,1,0:T(8,128)(2,1)} %param.19), kind=kOutput, calls=%fused_computation.31 | convolution fusion | flops 805830656 | bytes 7733248 | tf_op jit(solution)/shard_map/jqbf,jfd->qjbd/dot_general | solution.py:13
  103.1 1.1 copy.36
  104.2 21.4 %all-to-all-done.3 = bf16[8,32,2048]{2,1,0:T(8,128)(2,1)S(1)} async-done(((bf16[8,32,2048]{2,1,0:T(8,128)(2,1)}), bf16[8,32,2048]{2,1,0:T(8,128)(2,1)S(1)}, u32[]{:S(2)}, u32[]{:S(2)}) %all-to-all-start.3) | async-done | bytes 1048608 | tf_op jit(solution)/shard_map/all_to_all | solution.py:107
  125.6 3.8 %all-to-all-start.1 = ((bf16[8,32,2048]{2,1,0:T(8,128)(2,1)}), bf16[8,32,2048]{2,1,0:T(8,128)(2,1)S(1)}, u32[]{:S(2)}, u32[]{:S(2)}) async-start(bf16[8,32,2048]{2,1,0:T(8,128)(2,1)} %bitcast.9), calls=%async_computation.1 | async-start | bytes 2097152 | tf_op jit(solution)/shard_map/all_to_all | solution.py:98
  129.7 26.0 %all-to-all-done.1 = bf16[8,32,2048]{2,1,0:T(8,128)(2,1)S(1)} async-done(((bf16[8,32,2048]{2,1,0:T(8,128)(2,1)}), bf16[8,32,2048]{2,1,0:T(8,128)(2,1)S(1)}, u32[]{:S(2)}, u32[]{:S(2)}) %all-to-all-start.1) | async-done | bytes 1048608 | tf_op jit(solution)/shard_map/all_to_all | solution.py:98
  155.7 4.5 %fusion.35 = (f32[256,2048]{1,0:T(8,128)S(1)}, f32[256,2048]{1,0:T(8,128)}) fusion(bf16[8,32,2048]{2,1,0:T(8,128)(2,1)} %copy-done.3, f32[16,2048]{1,0:T(8,128)S(1)} %convert_element_type.94, f32[256]{0:T(256)S(1)} %broadcast_maximum_fusion, bf16[256,2048]{1,0:T(8,128)(2,1)} %fusion.20, bf16[8,32,2048]{2,1,0:T(8,128)(2,1)S(1)} %all-to-all-done.1, ...), kind=kLoop, calls=%fused_computation.35 | loop fusion | flops 5242880 | bytes 9569280 | tf_op jit(solution)/shard_map/div | solution.py:118
  160.2 10.6 %gather_fusion = f32[1024,2048]{1,0:T(8,128)} fusion(f32[256,2048]{1,0:T(8,128)} %get-tuple-element.19, s32[1024]{0:T(1024)S(1)} %broadcast_clamp_fusion), kind=kCustom, calls=%fused_computation | custom fusion | bytes 16781312 | tf_op jit(solution)/shard_map/gather | solution.py:114
  170.7 6.9 %gather_fusion.1 = f32[1024,2048]{1,0:T(8,128)} fusion(f32[256,2048]{1,0:T(8,128)S(1)} %get-tuple-element.18, s32[1024]{0:T(1024)S(1)} %broadcast_clamp_fusion), kind=kCustom, calls=%fused_computation.1 | custom fusion | bytes 16781312 | tf_op jit(solution)/shard_map/gather | solution.py:122
  177.6 8.7 %bitcast_reduce_fusion = (f32[128,2048]{1,0:T(8,128)S(1)}, f32[128,2048]{1,0:T(8,128)S(1)}) fusion(f32[1024,2048]{1,0:T(8,128)} %gather_fusion.1, f32[1024,2048]{1,0:T(8,128)} %gather_fusion, f32[128,8]{1,0:T(8,128)S(1)} %copy-done.8), kind=kLoop, calls=%fused_computation.4 | loop fusion | flops 5767168 | bytes 18878464 | tf_op jit(solution)/shard_map/reduce_sum | solution.py:122
  186.4 1.8 add_convert_fusion
  188.2 2.6 %copy.43 = bf16[2,768,512]{2,1,0:T(8,128)(2,1)} copy(bf16[2,768,512]{1,2,0:T(8,128)(2,1)} %bitcast.85) | data formatting | bytes 3145728
  (44 shorter events, 0.9 us)
Async XLA Ops:
  7.2 11.2 %copy-start.13 = (f32[128,8]{0,1:T(8,128)S(1)}, f32[128,8]{0,1:T(8,128)}, u32[]{:S(2)}) copy-start(f32[128,8]{0,1:T(8,128)} %param.13) | copy-start | bytes 12292
  7.2 11.9 %copy-start.4 = (bf16[128,2048]{1,0:T(8,128)(2,1)S(1)}, bf16[128,2048]{1,0:T(8,128)(2,1)}, u32[]{:S(2)}) copy-start(bf16[128,2048]{1,0:T(8,128)(2,1)} %param.14) | copy-start | bytes 1572868
  11.9 32.9 %all-to-all-start = ((bf16[8,32,2048]{2,1,0:T(8,128)(2,1)}), bf16[8,32,2048]{2,1,0:T(8,128)(2,1)S(1)}, u32[]{:S(2)}, u32[]{:S(2)}) async-start(bf16[8,32,2048]{2,1,0:T(8,128)(2,1)} %bitcast), calls=%async_computation | async-start | bytes 2097152 | tf_op jit(solution)/shard_map/all_to_all | solution.py:95
  18.4 0.6 copy-start.7
  35.0 18.1 %copy-start = (f32[256,2048]{1,0:T(8,128)}, f32[256,2048]{1,0:T(8,128)S(1)}, u32[]{:S(2)}) copy-start(f32[256,2048]{1,0:T(8,128)S(1)} %scatter_custom_fusion) | copy-start | bytes 6291460
  44.8 30.8 %all-to-all-start.2 = ((bf16[8,32,2048]{2,1,0:T(8,128)(2,1)}), bf16[8,32,2048]{2,1,0:T(8,128)(2,1)}, u32[]{:S(2)}, u32[]{:S(2)}) async-start(bf16[8,32,2048]{2,1,0:T(8,128)(2,1)} %bitcast.84), calls=%async_computation.2 | async-start | bytes 2097152 | tf_op jit(solution)/shard_map/all_to_all | solution.py:102
  49.1 139.1 %reduce-scatter.2.cloned.1.call-start = ((), (), s32[]{:S(2)}) async-start(), calls=%async_computation.5 | async-start | bytes 7864320 | tf_op jit(solution)/shard_map/reduce_scatter | solution.py:30
  53.1 0.9 copy-start.1
  81.4 5.5 %copy-start.2 = (f32[2,8,16,768]{3,2,1,0:T(8,128)S(1)}, f32[2,8,16,768]{3,2,1,0:T(8,128)}, u32[]{:S(2)}) copy-start(f32[2,8,16,768]{3,2,1,0:T(8,128)} %copy-done.1) | copy-start | bytes 2359300
  81.4 10.9 %slice-start = ((s8[6291456]{0:T(1024)(128)(4,1)}), s8[4194304]{0:T(1024)(128)(4,1)S(1)}, s32[]{:S(2)}) async-start(s8[6291456]{0:T(1024)(128)(4,1)} %bitcast.80), calls=%async_computation.6 | async-start | bytes 8388608
  86.9 5.4 %slice-start.1 = ((s8[6291456]{0:T(1024)(128)(4,1)}), s8[2097152]{0:T(1024)(128)(4,1)S(1)}, s32[]{:S(2)}) async-start(s8[6291456]{0:T(1024)(128)(4,1)} %bitcast.80), calls=%async_computation.7 | async-start | bytes 4194304
  86.9 5.4 %copy-start.6 = (f32[2,8,16,768]{3,2,1,0:T(8,128)S(1)}, f32[2,8,16,768]{3,2,1,0:T(8,128)}, u32[]{:S(2)}) copy-start(f32[2,8,16,768]{3,2,1,0:T(8,128)} %get-tuple-element.21) | copy-start | bytes 2359300
  95.5 30.1 %all-to-all-start.3 = ((bf16[8,32,2048]{2,1,0:T(8,128)(2,1)}), bf16[8,32,2048]{2,1,0:T(8,128)(2,1)S(1)}, u32[]{:S(2)}, u32[]{:S(2)}) async-start(bf16[8,32,2048]{2,1,0:T(8,128)(2,1)} %bitcast.20), calls=%async_computation.3 | async-start | bytes 2097152 | tf_op jit(solution)/shard_map/all_to_all | solution.py:107
  99.1 30.3 %copy-start.10 = (bf16[16,2048]{1,0:T(8,128)(2,1)S(1)}, bf16[16,2048]{1,0:T(8,128)(2,1)}, u32[]{:S(2)}) copy-start(bf16[16,2048]{1,0:T(8,128)(2,1)} %param.16) | copy-start | bytes 196612
  99.1 30.5 %copy-start.12 = (s32[128,8]{0,1:T(8,128)S(1)}, s32[128,8]{0,1:T(8,128)}, u32[]{:S(2)}) copy-start(s32[128,8]{0,1:T(8,128)} %param.11) | copy-start | bytes 12292
  125.6 4.1 %copy-start.3 = (bf16[8,32,2048]{2,1,0:T(8,128)(2,1)}, bf16[8,32,2048]{2,1,0:T(8,128)(2,1)S(1)}, u32[]{:S(2)}) copy-start(bf16[8,32,2048]{2,1,0:T(8,128)(2,1)S(1)} %all-to-all-done.3) | copy-start | bytes 3145732
  125.6 30.1 %all-to-all-start.1 = ((bf16[8,32,2048]{2,1,0:T(8,128)(2,1)}), bf16[8,32,2048]{2,1,0:T(8,128)(2,1)S(1)}, u32[]{:S(2)}, u32[]{:S(2)}) async-start(bf16[8,32,2048]{2,1,0:T(8,128)(2,1)} %bitcast.9), calls=%async_computation.1 | async-start | bytes 2097152 | tf_op jit(solution)/shard_map/all_to_all | solution.py:98
  170.7 6.9 %copy-start.8 = (f32[128,8]{1,0:T(8,128)S(1)}, f32[128,8]{1,0:T(8,128)}, u32[]{:S(2)}) copy-start(f32[128,8]{1,0:T(8,128)} %copy-done.7) | copy-start | bytes 12292
  177.6 8.8 %copy-start.5 = (bf16[128,2048]{1,0:T(8,128)(2,1)S(1)}, bf16[128,2048]{1,0:T(8,128)(2,1)}, u32[]{:S(2)}) copy-start(bf16[128,2048]{1,0:T(8,128)(2,1)} %param.14) | copy-start | bytes 1572868
  177.6 8.8 %copy-start.9 = (bf16[128,2048]{1,0:T(8,128)(2,1)S(1)}, bf16[128,2048]{1,0:T(8,128)(2,1)}, u32[]{:S(2)}) copy-start(bf16[128,2048]{1,0:T(8,128)(2,1)} %param.10) | copy-start | bytes 1572868
  177.6 8.8 %copy-start.11 = (bf16[16,2048]{1,0:T(8,128)(2,1)S(1)}, bf16[16,2048]{1,0:T(8,128)(2,1)}, u32[]{:S(2)}) copy-start(bf16[16,2048]{1,0:T(8,128)(2,1)} %param.16) | copy-start | bytes 196612
Sparse Core Ops, SparseCore 0:
  81.5 69.0 reduce-scatter.1
where the time goes:
time: 198 us
  waiting for transfers between devices  72.9 us (37%)
  matrix products  35.6 us (18%)
  other arithmetic  32.6 us (16%)
  local copies, waits for them, and re-layouts  24.2 us (12%)
  starting transfers between devices  18.1 us (9%)
  between operations  14.3 us (7%)
    all_to_all x1, waiting for transfers between devices, on_device(): lax.all_to_all(owner_out(expert_out), 'expert', split_axis=0, concat_axis...  26 us
    all_to_all x1, waiting for transfers between devices, on_device(): lax.all_to_all(owner_out(back_rows), 'expert', split_axis=0, concat_axis=...  21.4 us
    all_to_all x1, waiting for transfers between devices, on_device(): lax.all_to_all(source_out(pull_sum), 'expert', split_axis=0, concat_axis=...  16.9 us
    scatter-add x1, other arithmetic, on_device(): jax.ops.segment_sum(pair_pull, flat_slots, num_segments=slot_total)  14.9 us
    gather x1, local copies, waits for them, and re-layouts, on_device(): layer_pairs = route_weights[:, :, None] * combined[slot_id]  10.6 us
    reduce_sum x1, other arithmetic, on_device(): jnp.sum(correction[slot_id], axis=1)  8.74 us
    all_to_all x1, waiting for transfers between devices, on_device(): lax.all_to_all(source_out(centroid), 'expert', split_axis=0, concat_axis=...  8.55 us
    gather x1, local copies, waits for them, and re-layouts, on_device(): correction[slot_id]  6.86 us
  transfers between devices with their start and end apart: 5, of which 4 were waited for; matrix products, arithmetic and copies ran while one was open for 39% of the time, Pallas kernels for 0%

commit v1 on v0

v1 whole, which is shorter than its diff:
```python
import functools

import jax
import jax.numpy as jnp
from jax import lax
from jax.experimental import pallas as pl
from jax.experimental.pallas import tpu as pltpu
from jax.sharding import PartitionSpec as P

PAIR_ROWS = 20
HALVES = 2
BLOCK_ROWS = HALVES * PAIR_ROWS
CHUNK = 8
FF_TILE = 256
VMEM_LIMIT = 48 * 1024 * 1024
F32 = jnp.float32
BF16 = jnp.bfloat16

NN = (((1,), (0,)), ((), ()))
NT = (((1,), (1,)), ((), ()))
TN = (((0,), (0,)), ((), ()))


def mm(a, b, dims=NN):
    return lax.dot_general(a, b, dims, preferred_element_type=F32)


def iota(shape, dim):
    return lax.broadcasted_iota(jnp.int32, shape, dim)


def over_pair_rows(index):
    return jnp.floor((index.astype(F32) + 0.5) * (1.0 / PAIR_ROWS)).astype(jnp.int32)


def pair_rows_of(ids, codes, counts_ref, group):
    count = jnp.zeros_like(ids)
    base = jnp.zeros_like(ids)
    for expert in range(counts_ref.shape[0]):
        hit = ids == expert
        count = jnp.where(hit, counts_ref[expert], count)
        if expert % 2:
            base = jnp.where(hit, counts_ref[expert - 1], base)
    laps = jnp.floor((codes.astype(F32) + 0.5) / count.astype(F32)).astype(jnp.int32)
    bucket = codes - laps * count
    return ((ids >> 1) ^ group) * BLOCK_ROWS + base + bucket


def membership(rows, total, values):
    picks, tokens = rows.shape
    index = iota((total, tokens), 0)
    parts = []
    for half in range(HALVES):
        part = jnp.zeros((total, tokens), F32)
        for pick in range(picks):
            hit = index == rows[pick : pick + 1, :] + half * PAIR_ROWS
            value = 1.0 if values is None else values[pick : pick + 1, :]
            part = jnp.where(hit, value, part)
        parts.append(part)
    return jnp.concatenate(parts, axis=1)


def split_halves(x):
    width = x.shape[1] // HALVES
    return jnp.concatenate([x[:, :width], x[:, width:]], axis=0)


def unpack_rows(blocks):
    flat = jnp.concatenate([b[...] for b in blocks], axis=0)
    rows = len(blocks) * PAIR_ROWS
    shape = (rows, len(blocks) * BLOCK_ROWS)
    row = iota(shape, 0)
    start = row + PAIR_ROWS * over_pair_rows(row)
    col = iota(shape, 1)
    out = []
    for half in range(HALVES):
        pick = (col == start + half * PAIR_ROWS).astype(F32).astype(BF16)
        out.append(mm(pick, flat).astype(BF16))
    return jnp.concatenate(out, axis=1)


def pack_rows(x, blocks):
    rows = len(blocks) * PAIR_ROWS
    total = len(blocks) * BLOCK_ROWS
    row = iota((total, rows), 0)
    col = iota((total, rows), 1)
    start = col + PAIR_ROWS * over_pair_rows(col)
    pick = jnp.concatenate(
        [(row == start + half * PAIR_ROWS).astype(F32) for half in range(HALVES)], axis=1
    ).astype(BF16)
    out = mm(pick, split_halves(x))
    for j, block in enumerate(blocks):
        block[...] = out[j * BLOCK_ROWS : (j + 1) * BLOCK_ROWS].astype(BF16)


def first_rows(rows, counts_ref, group):
    index = iota((rows, 1), 0)
    inside = index - PAIR_ROWS * over_pair_rows(index)
    return inside < counts_ref[2 * group]


def gather_kernel(mean, counts_ref, group_ref, ids_ref, codes_ref, weights_ref, x_ref, *outs):
    rows = pair_rows_of(ids_ref[...], codes_ref[...], counts_ref, group_ref[0])
    total = len(outs) * BLOCK_ROWS
    member = membership(rows, total, None if mean else weights_ref[...])
    sums = mm(member.astype(BF16), split_halves(x_ref[...]))
    if mean:
        occupancy = jnp.sum(member, axis=1, keepdims=True)
        sums = sums / jnp.maximum(occupancy, 1.0)
    for j, out in enumerate(outs):
        out[...] = sums[j * BLOCK_ROWS : (j + 1) * BLOCK_ROWS].astype(BF16)


def spread_kernel(mean, counts_ref, group_ref, ids_ref, codes_ref, weights_ref, x_ref, scale_ref, *refs):
    blocks, out_ref = refs[:-1], refs[-1]
    ids = ids_ref[...]
    weights = weights_ref[...]
    experts, width = scale_ref.shape
    tokens = ids.shape[1]
    expert = iota((experts, tokens), 0)
    mix = jnp.zeros((experts, tokens), F32)
    for pick in range(ids.shape[0]):
        mix = jnp.where(expert == ids[pick : pick + 1, :], weights[pick : pick + 1, :], mix)
    high = mix.astype(BF16)
    low = (mix - high.astype(F32)).astype(BF16)
    scale = scale_ref[...]
    gain = mm(high, scale, TN) + mm(low, scale, TN)
    base = gain * x_ref[...].astype(F32)
    rows = pair_rows_of(ids, codes_ref[...], counts_ref, group_ref[0])
    total = len(blocks) * BLOCK_ROWS
    member = membership(rows, total, None if mean else weights)
    if mean:
        occupancy = jnp.sum(member, axis=1, keepdims=True)
        member = member / jnp.maximum(occupancy, 1.0)
    flat = jnp.concatenate([b[...] for b in blocks], axis=0)
    back = mm(member.astype(BF16), flat, TN)
    half = width // HALVES
    for h in range(HALVES):
        cols = slice(h * half, (h + 1) * half)
        out_ref[:, cols] = (base[:, cols] + back[h * tokens : (h + 1) * tokens]).astype(BF16)


def forward_kernel(n, counts_ref, group_ref, scale_ref, wg_ref, wu_ref, wd_ref, *refs):
    blocks, outs = refs[:n], refs[n : 2 * n]
    hidden_ref, slope_ref, silu_ref, x_ref, acc_ref = refs[2 * n :]
    e, f = pl.program_id(0), pl.program_id(1)
    rows = n * PAIR_ROWS

    @pl.when((e == 0) & (f == 0))
    def _():
        for c in range(0, n, CHUNK):
            part = blocks[c : c + CHUNK]
            x_ref[c * PAIR_ROWS : (c + len(part)) * PAIR_ROWS, :] = unpack_rows(part)
        acc_ref[...] = jnp.zeros_like(acc_ref)

    x = x_ref[...]
    gate = mm(x, wg_ref[0])
    up = mm(x, wu_ref[0])
    sg = 1.0 / (1.0 + jnp.exp(-gate))
    silu = gate * sg
    first = first_rows(rows, counts_ref, group_ref[0])
    mine = first == (e == 0)
    hidden = jnp.where(mine, silu * up, 0.0).astype(BF16)
    slope = jnp.where(mine, up * sg * (1.0 + gate * (1.0 - sg)), 0.0)
    silu = jnp.where(mine, silu, 0.0)
    acc_ref[...] += mm(hidden, wd_ref[0])
    tile = hidden.shape[1]
    cols = pl.ds(pl.multiple_of(f * tile, tile), tile)

    @pl.when(e == 0)
    def _():
        hidden_ref[:, cols] = hidden
        slope_ref[:, cols] = slope
        silu_ref[:, cols] = silu

    @pl.when(e == 1)
    def _():
        hidden_ref[:, cols] += hidden
        slope_ref[:, cols] += slope
        silu_ref[:, cols] += silu

    @pl.when((e == pl.num_programs(0) - 1) & (f == pl.num_programs(1) - 1))
    def _():
        scale = jnp.where(first, scale_ref[0, 0:1, :].astype(F32), scale_ref[0, 1:2, :].astype(F32))
        out = (acc_ref[...] - scale * x_ref[...].astype(F32)).astype(BF16)
        for c in range(0, n, CHUNK):
            part = outs[c : c + CHUNK]
            pack_rows(out[c * PAIR_ROWS : (c + len(part)) * PAIR_ROWS], part)


def unpack_kernel(n, parts, dp_ref, *refs):
    blocks, pull_ref, shares = refs[:n], refs[n], refs[n + 1 :]
    for c in range(0, n, CHUNK):
        part = blocks[c : c + CHUNK]
        pull_ref[c * PAIR_ROWS : (c + len(part)) * PAIR_ROWS, :] = unpack_rows(part)
    width = pull_ref.shape[1] // parts
    for k, share in enumerate(shares):
        start = pl.multiple_of((dp_ref[0] ^ k) * width, width)
        share[...] = pull_ref[:, pl.ds(start, width)]


def backward_kernel(n, counts_ref, group_ref, scale_ref, wg_ref, wu_ref, wd_ref, pull_ref, slope_ref, silu_ref, *refs):
    outs, acc_ref = refs[:n], refs[n]
    e, f = pl.program_id(0), pl.program_id(1)
    rows = n * PAIR_ROWS

    @pl.when((e == 0) & (f == 0))
    def _():
        acc_ref[...] = jnp.zeros_like(acc_ref)

    first = first_rows(rows, counts_ref, group_ref[0])
    mine = first == (e == 0)
    tile = wg_ref.shape[2]
    cols = pl.ds(pl.multiple_of(f * tile, tile), tile)
    d_hidden = jnp.where(mine, mm(pull_ref[...], wd_ref[0], NT), 0.0)
    d_gate = (d_hidden * slope_ref[:, cols]).astype(BF16)
    d_up = (d_hidden * silu_ref[:, cols]).astype(BF16)
    acc_ref[...] += mm(d_gate, wg_ref[0], NT) + mm(d_up, wu_ref[0], NT)

    @pl.when((e == pl.num_programs(0) - 1) & (f == pl.num_programs(1) - 1))
    def _():
        scale = jnp.where(first, scale_ref[0, 0:1, :].astype(F32), scale_ref[0, 1:2, :].astype(F32))
        out = (acc_ref[...] - scale * pull_ref[...].astype(F32)).astype(BF16)
        for c in range(0, n, CHUNK):
            part = outs[c : c + CHUNK]
            pack_rows(out[c * PAIR_ROWS : (c + len(part)) * PAIR_ROWS], part)


def grad_kernel(parts, counts_ref, group_ref, *refs):
    hidden, shares, out_ref = refs[:parts], refs[parts : 2 * parts], refs[2 * parts]
    rows = hidden[0].shape[0]
    first = first_rows(rows, counts_ref, group_ref[0])
    h_all = jnp.concatenate([h[...] for h in hidden], axis=0)
    lane = []
    for keep in (first, jnp.logical_not(first)):
        lane.append(
            jnp.concatenate(
                [jnp.where(keep, s[...].astype(F32), 0.0).astype(BF16) for s in shares], axis=0
            )
        )
    for e in range(2):
        out_ref[e] = mm(h_all, lane[e], TN).astype(BF16)


SMEM = pl.BlockSpec(memory_space=pltpu.SMEM)
VMEM = pl.BlockSpec(memory_space=pltpu.VMEM)


def call(kernel, n_smem, n_vmem, outs, flops, nbytes):
    return pl.pallas_call(
        kernel,
        out_shape=outs,
        in_specs=[SMEM] * n_smem + [VMEM] * n_vmem,
        out_specs=jax.tree.map(lambda _: VMEM, outs),
        compiler_params=pltpu.CompilerParams(vmem_limit_bytes=VMEM_LIMIT),
        cost_estimate=pl.CostEstimate(flops=flops, bytes_accessed=nbytes, transcendentals=0),
    )


def on_device(
    tokens, expert_ids, bucket_codes, route_weights, cotangent, counts, comp_scale, w_gate, w_up, w_down
):
    tok_count, width = tokens.shape
    n = lax.axis_size("expert")
    parts = lax.axis_size("dp")
    ff = w_gate.shape[2]
    half = width // HALVES
    rows = n * PAIR_ROWS
    total = n * BLOCK_ROWS
    group = lax.axis_index("expert").astype(jnp.int32).reshape(1)
    dp = lax.axis_index("dp").astype(jnp.int32).reshape(1)
    ids, codes, weights = expert_ids.T, bucket_codes.T, route_weights.T
    block = jax.ShapeDtypeStruct((BLOCK_ROWS, half), BF16)
    blocks = [block] * n
    block_bytes = total * width

    def exchange(values):
        return [values[0]] + [
            lax.ppermute(values[k], "expert", [(i, i ^ k) for i in range(n)]) for k in range(1, n)
        ]

    def exchange_dp(values):
        return [values[0]] + [
            lax.ppermute(values[k], "dp", [(i, i ^ k) for i in range(parts)]) for k in range(1, parts)
        ]

    def gather(mean, x):
        return call(
            functools.partial(gather_kernel, mean), 2, 4, blocks, 2 * total * tok_count * width, block_bytes
        )(counts, group, ids, codes, weights, x)

    def spread(mean, x, got):
        return call(
            functools.partial(spread_kernel, mean),
            2,
            5 + n,
            jax.ShapeDtypeStruct(tokens.shape, BF16),
            2 * total * tok_count * width,
            block_bytes,
        )(counts, group, ids, codes, weights, x, comp_scale, *got)

    sent_c = gather(True, tokens)
    got_c = exchange(sent_c)
    sent_p = gather(False, cotangent)
    got_p = exchange(sent_p)

    local = w_gate.shape[0]
    scale_three = comp_scale.reshape(n, local, width)
    tile_grid = (local, ff // FF_TILE)
    whole = lambda shape: pl.BlockSpec(shape, lambda e, f: (0,) * len(shape))
    scale_spec = pl.BlockSpec((1, local, width), lambda e, f: (0, 0, 0))
    own_scale = lax.dynamic_slice_in_dim(scale_three, group[0], 1, axis=0)
    weight_specs = [
        pl.BlockSpec((1, width, FF_TILE), lambda e, f: (e, 0, f)),
        pl.BlockSpec((1, width, FF_TILE), lambda e, f: (e, 0, f)),
        pl.BlockSpec((1, FF_TILE, width), lambda e, f: (e, f, 0)),
    ]
    weight_bytes = 3 * local * width * ff * 2
    expert_flops = 2 * 3 * rows * local * width * ff
    params = pltpu.CompilerParams(
        vmem_limit_bytes=VMEM_LIMIT, dimension_semantics=("arbitrary", "arbitrary")
    )
    cost = pl.CostEstimate(flops=expert_flops, bytes_accessed=weight_bytes, transcendentals=rows * ff)

    results = pl.pallas_call(
        functools.partial(forward_kernel, n),
        grid=tile_grid,
        in_specs=[SMEM, SMEM, scale_spec] + weight_specs + [whole(block.shape)] * n,
        out_specs=[whole(block.shape)] * n + [whole((rows, ff))] * 3,
        out_shape=blocks
        + [
            jax.ShapeDtypeStruct((rows, ff), BF16),
            jax.ShapeDtypeStruct((rows, ff), F32),
            jax.ShapeDtypeStruct((rows, ff), F32),
        ],
        scratch_shapes=[pltpu.VMEM((rows, width), BF16), pltpu.VMEM((rows, width), F32)],
        compiler_params=params,
        cost_estimate=cost,
    )(counts, group, own_scale, w_gate, w_up, w_down, *got_c)
    sent_o, (hidden, slope, silu) = results[:n], results[n:]
    got_o = exchange(sent_o)
    all_hidden = exchange_dp([hidden] * parts)

    pull_and_shares = call(
        functools.partial(unpack_kernel, n, parts),
        1,
        n,
        [jax.ShapeDtypeStruct((rows, width), BF16)]
        + [jax.ShapeDtypeStruct((rows, width // parts), BF16)] * parts,
        2 * rows * min(n, CHUNK) * BLOCK_ROWS * width,
        2 * block_bytes,
    )(dp, *got_p)
    pull = pull_and_shares[0]
    all_shares = exchange_dp(pull_and_shares[1:])

    sent_b = pl.pallas_call(
        functools.partial(backward_kernel, n),
        grid=tile_grid,
        in_specs=[SMEM, SMEM, scale_spec]
        + weight_specs
        + [whole((rows, width)), whole((rows, ff)), whole((rows, ff))],
        out_specs=[whole(block.shape)] * n,
        out_shape=blocks,
        scratch_shapes=[pltpu.VMEM((rows, width), F32)],
        compiler_params=params,
        cost_estimate=cost,
    )(counts, group, own_scale, w_gate, w_up, w_down, pull, slope, silu)
    got_b = exchange(sent_b)

    grad_down = call(
        functools.partial(grad_kernel, parts),
        2,
        2 * parts,
        jax.ShapeDtypeStruct((local, ff, width // parts), BF16),
        2 * parts * rows * ff * local * width // parts,
        parts * rows * (ff + width // parts) * 2,
    )(counts, group, *all_hidden, *all_shares)
    layer_output = spread(False, tokens, got_o)
    grad_tokens = spread(True, cotangent, got_b)
    return (layer_output, grad_tokens, grad_down)


def solution(mesh):
    token_spec = P(("dp", "expert"), None)
    weight_spec = P("expert", None, None)
    in_specs = (token_spec,) * 5 + (P(), P()) + (weight_spec,) * 3
    out_specs = (token_spec, token_spec, P("expert", None, "dp"))
    return jax.shard_map(
        on_device, mesh=mesh, in_specs=in_specs, out_specs=out_specs, check_vma=False
    )
```

time: 198 us -> 117 us (0.59)
  waiting for transfers between devices: 72.9 us -> 23.5 us
  matrix products: 35.6 us -> 0 us
  Pallas kernels: 0 us -> 34.6 us
  starting transfers between devices: 18.1 us -> 50.8 us
  other arithmetic: 32.6 us -> 0 us
  local copies, waits for them, and re-layouts: 24.2 us -> 6.39 us
  between operations: 14.3 us -> 0.86 us
    all_to_all x4 -> x0, waiting for transfers between devices: 72.9 us -> none  [the longest x1 26 us: on_device(): lax.all_to_all(owner_out(expert_out), 'expert', split_axis=0, concat_axis...]
    ppermute x0 -> x34, starting transfers between devices: none -> 50.8 us  [the longest x28 42.1 us: exchange(): lax.ppermute(values[k], 'expert', [(i, i ^ k) for i in range(n)])]
    dot_general x9 -> x0, matrix products: 35.6 us -> none  [the longest x1 5.71 us: expert_backward(): jnp.einsum('jqbf,qjbd->djf', hidden, pull_rows, preferred_element_type=jn...]
    pallas_call x0 -> x8, Pallas kernels: none -> 34.6 us  [the longest x1 13.4 us: on_device(): pl.pallas_call(functools.partial(backward_kernel, n), grid=tile_grid, in_...]
    ppermute x0 -> x34, waiting for transfers between devices: none -> 23.5 us  [the longest x28 13.8 us: exchange(): lax.ppermute(values[k], 'expert', [(i, i ^ k) for i in range(n)])]
    all_to_all x4 -> x0, starting transfers between devices: 17.9 us -> none  [the longest x1 6.33 us: on_device(): lax.all_to_all(source_out(centroid), 'expert', split_axis=0, concat_axis=...]
    gather x2 -> x0, local copies, waits for them, and re-layouts: 17.4 us -> none  [the longest x1 10.6 us: on_device(): layer_pairs = route_weights[:, :, None] * combined[slot_id]]
    scatter-add x1 -> x0, other arithmetic: 14.9 us -> none  [on_device(): jax.ops.segment_sum(pair_pull, flat_slots, num_segments=slot_total)]
  transfers between devices with their start and end apart: 5 -> 34, of which waited for: 4 -> 4; matrix products, arithmetic and copies ran while one was open for 39% -> 1% of each run, Pallas kernels for 0% -> 26%
where the time goes in v1:
time: 117 us; the launch traced here: 116 us
  starting transfers between devices  50.8 us (43%)
  Pallas kernels  34.6 us (30%)
  waiting for transfers between devices  23.5 us (20%)
  local copies, waits for them, and re-layouts  6.39 us (5%)
    ppermute x28, starting transfers between devices, exchange(): lax.ppermute(values[k], 'expert', [(i, i ^ k) for i in range(n)])  42.1 us
    ppermute x28, waiting for transfers between devices, exchange(): lax.ppermute(values[k], 'expert', [(i, i ^ k) for i in range(n)])  13.8 us
    pallas_call x1, Pallas kernels, on_device(): pl.pallas_call(functools.partial(backward_kernel, n), grid=tile_grid, in_...  13.4 us
    pallas_call x1, Pallas kernels, on_device(): pl.pallas_call(functools.partial(forward_kernel, n), grid=tile_grid, in_s...  11.2 us
    ppermute x6, waiting for transfers between devices, exchange_dp(): lax.ppermute(values[k], 'dp', [(i, i ^ k) for i in range(parts)])  9.76 us
    ppermute x6, starting transfers between devices, exchange_dp(): lax.ppermute(values[k], 'dp', [(i, i ^ k) for i in range(parts)])  8.79 us
    unnamed x28, local copies, waits for them, and re-layouts  5.49 us
    pallas_call x2, Pallas kernels, spread(): call(functools.partial(spread_kernel, mean), 2, 5 + n, jax.ShapeDtypeStru...  4.32 us
  transfers between devices with their start and end apart: 34, of which 4 were waited for; matrix products, arithmetic and copies ran while one was open for 1% of the time, Pallas kernels for 26%

profile of v1, /device:TPU:0, one launch (start us, length us, event | category | flops | bytes accessed | tf_op | source)
XLA Modules:
  0.0 116.2 jit_solution(2780671107217508374)
XLA Ops:
  0.6 1.0 copy-done.3
  5.9 2.7 %collective-permute-start.15 = (bf16[40,1024]{1,0:T(8,128)(2,1)S(1)}, bf16[40,1024]{1,0:T(8,128)(2,1)S(1)}, u32[]{:S(2)}, u32[]{:S(2)}) collective-permute-start(bf16[40,1024]{1,0:T(8,128)(2,1)S(1)} %get-tuple-element.61), channel_id=1, source_target_pairs={{0,2},{1,3},{2,0},{3,1},{4,6},{5,7},{6,4},{7,5},{8,10},{9,11},{10,... | collective-permute-start | bytes 245768 | tf_op jit(solution)/shard_map/ppermute | solution.py:279
  8.6 1.0 copy-done.1
  11.2 1.4 %collective-permute-start.2 = (bf16[40,1024]{1,0:T(8,128)(2,1)S(1)}, bf16[40,1024]{1,0:T(8,128)(2,1)S(1)}, u32[]{:S(2)}, u32[]{:S(2)}) collective-permute-start(bf16[40,1024]{1,0:T(8,128)(2,1)S(1)} %get-tuple-element.46), channel_id=1, source_target_pairs={{0,3},{1,2},{2,1},{3,0},{4,7},{5,6},{6,5},{7,4},{8,11},{9,10},{10,... | collective-permute-start | bytes 245768 | tf_op jit(solution)/shard_map/ppermute | solution.py:279
  13.5 2.7 %collective-permute-start.3 = (bf16[40,1024]{1,0:T(8,128)(2,1)S(1)}, bf16[40,1024]{1,0:T(8,128)(2,1)S(1)}, u32[]{:S(2)}, u32[]{:S(2)}) collective-permute-start(bf16[40,1024]{1,0:T(8,128)(2,1)S(1)} %get-tuple-element.47), channel_id=1, source_target_pairs={{0,4},{1,5},{2,6},{3,7},{4,0},{5,1},{6,2},{7,3},{8,12},{9,13},{10,... | collective-permute-start | bytes 245768 | tf_op jit(solution)/shard_map/ppermute | solution.py:279
  16.3 2.4 %collective-permute-start.5 = (bf16[40,1024]{1,0:T(8,128)(2,1)S(1)}, bf16[40,1024]{1,0:T(8,128)(2,1)S(1)}, u32[]{:S(2)}, u32[]{:S(2)}) collective-permute-start(bf16[40,1024]{1,0:T(8,128)(2,1)S(1)} %get-tuple-element.49), channel_id=1, source_target_pairs={{0,6},{1,7},{2,4},{3,5},{4,2},{5,3},{6,0},{7,1},{8,14},{9,15},{10,... | collective-permute-start | bytes 245768 | tf_op jit(solution)/shard_map/ppermute | solution.py:279
  19.9 3.1 %collective-permute-start.17 = (bf16[40,1024]{1,0:T(8,128)(2,1)S(1)}, bf16[40,1024]{1,0:T(8,128)(2,1)S(1)}, u32[]{:S(2)}, u32[]{:S(2)}) collective-permute-start(bf16[40,1024]{1,0:T(8,128)(2,1)S(1)} %get-tuple-element.63), channel_id=1, source_target_pairs={{0,4},{1,5},{2,6},{3,7},{4,0},{5,1},{6,2},{7,3},{8,12},{9,13},{10,... | collective-permute-start | bytes 245768 | tf_op jit(solution)/shard_map/ppermute | solution.py:279
  22.9 5.3 %collective-permute-done.4.refs_5_ = bf16[40,1024]{1,0:T(8,128)(2,1)S(1)} collective-permute-done((bf16[40,1024]{1,0:T(8,128)(2,1)S(1)}, bf16[40,1024]{1,0:T(8,128)(2,1)S(1)}, u32[]{:S(2)}, u32[]{:S(2)}) %collective-permute-start.4) | collective-permute-done | bytes 81952 | tf_op jit(solution)/shard_map/ppermute | solution.py:279
  28.2 3.6 %collective-permute-start.19 = (bf16[40,1024]{1,0:T(8,128)(2,1)S(1)}, bf16[40,1024]{1,0:T(8,128)(2,1)S(1)}, u32[]{:S(2)}, u32[]{:S(2)}) collective-permute-start(bf16[40,1024]{1,0:T(8,128)(2,1)S(1)} %get-tuple-element.65), channel_id=1, source_target_pairs={{0,6},{1,7},{2,4},{3,5},{4,2},{5,3},{6,0},{7,1},{8,14},{9,15},{10,... | collective-permute-start | bytes 245768 | tf_op jit(solution)/shard_map/ppermute | solution.py:279
  32.9 11.2 %shard_map.122 = (bf16[40,1024]{1,0:T(8,128)(2,1)S(1)}, bf16[40,1024]{1,0:T(8,128)(2,1)S(1)}, bf16[40,1024]{1,0:T(8,128)(2,1)S(1)}, bf16[40,1024]{1,0:T(8,128)(2...) custom-call(s32[16]{0:T(128)S(1)} %copy-done.12, ...), custom_call_target="tpu_custom_call" | custom-call | flops 3019898880 | bytes 18874368 | tf_op jit(solution)/shard_map/pallas_call | solution.py:325
  44.2 8.4 %collective-permute-start.8 = (bf16[40,1024]{1,0:T(8,128)(2,1)S(1)}, bf16[40,1024]{1,0:T(8,128)(2,1)S(1)}, u32[]{:S(2)}, u32[]{:S(2)}) collective-permute-start(bf16[40,1024]{1,0:T(8,128)(2,1)S(1)} %get-tuple-element.53), channel_id=1, source_target_pairs={{0,2},{1,3},{2,0},{3,1},{4,6},{5,7},{6,4},{7,5},{8,10},{9,11},{10,... | collective-permute-start | bytes 245768 | tf_op jit(solution)/shard_map/ppermute | solution.py:279
  52.7 1.1 collective-permute-start.10
  53.8 1.3 %collective-permute-start.11 = (bf16[40,1024]{1,0:T(8,128)(2,1)S(1)}, bf16[40,1024]{1,0:T(8,128)(2,1)S(1)}, u32[]{:S(2)}, u32[]{:S(2)}) collective-permute-start(bf16[40,1024]{1,0:T(8,128)(2,1)S(1)} %get-tuple-element.56), channel_id=1, source_target_pairs={{0,5},{1,4},{2,7},{3,6},{4,1},{5,0},{6,3},{7,2},{8,13},{9,12},{10,... | collective-permute-start | bytes 245768 | tf_op jit(solution)/shard_map/ppermute | solution.py:279
  55.7 13.4 %shard_map.126 = (bf16[40,1024]{1,0:T(8,128)(2,1)S(1)}, bf16[40,1024]{1,0:T(8,128)(2,1)S(1)}, bf16[40,1024]{1,0:T(8,128)(2,1)S(1)}, bf16[40,1024]{1,0:T(8,128)(2...) custom-call(s32[16]{0:T(128)S(1)} %copy-done.13, ...), custom_call_target="tpu_custom_call" | custom-call | flops 3019898880 | bytes 18874368 | tf_op jit(solution)/shard_map/pallas_call | solution.py:356
  69.2 1.8 %collective-permute-start.12 = (bf16[40,1024]{1,0:T(8,128)(2,1)S(1)}, bf16[40,1024]{1,0:T(8,128)(2,1)S(1)}, u32[]{:S(2)}, u32[]{:S(2)}) collective-permute-start(bf16[40,1024]{1,0:T(8,128)(2,1)S(1)} %get-tuple-element.57), channel_id=1, source_target_pairs={{0,6},{1,7},{2,4},{3,5},{4,2},{5,3},{6,0},{7,1},{8,14},{9,15},{10,... | collective-permute-start | bytes 245768 | tf_op jit(solution)/shard_map/ppermute | solution.py:279
  70.9 2.1 %collective-permute-start.13 = (bf16[40,1024]{1,0:T(8,128)(2,1)S(1)}, bf16[40,1024]{1,0:T(8,128)(2,1)S(1)}, u32[]{:S(2)}, u32[]{:S(2)}) collective-permute-start(bf16[40,1024]{1,0:T(8,128)(2,1)S(1)} %get-tuple-element.58), channel_id=1, source_target_pairs={{0,7},{1,6},{2,5},{3,4},{4,3},{5,2},{6,1},{7,0},{8,15},{9,14},{10,... | collective-permute-start | bytes 245768 | tf_op jit(solution)/shard_map/ppermute | solution.py:279
  73.3 1.5 %collective-permute-start.31 = (bf16[160,512]{1,0:T(8,128)(2,1)S(1)}, bf16[160,512]{1,0:T(8,128)(2,1)S(1)}, u32[]{:S(2)}, u32[]{:S(2)}) collective-permute-start(bf16[160,512]{1,0:T(8,128)(2,1)S(1)} %get-tuple-element.80), channel_id=1, source_target_pairs={{0,8},{8,0},{16,24},{24,16},{1,9},{9,1},{17,25},{25,17},{2,10},{10... | collective-permute-start | bytes 491528 | tf_op jit(solution)/shard_map/ppermute | solution.py:284
  74.8 1.7 %collective-permute-done.12.refs_6_ = bf16[40,1024]{1,0:T(8,128)(2,1)S(1)} collective-permute-done((bf16[40,1024]{1,0:T(8,128)(2,1)S(1)}, bf16[40,1024]{1,0:T(8,128)(2,1)S(1)}, u32[]{:S(2)}, u32[]{:S(2)}) %collective-permute-start.12) | collective-permute-done | bytes 81952 | tf_op jit(solution)/shard_map/ppermute | solution.py:279
  76.5 2.2 %collective-permute-start.23 = (bf16[40,1024]{1,0:T(8,128)(2,1)S(1)}, bf16[40,1024]{1,0:T(8,128)(2,1)S(1)}, u32[]{:S(2)}, u32[]{:S(2)}) collective-permute-start(bf16[40,1024]{1,0:T(8,128)(2,1)S(1)} %get-tuple-element.73), channel_id=1, source_target_pairs={{0,3},{1,2},{2,1},{3,0},{4,7},{5,6},{6,5},{7,4},{8,11},{9,10},{10,... | collective-permute-start | bytes 245768 | tf_op jit(solution)/shard_map/ppermute | solution.py:279
  78.7 1.7 %collective-permute-start.24 = (bf16[40,1024]{1,0:T(8,128)(2,1)S(1)}, bf16[40,1024]{1,0:T(8,128)(2,1)S(1)}, u32[]{:S(2)}, u32[]{:S(2)}) collective-permute-start(bf16[40,1024]{1,0:T(8,128)(2,1)S(1)} %get-tuple-element.74), channel_id=1, source_target_pairs={{0,4},{1,5},{2,6},{3,7},{4,0},{5,1},{6,2},{7,3},{8,12},{9,13},{10,... | collective-permute-start | bytes 245768 | tf_op jit(solution)/shard_map/ppermute | solution.py:279
  80.4 1.9 %collective-permute-start.25 = (bf16[40,1024]{1,0:T(8,128)(2,1)S(1)}, bf16[40,1024]{1,0:T(8,128)(2,1)S(1)}, u32[]{:S(2)}, u32[]{:S(2)}) collective-permute-start(bf16[40,1024]{1,0:T(8,128)(2,1)S(1)} %get-tuple-element.75), channel_id=1, source_target_pairs={{0,5},{1,4},{2,7},{3,6},{4,1},{5,0},{6,3},{7,2},{8,13},{9,12},{10,... | collective-permute-start | bytes 245768 | tf_op jit(solution)/shard_map/ppermute | solution.py:279
  82.3 1.2 %collective-permute-start.26 = (bf16[40,1024]{1,0:T(8,128)(2,1)S(1)}, bf16[40,1024]{1,0:T(8,128)(2,1)S(1)}, u32[]{:S(2)}, u32[]{:S(2)}) collective-permute-start(bf16[40,1024]{1,0:T(8,128)(2,1)S(1)} %get-tuple-element.76), channel_id=1, source_target_pairs={{0,6},{1,7},{2,4},{3,5},{4,2},{5,3},{6,0},{7,1},{8,14},{9,15},{10,... | collective-permute-start | bytes 245768 | tf_op jit(solution)/shard_map/ppermute | solution.py:279
  83.5 1.4 %collective-permute-start.27 = (bf16[40,1024]{1,0:T(8,128)(2,1)S(1)}, bf16[40,1024]{1,0:T(8,128)(2,1)S(1)}, u32[]{:S(2)}, u32[]{:S(2)}) collective-permute-start(bf16[40,1024]{1,0:T(8,128)(2,1)S(1)} %get-tuple-element.77), channel_id=1, source_target_pairs={{0,7},{1,6},{2,5},{3,4},{4,3},{5,2},{6,1},{7,0},{8,15},{9,14},{10,... | collective-permute-start | bytes 245768 | tf_op jit(solution)/shard_map/ppermute | solution.py:279
  84.9 6.8 %collective-permute-done.24.refs_4_ = bf16[40,1024]{1,0:T(8,128)(2,1)S(1)} collective-permute-done((bf16[40,1024]{1,0:T(8,128)(2,1)S(1)}, bf16[40,1024]{1,0:T(8,128)(2,1)S(1)}, u32[]{:S(2)}, u32[]{:S(2)}) %collective-permute-start.24) | collective-permute-done | bytes 81952 | tf_op jit(solution)/shard_map/ppermute | solution.py:279
  91.7 2.4 %collective-permute-start.30 = (bf16[160,768]{1,0:T(8,128)(2,1)S(1)}, bf16[160,768]{1,0:T(8,128)(2,1)S(1)}, u32[]{:S(2)}, u32[]{:S(2)}) collective-permute-start(bf16[160,768]{1,0:T(8,128)(2,1)S(1)} %get-tuple-element.78.refs_0_), channel_id=1, source_target_pairs={{0,24},{8,16},{16,8},{24,0},{1,25},{9,17},{17,9},{25,1},{2,26},{10... | collective-permute-start | bytes 737288 | tf_op jit(solution)/shard_map/ppermute | solution.py:284
  94.1 1.3 %collective-permute-start.29 = (bf16[160,768]{1,0:T(8,128)(2,1)S(1)}, bf16[160,768]{1,0:T(8,128)(2,1)S(1)}, u32[]{:S(2)}, u32[]{:S(2)}) collective-permute-start(bf16[160,768]{1,0:T(8,128)(2,1)S(1)} %get-tuple-element.78.refs_0_), channel_id=1, source_target_pairs={{0,16},{8,24},{16,0},{24,8},{1,17},{9,25},{17,1},{25,9},{2,18},{10... | collective-permute-start | bytes 737288 | tf_op jit(solution)/shard_map/ppermute | solution.py:284
  95.5 1.5 %collective-permute-start.28 = (bf16[160,768]{1,0:T(8,128)(2,1)S(1)}, bf16[160,768]{1,0:T(8,128)(2,1)S(1)}, u32[]{:S(2)}, u32[]{:S(2)}) collective-permute-start(bf16[160,768]{1,0:T(8,128)(2,1)S(1)} %get-tuple-element.78.refs_0_), channel_id=1, source_target_pairs={{0,8},{8,0},{16,24},{24,16},{1,9},{9,1},{17,25},{25,17},{2,10},{10... | collective-permute-start | bytes 737288 | tf_op jit(solution)/shard_map/ppermute | solution.py:284
  97.5 1.5 %collective-permute-start.33 = (bf16[160,512]{1,0:T(8,128)(2,1)S(1)}, bf16[160,512]{1,0:T(8,128)(2,1)S(1)}, u32[]{:S(2)}, u32[]{:S(2)}) collective-permute-start(bf16[160,512]{1,0:T(8,128)(2,1)S(1)} %get-tuple-element.82), channel_id=1, source_target_pairs={{0,24},{8,16},{16,8},{24,0},{1,25},{9,17},{17,9},{25,1},{2,26},{10... | collective-permute-start | bytes 491528 | tf_op jit(solution)/shard_map/ppermute | solution.py:284
  99.0 2.2 %shard_map.123 = bf16[128,2048]{1,0:T(8,128)(2,1)} custom-call(s32[16]{0:T(128)S(1)} %copy-done.13, s32[1]{0:T(128)} %bitcast.group_ref, s32[8,128]{1,0:T(8,128)S(1)} %bitcast.7, s32[8,128]{1,0:T(8,128)S(1)} %bitcast.11, f32[8,128]{1,0:T(8,128)S(1)} %bitcast.15, bf16[128,2048]{1,0:T(8,128)(2,1)S(1)} %copy-done.2, bf16[16,2048]{1,0:T(8,128)(2,1)S(1)} %copy-done, ...), custom_call_target="tpu_custom_call" | custom-call | flops 167772160 | bytes 655360 | tf_op jit(solution)/shard_map/pallas_call | solution.py:293
  101.1 2.2 %shard_map.127 = bf16[128,2048]{1,0:T(8,128)(2,1)} custom-call(s32[16]{0:T(128)S(1)} %copy-done.13, s32[1]{0:T(128)} %bitcast.group_ref, s32[8,128]{1,0:T(8,128)S(1)} %bitcast.8, s32[8,128]{1,0:T(8,128)S(1)} %bitcast.12, f32[8,128]{1,0:T(8,128)S(1)} %bitcast.16, bf16[128,2048]{1,0:T(8,128)(2,1)S(1)} %copy-done.4, bf16[16,2048]{1,0:T(8,128)(2,1)S(1)} %copy-done, ...), custom_call_target="tpu_custom_call" | custom-call | flops 167772160 | bytes 655360 | tf_op jit(solution)/shard_map/pallas_call | solution.py:293
  103.3 9.7 %collective-permute-done.32.refs_6_ = bf16[160,512]{1,0:T(8,128)(2,1)S(1)} collective-permute-done((bf16[160,512]{1,0:T(8,128)(2,1)S(1)}, bf16[160,512]{1,0:T(8,128)(2,1)S(1)}, u32[]{:S(2)}, u32[]{:S(2)}) %collective-permute-start.32) | collective-permute-done | bytes 163872 | tf_op jit(solution)/shard_map/ppermute | solution.py:284
  113.1 3.1 %shard_map.128 = bf16[2,768,512]{2,1,0:T(8,128)(2,1)} custom-call(s32[16]{0:T(128)S(1)} %copy-done.13, s32[1]{0:T(128)} %bitcast.group_ref, bf16[160,768]{1,0:T(8,128)(2,1)S(1)} %get-tuple-element.78.refs_0_, bf16[160,768]{1,0:T(8,128)(2,1)S(1)} %collective-permute-done.28.refs_1_, bf16[160,768]{1,0:T(8,128)(2,1)S(1)} %collective-permute-done.29.refs_2_, ...), custom_call_target="tpu_custom_call" | custom-call | flops 1006632960 | bytes 1638400 | tf_op jit(solution)/shard_map/pallas_call | solution.py:370
  (74 shorter events, 10.6 us)
Async XLA Ops:
  5.4 8.1 %collective-permute-start.14 = (bf16[40,1024]{1,0:T(8,128)(2,1)S(1)}, bf16[40,1024]{1,0:T(8,128)(2,1)S(1)}, u32[]{:S(2)}, u32[]{:S(2)}) collective-permute-start(bf16[40,1024]{1,0:T(8,128)(2,1)S(1)} %get-tuple-element.60), channel_id=1, source_target_pairs={{0,1},{1,0},{2,3},{3,2},{4,5},{5,4},{6,7},{7,6},{8,9},{9,8},{10,11... | collective-permute-start | bytes 245768 | tf_op jit(solution)/shard_map/ppermute | solution.py:279
  5.9 10.2 %collective-permute-start.15 = (bf16[40,1024]{1,0:T(8,128)(2,1)S(1)}, bf16[40,1024]{1,0:T(8,128)(2,1)S(1)}, u32[]{:S(2)}, u32[]{:S(2)}) collective-permute-start(bf16[40,1024]{1,0:T(8,128)(2,1)S(1)} %get-tuple-element.61), channel_id=1, source_target_pairs={{0,2},{1,3},{2,0},{3,1},{4,6},{5,7},{6,4},{7,5},{8,10},{9,11},{10,... | collective-permute-start | bytes 245768 | tf_op jit(solution)/shard_map/ppermute | solution.py:279
  10.9 7.8 %collective-permute-start.1 = (bf16[40,1024]{1,0:T(8,128)(2,1)S(1)}, bf16[40,1024]{1,0:T(8,128)(2,1)S(1)}, u32[]{:S(2)}, u32[]{:S(2)}) collective-permute-start(bf16[40,1024]{1,0:T(8,128)(2,1)S(1)} %get-tuple-element.45), channel_id=1, source_target_pairs={{0,2},{1,3},{2,0},{3,1},{4,6},{5,7},{6,4},{7,5},{8,10},{9,11},{10,... | collective-permute-start | bytes 245768 | tf_op jit(solution)/shard_map/ppermute | solution.py:279
  11.2 8.6 %collective-permute-start.2 = (bf16[40,1024]{1,0:T(8,128)(2,1)S(1)}, bf16[40,1024]{1,0:T(8,128)(2,1)S(1)}, u32[]{:S(2)}, u32[]{:S(2)}) collective-permute-start(bf16[40,1024]{1,0:T(8,128)(2,1)S(1)} %get-tuple-element.46), channel_id=1, source_target_pairs={{0,3},{1,2},{2,1},{3,0},{4,7},{5,6},{6,5},{7,4},{8,11},{9,10},{10,... | collective-permute-start | bytes 245768 | tf_op jit(solution)/shard_map/ppermute | solution.py:279
  16.2 12.1 %collective-permute-start.4 = (bf16[40,1024]{1,0:T(8,128)(2,1)S(1)}, bf16[40,1024]{1,0:T(8,128)(2,1)S(1)}, u32[]{:S(2)}, u32[]{:S(2)}) collective-permute-start(bf16[40,1024]{1,0:T(8,128)(2,1)S(1)} %get-tuple-element.48), channel_id=1, source_target_pairs={{0,5},{1,4},{2,7},{3,6},{4,1},{5,0},{6,3},{7,2},{8,13},{9,12},{10,... | collective-permute-start | bytes 245768 | tf_op jit(solution)/shard_map/ppermute | solution.py:279
  16.3 11.9 %collective-permute-start.5 = (bf16[40,1024]{1,0:T(8,128)(2,1)S(1)}, bf16[40,1024]{1,0:T(8,128)(2,1)S(1)}, u32[]{:S(2)}, u32[]{:S(2)}) collective-permute-start(bf16[40,1024]{1,0:T(8,128)(2,1)S(1)} %get-tuple-element.49), channel_id=1, source_target_pairs={{0,6},{1,7},{2,4},{3,5},{4,2},{5,3},{6,0},{7,1},{8,14},{9,15},{10,... | collective-permute-start | bytes 245768 | tf_op jit(solution)/shard_map/ppermute | solution.py:279
  18.7 13.1 %collective-permute-start.6 = (bf16[40,1024]{1,0:T(8,128)(2,1)S(1)}, bf16[40,1024]{1,0:T(8,128)(2,1)S(1)}, u32[]{:S(2)}, u32[]{:S(2)}) collective-permute-start(bf16[40,1024]{1,0:T(8,128)(2,1)S(1)} %get-tuple-element.50), channel_id=1, source_target_pairs={{0,7},{1,6},{2,5},{3,4},{4,3},{5,2},{6,1},{7,0},{8,15},{9,14},{10,... | collective-permute-start | bytes 245768 | tf_op jit(solution)/shard_map/ppermute | solution.py:279
  19.8 24.3 %collective-permute-start.16 = (bf16[40,1024]{1,0:T(8,128)(2,1)S(1)}, bf16[40,1024]{1,0:T(8,128)(2,1)S(1)}, u32[]{:S(2)}, u32[]{:S(2)}) collective-permute-start(bf16[40,1024]{1,0:T(8,128)(2,1)S(1)} %get-tuple-element.62), channel_id=1, source_target_pairs={{0,3},{1,2},{2,1},{3,0},{4,7},{5,6},{6,5},{7,4},{8,11},{9,10},{10,... | collective-permute-start | bytes 245768 | tf_op jit(solution)/shard_map/ppermute | solution.py:279
  19.9 24.3 %collective-permute-start.17 = (bf16[40,1024]{1,0:T(8,128)(2,1)S(1)}, bf16[40,1024]{1,0:T(8,128)(2,1)S(1)}, u32[]{:S(2)}, u32[]{:S(2)}) collective-permute-start(bf16[40,1024]{1,0:T(8,128)(2,1)S(1)} %get-tuple-element.63), channel_id=1, source_target_pairs={{0,4},{1,5},{2,6},{3,7},{4,0},{5,1},{6,2},{7,3},{8,12},{9,13},{10,... | collective-permute-start | bytes 245768 | tf_op jit(solution)/shard_map/ppermute | solution.py:279
  28.2 24.4 %collective-permute-start.18 = (bf16[40,1024]{1,0:T(8,128)(2,1)S(1)}, bf16[40,1024]{1,0:T(8,128)(2,1)S(1)}, u32[]{:S(2)}, u32[]{:S(2)}) collective-permute-start(bf16[40,1024]{1,0:T(8,128)(2,1)S(1)} %get-tuple-element.64), channel_id=1, source_target_pairs={{0,5},{1,4},{2,7},{3,6},{4,1},{5,0},{6,3},{7,2},{8,13},{9,12},{10,... | collective-permute-start | bytes 245768 | tf_op jit(solution)/shard_map/ppermute | solution.py:279
  28.2 24.5 %collective-permute-start.19 = (bf16[40,1024]{1,0:T(8,128)(2,1)S(1)}, bf16[40,1024]{1,0:T(8,128)(2,1)S(1)}, u32[]{:S(2)}, u32[]{:S(2)}) collective-permute-start(bf16[40,1024]{1,0:T(8,128)(2,1)S(1)} %get-tuple-element.65), channel_id=1, source_target_pairs={{0,6},{1,7},{2,4},{3,5},{4,2},{5,3},{6,0},{7,1},{8,14},{9,15},{10,... | collective-permute-start | bytes 245768 | tf_op jit(solution)/shard_map/ppermute | solution.py:279
  31.9 21.9 %collective-permute-start.20 = (bf16[40,1024]{1,0:T(8,128)(2,1)S(1)}, bf16[40,1024]{1,0:T(8,128)(2,1)S(1)}, u32[]{:S(2)}, u32[]{:S(2)}) collective-permute-start(bf16[40,1024]{1,0:T(8,128)(2,1)S(1)} %get-tuple-element.66), channel_id=1, source_target_pairs={{0,7},{1,6},{2,5},{3,4},{4,3},{5,2},{6,1},{7,0},{8,15},{9,14},{10,... | collective-permute-start | bytes 245768 | tf_op jit(solution)/shard_map/ppermute | solution.py:279
  44.1 25.0 %collective-permute-start.7 = (bf16[40,1024]{1,0:T(8,128)(2,1)S(1)}, bf16[40,1024]{1,0:T(8,128)(2,1)S(1)}, u32[]{:S(2)}, u32[]{:S(2)}) collective-permute-start(bf16[40,1024]{1,0:T(8,128)(2,1)S(1)} %get-tuple-element.52), channel_id=1, source_target_pairs={{0,1},{1,0},{2,3},{3,2},{4,5},{5,4},{6,7},{7,6},{8,9},{9,8},{10,11... | collective-permute-start | bytes 245768 | tf_op jit(solution)/shard_map/ppermute | solution.py:279
  44.2 26.7 %collective-permute-start.8 = (bf16[40,1024]{1,0:T(8,128)(2,1)S(1)}, bf16[40,1024]{1,0:T(8,128)(2,1)S(1)}, u32[]{:S(2)}, u32[]{:S(2)}) collective-permute-start(bf16[40,1024]{1,0:T(8,128)(2,1)S(1)} %get-tuple-element.53), channel_id=1, source_target_pairs={{0,2},{1,3},{2,0},{3,1},{4,6},{5,7},{6,4},{7,5},{8,10},{9,11},{10,... | collective-permute-start | bytes 245768 | tf_op jit(solution)/shard_map/ppermute | solution.py:279
  52.6 20.5 %collective-permute-start.9 = (bf16[40,1024]{1,0:T(8,128)(2,1)S(1)}, bf16[40,1024]{1,0:T(8,128)(2,1)S(1)}, u32[]{:S(2)}, u32[]{:S(2)}) collective-permute-start(bf16[40,1024]{1,0:T(8,128)(2,1)S(1)} %get-tuple-element.54), channel_id=1, source_target_pairs={{0,3},{1,2},{2,1},{3,0},{4,7},{5,6},{6,5},{7,4},{8,11},{9,10},{10,... | collective-permute-start | bytes 245768 | tf_op jit(solution)/shard_map/ppermute | solution.py:279
  52.7 20.4 %collective-permute-start.10 = (bf16[40,1024]{1,0:T(8,128)(2,1)S(1)}, bf16[40,1024]{1,0:T(8,128)(2,1)S(1)}, u32[]{:S(2)}, u32[]{:S(2)}) collective-permute-start(bf16[40,1024]{1,0:T(8,128)(2,1)S(1)} %get-tuple-element.55), channel_id=1, source_target_pairs={{0,4},{1,5},{2,6},{3,7},{4,0},{5,1},{6,2},{7,3},{8,12},{9,13},{10,... | collective-permute-start | bytes 245768 | tf_op jit(solution)/shard_map/ppermute | solution.py:279
  53.8 19.5 %collective-permute-start.11 = (bf16[40,1024]{1,0:T(8,128)(2,1)S(1)}, bf16[40,1024]{1,0:T(8,128)(2,1)S(1)}, u32[]{:S(2)}, u32[]{:S(2)}) collective-permute-start(bf16[40,1024]{1,0:T(8,128)(2,1)S(1)} %get-tuple-element.56), channel_id=1, source_target_pairs={{0,5},{1,4},{2,7},{3,6},{4,1},{5,0},{6,3},{7,2},{8,13},{9,12},{10,... | collective-permute-start | bytes 245768 | tf_op jit(solution)/shard_map/ppermute | solution.py:279
  69.2 7.3 %collective-permute-start.12 = (bf16[40,1024]{1,0:T(8,128)(2,1)S(1)}, bf16[40,1024]{1,0:T(8,128)(2,1)S(1)}, u32[]{:S(2)}, u32[]{:S(2)}) collective-permute-start(bf16[40,1024]{1,0:T(8,128)(2,1)S(1)} %get-tuple-element.57), channel_id=1, source_target_pairs={{0,6},{1,7},{2,4},{3,5},{4,2},{5,3},{6,0},{7,1},{8,14},{9,15},{10,... | collective-permute-start | bytes 245768 | tf_op jit(solution)/shard_map/ppermute | solution.py:279
  70.9 7.8 %collective-permute-start.13 = (bf16[40,1024]{1,0:T(8,128)(2,1)S(1)}, bf16[40,1024]{1,0:T(8,128)(2,1)S(1)}, u32[]{:S(2)}, u32[]{:S(2)}) collective-permute-start(bf16[40,1024]{1,0:T(8,128)(2,1)S(1)} %get-tuple-element.58), channel_id=1, source_target_pairs={{0,7},{1,6},{2,5},{3,4},{4,3},{5,2},{6,1},{7,0},{8,15},{9,14},{10,... | collective-permute-start | bytes 245768 | tf_op jit(solution)/shard_map/ppermute | solution.py:279
  73.1 7.3 %collective-permute-start.21 = (bf16[40,1024]{1,0:T(8,128)(2,1)S(1)}, bf16[40,1024]{1,0:T(8,128)(2,1)S(1)}, u32[]{:S(2)}, u32[]{:S(2)}) collective-permute-start(bf16[40,1024]{1,0:T(8,128)(2,1)S(1)} %get-tuple-element.71), channel_id=1, source_target_pairs={{0,1},{1,0},{2,3},{3,2},{4,5},{5,4},{6,7},{7,6},{8,9},{9,8},{10,11... | collective-permute-start | bytes 245768 | tf_op jit(solution)/shard_map/ppermute | solution.py:279
  73.2 9.1 %collective-permute-start.22 = (bf16[40,1024]{1,0:T(8,128)(2,1)S(1)}, bf16[40,1024]{1,0:T(8,128)(2,1)S(1)}, u32[]{:S(2)}, u32[]{:S(2)}) collective-permute-start(bf16[40,1024]{1,0:T(8,128)(2,1)S(1)} %get-tuple-element.72), channel_id=1, source_target_pairs={{0,2},{1,3},{2,0},{3,1},{4,6},{5,7},{6,4},{7,5},{8,10},{9,11},{10,... | collective-permute-start | bytes 245768 | tf_op jit(solution)/shard_map/ppermute | solution.py:279
  73.3 24.2 %collective-permute-start.31 = (bf16[160,512]{1,0:T(8,128)(2,1)S(1)}, bf16[160,512]{1,0:T(8,128)(2,1)S(1)}, u32[]{:S(2)}, u32[]{:S(2)}) collective-permute-start(bf16[160,512]{1,0:T(8,128)(2,1)S(1)} %get-tuple-element.80), channel_id=1, source_target_pairs={{0,8},{8,0},{16,24},{24,16},{1,9},{9,1},{17,25},{25,17},{2,10},{10... | collective-permute-start | bytes 491528 | tf_op jit(solution)/shard_map/ppermute | solution.py:284
  76.5 7.0 %collective-permute-start.23 = (bf16[40,1024]{1,0:T(8,128)(2,1)S(1)}, bf16[40,1024]{1,0:T(8,128)(2,1)S(1)}, u32[]{:S(2)}, u32[]{:S(2)}) collective-permute-start(bf16[40,1024]{1,0:T(8,128)(2,1)S(1)} %get-tuple-element.73), channel_id=1, source_target_pairs={{0,3},{1,2},{2,1},{3,0},{4,7},{5,6},{6,5},{7,4},{8,11},{9,10},{10,... | collective-permute-start | bytes 245768 | tf_op jit(solution)/shard_map/ppermute | solution.py:279
  78.7 13.0 %collective-permute-start.24 = (bf16[40,1024]{1,0:T(8,128)(2,1)S(1)}, bf16[40,1024]{1,0:T(8,128)(2,1)S(1)}, u32[]{:S(2)}, u32[]{:S(2)}) collective-permute-start(bf16[40,1024]{1,0:T(8,128)(2,1)S(1)} %get-tuple-element.74), channel_id=1, source_target_pairs={{0,4},{1,5},{2,6},{3,7},{4,0},{5,1},{6,2},{7,3},{8,12},{9,13},{10,... | collective-permute-start | bytes 245768 | tf_op jit(solution)/shard_map/ppermute | solution.py:279
  80.4 13.7 %collective-permute-start.25 = (bf16[40,1024]{1,0:T(8,128)(2,1)S(1)}, bf16[40,1024]{1,0:T(8,128)(2,1)S(1)}, u32[]{:S(2)}, u32[]{:S(2)}) collective-permute-start(bf16[40,1024]{1,0:T(8,128)(2,1)S(1)} %get-tuple-element.75), channel_id=1, source_target_pairs={{0,5},{1,4},{2,7},{3,6},{4,1},{5,0},{6,3},{7,2},{8,13},{9,12},{10,... | collective-permute-start | bytes 245768 | tf_op jit(solution)/shard_map/ppermute | solution.py:279
  82.3 13.2 %collective-permute-start.26 = (bf16[40,1024]{1,0:T(8,128)(2,1)S(1)}, bf16[40,1024]{1,0:T(8,128)(2,1)S(1)}, u32[]{:S(2)}, u32[]{:S(2)}) collective-permute-start(bf16[40,1024]{1,0:T(8,128)(2,1)S(1)} %get-tuple-element.76), channel_id=1, source_target_pairs={{0,6},{1,7},{2,4},{3,5},{4,2},{5,3},{6,0},{7,1},{8,14},{9,15},{10,... | collective-permute-start | bytes 245768 | tf_op jit(solution)/shard_map/ppermute | solution.py:279
  83.5 13.5 %collective-permute-start.27 = (bf16[40,1024]{1,0:T(8,128)(2,1)S(1)}, bf16[40,1024]{1,0:T(8,128)(2,1)S(1)}, u32[]{:S(2)}, u32[]{:S(2)}) collective-permute-start(bf16[40,1024]{1,0:T(8,128)(2,1)S(1)} %get-tuple-element.77), channel_id=1, source_target_pairs={{0,7},{1,6},{2,5},{3,4},{4,3},{5,2},{6,1},{7,0},{8,15},{9,14},{10,... | collective-permute-start | bytes 245768 | tf_op jit(solution)/shard_map/ppermute | solution.py:279
  91.7 21.4 %collective-permute-start.30 = (bf16[160,768]{1,0:T(8,128)(2,1)S(1)}, bf16[160,768]{1,0:T(8,128)(2,1)S(1)}, u32[]{:S(2)}, u32[]{:S(2)}) collective-permute-start(bf16[160,768]{1,0:T(8,128)(2,1)S(1)} %get-tuple-element.78.refs_0_), channel_id=1, source_target_pairs={{0,24},{8,16},{16,8},{24,0},{1,25},{9,17},{17,9},{25,1},{2,26},{10... | collective-permute-start | bytes 737288 | tf_op jit(solution)/shard_map/ppermute | solution.py:284
  94.1 19.0 %collective-permute-start.29 = (bf16[160,768]{1,0:T(8,128)(2,1)S(1)}, bf16[160,768]{1,0:T(8,128)(2,1)S(1)}, u32[]{:S(2)}, u32[]{:S(2)}) collective-permute-start(bf16[160,768]{1,0:T(8,128)(2,1)S(1)} %get-tuple-element.78.refs_0_), channel_id=1, source_target_pairs={{0,16},{8,24},{16,0},{24,8},{1,17},{9,25},{17,1},{25,9},{2,18},{10... | collective-permute-start | bytes 737288 | tf_op jit(solution)/shard_map/ppermute | solution.py:284
  95.5 17.6 %collective-permute-start.28 = (bf16[160,768]{1,0:T(8,128)(2,1)S(1)}, bf16[160,768]{1,0:T(8,128)(2,1)S(1)}, u32[]{:S(2)}, u32[]{:S(2)}) collective-permute-start(bf16[160,768]{1,0:T(8,128)(2,1)S(1)} %get-tuple-element.78.refs_0_), channel_id=1, source_target_pairs={{0,8},{8,0},{16,24},{24,16},{1,9},{9,1},{17,25},{25,17},{2,10},{10... | collective-permute-start | bytes 737288 | tf_op jit(solution)/shard_map/ppermute | solution.py:284
  97.0 16.1 %collective-permute-start.32 = (bf16[160,512]{1,0:T(8,128)(2,1)S(1)}, bf16[160,512]{1,0:T(8,128)(2,1)S(1)}, u32[]{:S(2)}, u32[]{:S(2)}) collective-permute-start(bf16[160,512]{1,0:T(8,128)(2,1)S(1)} %get-tuple-element.81), channel_id=1, source_target_pairs={{0,16},{8,24},{16,0},{24,8},{1,17},{9,25},{17,1},{25,9},{2,18},{10... | collective-permute-start | bytes 491528 | tf_op jit(solution)/shard_map/ppermute | solution.py:284
  97.5 15.6 %collective-permute-start.33 = (bf16[160,512]{1,0:T(8,128)(2,1)S(1)}, bf16[160,512]{1,0:T(8,128)(2,1)S(1)}, u32[]{:S(2)}, u32[]{:S(2)}) collective-permute-start(bf16[160,512]{1,0:T(8,128)(2,1)S(1)} %get-tuple-element.82), channel_id=1, source_target_pairs={{0,24},{8,16},{16,8},{24,0},{1,25},{9,17},{17,9},{25,1},{2,26},{10... | collective-permute-start | bytes 491528 | tf_op jit(solution)/shard_map/ppermute | solution.py:284
  (16 other events, 302.0 us)

commit v2 on v1

v2 whole, which is shorter than its diff:
```python
import functools

import jax
import jax.numpy as jnp
from jax import lax
from jax.experimental import pallas as pl
from jax.experimental.pallas import tpu as pltpu
from jax.sharding import PartitionSpec as P

PAIR_ROWS = 20
MOST = 16
HALVES = 2
BLOCK_ROWS = HALVES * PAIR_ROWS
CHUNK = 8
FF_TILE = 256
VMEM_LIMIT = 64 * 1024 * 1024 - 65536
EXPERT_LIMIT = 64 * 1024 * 1024 - 65536
AHEAD = 4
TIE_O = True
TIE_L = True
TIE_P = ()
TIE_B = "hidden"
GATHER_HIDDEN = False
PREPARE_EARLY = True
TIE_G = True
WAY_C = "permute"
WAY_P = "permute"
WAY_O = "all"
WAY_B = "all"
F32 = jnp.float32
BF16 = jnp.bfloat16

NN = (((1,), (0,)), ((), ()))
NT = (((1,), (1,)), ((), ()))
TN = (((0,), (0,)), ((), ()))


def mm(a, b, dims=NN):
    return lax.dot_general(a, b, dims, preferred_element_type=F32)


def iota(shape, dim):
    return lax.broadcasted_iota(jnp.int32, shape, dim)


def pair_rows_of(ids, codes, counts_ref, group):
    count = jnp.zeros_like(ids)
    base = jnp.zeros_like(ids)
    for expert in range(counts_ref.shape[0]):
        hit = ids == expert
        count = jnp.where(hit, counts_ref[expert], count)
        if expert % 2:
            base = jnp.where(hit, counts_ref[expert - 1], base)
    laps = jnp.floor((codes.astype(F32) + 0.5) / count.astype(F32)).astype(jnp.int32)
    bucket = codes - laps * count
    return ((ids >> 1) ^ group) * BLOCK_ROWS + base + bucket


def membership(rows, total, values):
    picks, tokens = rows.shape
    index = iota((total, tokens), 0)
    parts = []
    for half in range(HALVES):
        part = jnp.zeros((total, tokens), F32)
        for pick in range(picks):
            hit = index == rows[pick : pick + 1, :] + half * PAIR_ROWS
            value = 1.0 if values is None else values[pick : pick + 1, :]
            part = jnp.where(hit, value, part)
        parts.append(part)
    return jnp.concatenate(parts, axis=1)


def split_halves(x):
    width = x.shape[1] // HALVES
    return jnp.concatenate([x[:, :width], x[:, width:]], axis=0)


def row_places(row, blocks):
    inside = jnp.floor((row.astype(F32) + 0.5) * (1.0 / blocks)).astype(jnp.int32)
    return (row - inside * blocks) * BLOCK_ROWS + inside


def unpack_rows(blocks):
    flat = jnp.concatenate(blocks, axis=0)
    count = len(blocks)
    shape = (count * PAIR_ROWS, count * BLOCK_ROWS)
    place = row_places(iota(shape, 0), count)
    col = iota(shape, 1)
    out = []
    for half in range(HALVES):
        pick = (col == place + half * PAIR_ROWS).astype(F32).astype(BF16)
        out.append(mm(pick, flat).astype(BF16))
    return jnp.concatenate(out, axis=1)


class Blocks:
    def __init__(self, refs, group):
        self.refs, self.group = refs, group

    def at(self, j):
        if len(self.refs) > 1:
            return self.refs[j]
        return self.refs[0].at[self.group ^ j]

    def load(self, start, stop):
        return [self.at(j)[...] for j in range(start, stop)]

    def store(self, start, flat):
        for j in range(flat.shape[0] // BLOCK_ROWS):
            self.at(start + j)[...] = flat[j * BLOCK_ROWS : (j + 1) * BLOCK_ROWS].astype(BF16)


def pack_windows(parts, n, c, size, counts_ref, group, dims):
    total = None
    for e, (x, (start, stop)) in enumerate(zip(parts, windows(n))):
        shape = (size * BLOCK_ROWS, stop - start)
        row = iota(shape, 0)
        index = iota(shape, 1) + start
        inside = jnp.floor((index.astype(F32) + 0.5) * (1.0 / n)).astype(jnp.int32)
        place = (index - inside * n - c) * BLOCK_ROWS + inside
        first = inside < counts_ref[2 * group]
        place = jnp.where(first if e == 0 else jnp.logical_not(first), place, -BLOCK_ROWS * n)
        if n > size:
            block = index - inside * n
            place = jnp.where((block >= c) & (block < c + size), place, -BLOCK_ROWS * n)
        picks = [(row == place + h * PAIR_ROWS).astype(F32).astype(BF16) for h in range(HALVES)]
        part = None
        half = x.shape[1 if dims == NN else 0] // HALVES
        for h, pick in enumerate(picks):
            piece = x[:, h * half : (h + 1) * half] if dims == NN else x[h * half : (h + 1) * half, :]
            product = mm(pick, piece, dims)
            part = product if part is None else part + product
        total = part if total is None else total + part
    return total


def windows(n):
    return (0, MOST * n), ((PAIR_ROWS - MOST) * n, PAIR_ROWS * n)


def owned(e, start, stop, n, counts_ref, group):
    index = iota((stop - start, 1), 0) + start
    first = index < counts_ref[2 * group] * n
    return first if e == 0 else jnp.logical_not(first)


def gather_kernel(mean, n, group_ref, counts_ref, ids_ref, codes_ref, weights_ref, x_ref, *outs):
    group = group_ref[0]
    rows = pair_rows_of(ids_ref[...], codes_ref[...], counts_ref, group)
    member = membership(rows, n * BLOCK_ROWS, None if mean else weights_ref[...])
    sums = mm(member.astype(BF16), split_halves(x_ref[...]))
    if mean:
        sums = sums / jnp.maximum(jnp.sum(member, axis=1, keepdims=True), 1.0)
    Blocks(outs, group).store(0, sums)


def own_scale(scale_ref, group, e):
    row = iota(scale_ref.shape, 0)
    return jnp.sum(jnp.where(row == 2 * group + e, scale_ref[...].astype(F32), 0.0), axis=0, keepdims=True)


def gain_of(ids, weights, scale):
    experts, tokens = scale.shape[0], ids.shape[1]
    expert = iota((experts, tokens), 0)
    mix = jnp.zeros((experts, tokens), F32)
    for pick in range(ids.shape[0]):
        mix = jnp.where(expert == ids[pick : pick + 1, :], weights[pick : pick + 1, :], mix)
    high = mix.astype(BF16)
    low = (mix - high.astype(F32)).astype(BF16)
    return mm(high, scale, TN) + mm(low, scale, TN)


def prepare_kernel(n, counts_ref, group_ref, ids_ref, codes_ref, weights_ref, tok_ref, cot_ref, scale_ref, *outs):
    base_l_ref, base_g_ref, mix_l_ref, mix_g_ref = outs
    ids = ids_ref[...]
    weights = weights_ref[...]
    gain = gain_of(ids, weights, scale_ref[...])
    base_l_ref[...] = gain * tok_ref[...].astype(F32)
    base_g_ref[...] = gain * cot_ref[...].astype(F32)
    rows = pair_rows_of(ids, codes_ref[...], counts_ref, group_ref[0])
    member = membership(rows, n * BLOCK_ROWS, None)
    divisor = jnp.maximum(jnp.sum(member, axis=1, keepdims=True), 1.0)
    mix_g_ref[...] = (member / divisor).T.astype(BF16)
    mix_l_ref[...] = membership(rows, n * BLOCK_ROWS, weights).T.astype(BF16)


def spread_kernel(n, group_ref, base_ref, mix_ref, *refs):
    blocks, out_ref = refs[:-1], refs[-1]
    flat = jnp.concatenate(Blocks(blocks, group_ref[0]).load(0, n), axis=0)
    back = mm(mix_ref[...], flat)
    tokens, width = out_ref.shape
    half = width // HALVES
    for h in range(HALVES):
        cols = slice(h * half, (h + 1) * half)
        out_ref[:, cols] = (base_ref[:, cols] + back[h * tokens : (h + 1) * tokens]).astype(BF16)


class Weights:
    def __init__(self, hbm, vmem, sems):
        self.hbm, self.vmem, self.sems = hbm, vmem, sems
        self.per = vmem[0].shape[2] // FF_TILE
        self.steps = vmem[0].shape[0] * self.per

    def views(self, s):
        e = s // self.per
        cols = pl.ds(pl.multiple_of((s - e * self.per) * FF_TILE, FF_TILE), FF_TILE)
        return [(e, slice(None), cols)] * 2 + [(e, cols, slice(None))]

    def copies(self, s):
        return [
            pltpu.make_async_copy(h.at[view], v.at[view], self.sems.at[s, i])
            for i, (h, v, view) in enumerate(zip(self.hbm, self.vmem, self.views(s)))
        ]

    def start(self, s):
        for copy in self.copies(s):
            copy.start()

    def run(self, body):
        for e in range(self.vmem[0].shape[0]):

            def step(f, carry):
                s = e * self.per + f

                @pl.when(s + AHEAD < self.steps)
                def _():
                    self.start(s + AHEAD)

                for copy in self.copies(s):
                    copy.wait()
                cols = pl.ds(pl.multiple_of(f * FF_TILE, FF_TILE), FF_TILE)
                body(e, cols, *[v.at[view] for v, view in zip(self.vmem, self.views(s))])
                return carry

            lax.fori_loop(0, self.per, step, 0)


def unpack_all(x_ref, blocks, n):
    size = min(CHUNK, n)
    for c in range(0, n, size):
        part = unpack_rows(blocks.load(c, c + size))
        if n == size:
            x_ref[...] = part
        else:
            for r in range(PAIR_ROWS):
                x_ref[r * n + c : r * n + c + size, :] = part[r * size : (r + 1) * size]


def forward_kernel(n, n_in, n_out, counts_ref, group_ref, scale_ref, wg_hbm, wu_hbm, wd_hbm, *refs):
    group = group_ref[0]
    blocks, outs = Blocks(refs[:n_in], group), Blocks(refs[n_in : n_in + n_out], group)
    hidden_ref, slope_ref, silu_ref, x_ref, acc_ref, wg_ref, wu_ref, wd_ref, sems = refs[n_in + n_out :]
    weights = Weights((wg_hbm, wu_hbm, wd_hbm), (wg_ref, wu_ref, wd_ref), sems)
    for s in range(AHEAD):
        weights.start(s)
    unpack_all(x_ref, blocks, n)
    hidden_ref[...] = jnp.zeros_like(hidden_ref)
    for e, (start, stop) in enumerate(windows(n)):
        scale = own_scale(scale_ref, group, e)
        acc_ref[e] = -(scale * x_ref[start:stop, :].astype(F32))

    def body(e, cols, wg, wu, wd):
        start, stop = windows(n)[e]
        mine = owned(e, start, stop, n, counts_ref, group)
        x = x_ref[start:stop, :]
        gate = mm(x, wg[...])
        up = mm(x, wu[...])
        sg = 1.0 / (1.0 + jnp.exp(-gate))
        silu = gate * sg
        hidden = (silu * up).astype(BF16)
        slope = up * sg * (1.0 + gate * (1.0 - sg))
        acc_ref[e] += mm(hidden, wd[...])
        hidden_ref[start:stop, cols] = jnp.where(mine, hidden, hidden_ref[start:stop, cols])
        slope_ref[e, cols, :] = slope.T
        silu_ref[e, cols, :] = silu.T

    weights.run(body)
    size = min(n, CHUNK)
    parts = [acc_ref[e].astype(BF16) for e in range(2)]
    for c in range(0, n, size):
        outs.store(c, pack_windows(parts, n, c, size, counts_ref, group, NN))


def unpack_kernel(n, n_in, parts, dp_ref, group_ref, *refs):
    blocks, pull_ref, shares = Blocks(refs[:n_in], group_ref[0]), refs[n_in], refs[n_in + 1 :]
    unpack_all(pull_ref, blocks, n)
    width = pull_ref.shape[1] // parts
    for k, share in enumerate(shares):
        start = pl.multiple_of((dp_ref[0] ^ k) * width, width)
        share[...] = pull_ref[:, pl.ds(start, width)]


def backward_kernel(n, n_out, counts_ref, group_ref, scale_ref, wg_hbm, wu_hbm, wd_hbm, pull_ref, slope_ref, silu_ref, *refs):
    group = group_ref[0]
    outs = Blocks(refs[:n_out], group)
    turned_ref, acc_ref, wg_ref, wu_ref, wd_ref, sems = refs[n_out:]
    weights = Weights((wg_hbm, wu_hbm, wd_hbm), (wg_ref, wu_ref, wd_ref), sems)
    for s in range(AHEAD):
        weights.start(s)
    for e, (start, stop) in enumerate(windows(n)):
        pull = pull_ref[start:stop, :].astype(F32)
        turned_ref[e] = pull.T.astype(BF16)
        acc_ref[e] = -(own_scale(scale_ref, group, e) * pull).T

    def body(e, cols, wg, wu, wd):
        d_hidden = mm(wd[...], turned_ref[e])
        d_gate = (d_hidden * slope_ref[e, cols, :]).astype(BF16)
        d_up = (d_hidden * silu_ref[e, cols, :]).astype(BF16)
        acc_ref[e] += mm(wg[...], d_gate) + mm(wu[...], d_up)

    weights.run(body)
    size = min(n, CHUNK)
    parts = [acc_ref[e].astype(BF16) for e in range(2)]
    for c in range(0, n, size):
        outs.store(c, pack_windows(parts, n, c, size, counts_ref, group, NT))


def grad_kernel(n, parts, counts_ref, group_ref, dp_ref, *refs):
    if GATHER_HIDDEN:
        hidden = [refs[0].at[dp_ref[0] ^ k] for k in range(parts)]
    else:
        hidden = refs[:parts]
    shares, out_ref = refs[-1 - parts : -1], refs[-1]
    for e in range(2):
        start, stop = windows(n)[e]
        mine = owned(e, start, stop, n, counts_ref, group_ref[0])
        h_all = jnp.concatenate([h[start:stop, :] for h in hidden], axis=0)
        pull = jnp.concatenate(
            [jnp.where(mine, s[start:stop, :].astype(F32), 0.0).astype(BF16) for s in shares], axis=0
        )
        out_ref[e] = mm(h_all, pull, TN).astype(BF16)


SMEM = pl.BlockSpec(memory_space=pltpu.SMEM)
VMEM = pl.BlockSpec(memory_space=pltpu.VMEM)
HBM = pl.BlockSpec(memory_space=pltpu.HBM)


def call(kernel, ins, outs, flops, nbytes, scratch=(), limit=VMEM_LIMIT):
    arrays, specs, buffers = [], [], []
    for x, way in ins:
        if way in ("copy", "scalars", "stay"):
            x = pltpu.with_memory_space_constraint(x, pltpu.HBM)
        if way == "copy":
            buffers.append(pltpu.VMEM(x.shape, x.dtype))
        if way == "scalars":
            buffers.append(pltpu.SMEM(x.shape, x.dtype))
        arrays.append(x)
        specs.append({"smem": SMEM, "vmem": VMEM}.get(way, HBM))
    ways = [way for _, way in ins]
    copied = [i for i, way in enumerate(ways) if way in ("copy", "scalars")]
    if copied:
        buffers.append(pltpu.SemaphoreType.DMA((len(copied),)))

    def body(*refs):
        refs = list(refs)
        if copied:
            given = refs[len(refs) - len(buffers) : -1]
            sems = refs[-1]
            refs = refs[: len(refs) - len(buffers)]
            copies = [pltpu.make_async_copy(refs[i], given[k], sems.at[k]) for k, i in enumerate(copied)]
            for copy in copies:
                copy.start()
            for copy in copies:
                copy.wait()
            for k, i in enumerate(copied):
                refs[i] = given[k]
        kernel(*refs)

    return pl.pallas_call(
        body,
        out_shape=outs,
        in_specs=specs,
        out_specs=jax.tree.map(lambda _: VMEM, outs),
        scratch_shapes=list(scratch) + buffers,
        compiler_params=pltpu.CompilerParams(vmem_limit_bytes=limit),
        cost_estimate=pl.CostEstimate(flops=flops, bytes_accessed=nbytes, transcendentals=0),
    )(*arrays)


def on_device(
    tokens, expert_ids, bucket_codes, route_weights, cotangent, counts, comp_scale, w_gate, w_up, w_down
):
    tok_count, width = tokens.shape
    n = lax.axis_size("expert")
    parts = lax.axis_size("dp")
    local, _, ff = w_gate.shape
    expert_total = counts.shape[0]
    half = width // HALVES
    rows = n * PAIR_ROWS
    total = n * BLOCK_ROWS
    most = n * MOST
    group = lax.axis_index("expert").astype(jnp.int32).reshape(1)
    dp = lax.axis_index("dp").astype(jnp.int32).reshape(1)
    ids, codes, weights = expert_ids.T, bucket_codes.T, route_weights.T
    block_bytes = total * width
    picks = ids.shape[0]

    def layout(way):
        if way == "permute":
            return [jax.ShapeDtypeStruct((BLOCK_ROWS, half), BF16)] * n
        return [jax.ShapeDtypeStruct((n, BLOCK_ROWS, half), BF16)]

    def exchange(way, values):
        if way == "permute":
            return [values[0]] + [
                lax.ppermute(values[k], "expert", [(i, i ^ k) for i in range(n)])
                for k in sorted(range(1, n))
            ]
        return [lax.all_to_all(values[0], "expert", split_axis=0, concat_axis=0, tiled=True)]

    def exchange_dp(values):
        return [values[0]] + [
            lax.ppermute(values[k], "dp", [(i, i ^ k) for i in range(parts)]) for k in range(1, parts)
        ]

    scalars = (counts, "scalars")
    place = (group, "smem")
    copy = lambda *xs: [(x, "copy") for x in xs]
    vmem = lambda xs: [(x, "vmem") for x in xs]

    def gather(mean, way, x):
        return call(
            functools.partial(gather_kernel, mean, n),
            [place, scalars] + copy(ids, codes, weights, x),
            layout(way),
            2 * total * tok_count * width,
            block_bytes,
        )

    base = jax.ShapeDtypeStruct((tok_count, width), F32)
    mix = jax.ShapeDtypeStruct((HALVES * tok_count, total), BF16)
    sent_c = gather(True, WAY_C, tokens)
    got_c = exchange(WAY_C, sent_c)
    sent_p = gather(False, WAY_P, tie(cotangent, sent_c[0]))
    if TIE_P:
        sent_p = [tie(sent_p[0], [got_c[k] for k in TIE_P])] + list(sent_p[1:])
    got_p = exchange(WAY_P, sent_p)
    base_l, base_g, mix_l, mix_g = call(
        functools.partial(prepare_kernel, n),
        [scalars, place] + copy(ids, codes, weights, tie(tokens, sent_p[0]), cotangent, comp_scale),
        [base, base, mix, mix],
        4 * tok_count * expert_total * width,
        5 * tok_count * width * 4,
    )

    def spread(base, mix, got):
        return call(
            functools.partial(spread_kernel, n),
            [place] + copy(base, mix, *got),
            jax.ShapeDtypeStruct(tokens.shape, BF16),
            2 * total * tok_count * width,
            block_bytes,
        )

    if PREPARE_EARLY:
        got_c, base_l, base_g, mix_l, mix_g = lax.optimization_barrier((got_c, base_l, base_g, mix_l, mix_g))
    weight_bytes = 3 * local * width * ff * 2
    expert_flops = 2 * 3 * rows * local * width * ff
    out_o, out_b = layout(WAY_O), layout(WAY_B)
    stream = [
        pltpu.VMEM(w_gate.shape, BF16),
        pltpu.VMEM(w_up.shape, BF16),
        pltpu.VMEM(w_down.shape, BF16),
        pltpu.SemaphoreType.DMA((local * ff // FF_TILE, 3)),
    ]
    fixed = [scalars, place] + copy(comp_scale) + [(w, "stay") for w in (w_gate, w_up, w_down)]

    results = call(
        functools.partial(forward_kernel, n, len(got_c), len(out_o)),
        fixed + copy(*got_c),
        out_o
        + [
            jax.ShapeDtypeStruct((rows, ff), BF16),
            jax.ShapeDtypeStruct((local, ff, most), F32),
            jax.ShapeDtypeStruct((local, ff, most), F32),
        ],
        expert_flops,
        weight_bytes,
        [pltpu.VMEM((rows, width), BF16), pltpu.VMEM((local, most, width), F32)] + stream,
        EXPERT_LIMIT,
    )
    sent_o, (hidden, slope, silu) = results[: len(out_o)], results[len(out_o) :]
    if TIE_O:
        sent_o = tie(list(sent_o), got_p)
    got_o = exchange(WAY_O, sent_o)
    if GATHER_HIDDEN:
        all_hidden = [lax.all_gather(hidden, "dp")]
    else:
        all_hidden = exchange_dp([hidden] * parts)

    pull_and_shares = call(
        functools.partial(unpack_kernel, n, len(got_p), parts),
        [(dp, "smem"), place] + copy(*got_p),
        [jax.ShapeDtypeStruct((rows, width), BF16)]
        + [jax.ShapeDtypeStruct((rows, width // parts), BF16)] * parts,
        2 * rows * min(n, CHUNK) * BLOCK_ROWS * width,
        2 * block_bytes,
    )
    pull = pull_and_shares[0]
    all_shares = exchange_dp(pull_and_shares[1:])

    sent_b = call(
        functools.partial(backward_kernel, n, len(out_b)),
        fixed + copy(pull, slope, silu),
        out_b,
        expert_flops,
        weight_bytes,
        [pltpu.VMEM((local, width, most), BF16), pltpu.VMEM((local, width, most), F32)] + stream,
        EXPERT_LIMIT,
    )
    if TIE_B == "hidden":
        sent_b = tie(sent_b, all_hidden)
    if TIE_B == "both":
        sent_b = tie(sent_b, (all_hidden, all_shares))
    got_b = exchange(WAY_B, sent_b)

    layer_output = spread(base_l, mix_l, got_o)
    if TIE_L:
        all_shares = tie(all_shares, layer_output)
    grad_down = call(
        functools.partial(grad_kernel, n, parts),
        [scalars, place, (dp, "smem")] + copy(*all_hidden, *all_shares),
        jax.ShapeDtypeStruct((local, ff, width // parts), BF16),
        2 * parts * rows * ff * local * width // parts,
        parts * rows * (ff + width // parts) * 2,
    )
    if TIE_G:
        base_g = tie(base_g, (layer_output, grad_down))
    grad_tokens = spread(base_g, mix_g, got_b)
    return (layer_output, grad_tokens, grad_down)


def tie(x, after):
    return lax.optimization_barrier((x, after))[0]


def solution(mesh):
    token_spec = P(("dp", "expert"), None)
    weight_spec = P("expert", None, None)
    in_specs = (token_spec,) * 5 + (P(), P()) + (weight_spec,) * 3
    out_specs = (token_spec, token_spec, P("expert", None, "dp"))
    return jax.shard_map(
        on_device, mesh=mesh, in_specs=in_specs, out_specs=out_specs, check_vma=False
    )
```

time: 117 us -> 92 us (0.79)
  waiting for transfers between devices: 23.5 us -> 8.38 us
  starting transfers between devices: 50.8 us -> 39.3 us
  Pallas kernels: 34.6 us -> 42.9 us
  local copies, waits for them, and re-layouts: 6.39 us -> 0 us
    ppermute x28 -> x14, starting transfers between devices: 42.1 us -> 22.4 us  [exchange(): lax.ppermute(values[k], 'expert', [(i, i ^ k) for i in range(n)])]
    ppermute x28 -> x14, waiting for transfers between devices: 13.8 us -> 0.04 us  [exchange(): lax.ppermute(values[k], 'expert', [(i, i ^ k) for i in range(n)])]
    all_to_all x0 -> x2, starting transfers between devices: none -> 9.93 us  [exchange(): lax.all_to_all(values[0], 'expert', split_axis=0, concat_axis=0, tiled=True)]
    pallas_call x8 -> x9, Pallas kernels: 34.6 us -> 42.9 us  [call(): pl.pallas_call(body, out_shape=outs, in_specs=specs, out_specs=jax.tree.m...]
    unnamed x28 -> x0, local copies, waits for them, and re-layouts: 5.49 us -> none
    ppermute x6, waiting for transfers between devices: 9.76 us -> 5.45 us  [exchange_dp(): lax.ppermute(values[k], 'dp', [(i, i ^ k) for i in range(parts)])]
    all_to_all x0 -> x2, waiting for transfers between devices: none -> 2.89 us  [exchange(): lax.all_to_all(values[0], 'expert', split_axis=0, concat_axis=0, tiled=True)]
    ppermute x6, starting transfers between devices: 8.79 us -> 6.98 us  [exchange_dp(): lax.ppermute(values[k], 'dp', [(i, i ^ k) for i in range(parts)])]
  transfers between devices with their start and end apart: 34 -> 22, of which waited for: 4 -> 3; matrix products, arithmetic and copies ran while one was open for 1% -> 0% of each run, Pallas kernels for 26% -> 41%
where the time goes in v2:
time: 92 us; the launch traced here: 91.4 us
  Pallas kernels  42.9 us (47%)
  starting transfers between devices  39.3 us (43%)
  waiting for transfers between devices  8.38 us (9%)
    pallas_call x9, Pallas kernels, call(): pl.pallas_call(body, out_shape=outs, in_specs=specs, out_specs=jax.tree.m...  42.9 us
    ppermute x14, starting transfers between devices, exchange(): lax.ppermute(values[k], 'expert', [(i, i ^ k) for i in range(n)])  22.4 us
    all_to_all x2, starting transfers between devices, exchange(): lax.all_to_all(values[0], 'expert', split_axis=0, concat_axis=0, tiled=True)  9.93 us
    ppermute x6, starting transfers between devices, exchange_dp(): lax.ppermute(values[k], 'dp', [(i, i ^ k) for i in range(parts)])  6.98 us
    ppermute x6, waiting for transfers between devices, exchange_dp(): lax.ppermute(values[k], 'dp', [(i, i ^ k) for i in range(parts)])  5.45 us
    all_to_all x2, waiting for transfers between devices, exchange(): lax.all_to_all(values[0], 'expert', split_axis=0, concat_axis=0, tiled=True)  2.89 us
  transfers between devices with their start and end apart: 22, of which 3 were waited for; matrix products, arithmetic and copies ran while one was open for 0% of the time, Pallas kernels for 41%

profile of v2, /device:TPU:0, one launch (start us, length us, event | category | flops | bytes accessed | tf_op | source)
XLA Modules:
  0.0 91.4 jit_solution(13259448389720837912)
XLA Ops:
  0.6 2.4 %shard_map.121 = (bf16[40,1024]{1,0:T(8,128)(2,1)}, bf16[40,1024]{1,0:T(8,128)(2,1)}, bf16[40,1024]{1,0:T(8,128)(2,1)}, bf16[40,1024]{1,0:T(8,128)(2,1)}, bf16[4...) custom-call(s32[1]{0:T(128)} %bitcast.refs_0_.refs_1_, ...), custom_call_target="tpu_custom_call" | custom-call | flops 167772160 | bytes 655360 | tf_op jit(solution)/shard_map/pallas_call | solution.py:370
  3.0 0.5 collective-permute-start
  3.5 2.7 %collective-permute-start.1 = (bf16[40,1024]{1,0:T(8,128)(2,1)}, bf16[40,1024]{1,0:T(8,128)(2,1)}, u32[]{:S(2)}, u32[]{:S(2)}) collective-permute-start(bf16[40,1024]{1,0:T(8,128)(2,1)} %get-tuple-element.55), channel_id=1, source_target_pairs={{0,2},{1,3},{2,0},{3,1},{4,6},{5,7},{6,4},{7,5},{8,10},{9,11},{10,... | collective-permute-start | bytes 245768 | tf_op jit(solution)/shard_map/ppermute | solution.py:407
  6.2 0.1 collective-permute-start.2
  6.2 2.8 %collective-permute-start.3 = (bf16[40,1024]{1,0:T(8,128)(2,1)}, bf16[40,1024]{1,0:T(8,128)(2,1)}, u32[]{:S(2)}, u32[]{:S(2)}) collective-permute-start(bf16[40,1024]{1,0:T(8,128)(2,1)} %get-tuple-element.57), channel_id=1, source_target_pairs={{0,4},{1,5},{2,6},{3,7},{4,0},{5,1},{6,2},{7,3},{8,12},{9,13},{10,... | collective-permute-start | bytes 245768 | tf_op jit(solution)/shard_map/ppermute | solution.py:407
  9.0 0.0 collective-permute-start.4
  9.0 3.6 %collective-permute-start.5 = (bf16[40,1024]{1,0:T(8,128)(2,1)}, bf16[40,1024]{1,0:T(8,128)(2,1)}, u32[]{:S(2)}, u32[]{:S(2)}) collective-permute-start(bf16[40,1024]{1,0:T(8,128)(2,1)} %get-tuple-element.59), channel_id=1, source_target_pairs={{0,6},{1,7},{2,4},{3,5},{4,2},{5,3},{6,0},{7,1},{8,14},{9,15},{10,... | collective-permute-start | bytes 245768 | tf_op jit(solution)/shard_map/ppermute | solution.py:407
  12.6 0.1 collective-permute-start.6
  12.7 2.3 %shard_map.122 = (bf16[40,1024]{1,0:T(8,128)(2,1)}, bf16[40,1024]{1,0:T(8,128)(2,1)}, bf16[40,1024]{1,0:T(8,128)(2,1)}, bf16[40,1024]{1,0:T(8,128)(2,1)}, bf16[4...) custom-call(s32[1]{0:T(128)} %bitcast.refs_0_.refs_1_, ...), custom_call_target="tpu_custom_call" | custom-call | flops 167772160 | bytes 655360 | tf_op jit(solution)/shard_map/pallas_call | solution.py:370
  15.1 1.2 %collective-permute-start.7 = (bf16[40,1024]{1,0:T(8,128)(2,1)}, bf16[40,1024]{1,0:T(8,128)(2,1)}, u32[]{:S(2)}, u32[]{:S(2)}) collective-permute-start(bf16[40,1024]{1,0:T(8,128)(2,1)} %get-tuple-element.79), channel_id=1, source_target_pairs={{0,1},{1,0},{2,3},{3,2},{4,5},{5,4},{6,7},{7,6},{8,9},{9,8},{10,11... | collective-permute-start | bytes 245768 | tf_op jit(solution)/shard_map/ppermute | solution.py:407
  16.3 4.2 %collective-permute-start.8 = (bf16[40,1024]{1,0:T(8,128)(2,1)}, bf16[40,1024]{1,0:T(8,128)(2,1)}, u32[]{:S(2)}, u32[]{:S(2)}) collective-permute-start(bf16[40,1024]{1,0:T(8,128)(2,1)} %get-tuple-element.80), channel_id=1, source_target_pairs={{0,2},{1,3},{2,0},{3,1},{4,6},{5,7},{6,4},{7,5},{8,10},{9,11},{10,... | collective-permute-start | bytes 245768 | tf_op jit(solution)/shard_map/ppermute | solution.py:407
  20.5 3.5 %shard_map.123 = (f32[128,2048]{1,0:T(8,128)}, f32[128,2048]{1,0:T(8,128)}, bf16[256,320]{1,0:T(8,128)(2,1)}, bf16[256,320]{1,0:T(8,128)(2,1)}) custom-call(s32[16]{0:T(128)} %refs_0_.7, s32[1]{0:T(128)} %bitcast.refs_0_.refs_1_, s32[8,128]{1,0:T(8,128)} %bitcast.7, s32[8,128]{1,0:T(8,128)} %bitcast.10, f32[8,128]{1,0:T(8,128)} %bitcast.13, ...), custom_call_target="tpu_custom_call" | custom-call | flops 16777216 | bytes 5242880 | tf_op jit(solution)/shard_map/pallas_call | solution.py:370
  24.0 0.1 collective-permute-start.9
  24.1 3.4 %collective-permute-start.10 = (bf16[40,1024]{1,0:T(8,128)(2,1)}, bf16[40,1024]{1,0:T(8,128)(2,1)}, u32[]{:S(2)}, u32[]{:S(2)}) collective-permute-start(bf16[40,1024]{1,0:T(8,128)(2,1)} %get-tuple-element.82), channel_id=1, source_target_pairs={{0,4},{1,5},{2,6},{3,7},{4,0},{5,1},{6,2},{7,3},{8,12},{9,13},{10,... | collective-permute-start | bytes 245768 | tf_op jit(solution)/shard_map/ppermute | solution.py:407
  27.5 3.7 %collective-permute-start.12 = (bf16[40,1024]{1,0:T(8,128)(2,1)}, bf16[40,1024]{1,0:T(8,128)(2,1)}, u32[]{:S(2)}, u32[]{:S(2)}) collective-permute-start(bf16[40,1024]{1,0:T(8,128)(2,1)} %get-tuple-element.84), channel_id=1, source_target_pairs={{0,6},{1,7},{2,4},{3,5},{4,2},{5,3},{6,0},{7,1},{8,14},{9,15},{10,... | collective-permute-start | bytes 245768 | tf_op jit(solution)/shard_map/ppermute | solution.py:407
  31.2 10.7 %shard_map.124 = (bf16[8,40,1024]{2,1,0:T(8,128)(2,1)}, bf16[160,768]{1,0:T(8,128)(2,1)}, f32[2,768,128]{2,1,0:T(8,128)}, f32[2,768,128]{2,1,0:T(8,128)}) custom-call(s32[16]{0:T(128)} %refs_0_.7, s32[1]{0:T(128)} %bitcast.refs_0_.refs_1_, bf16[16,2048]{1,0:T(8,128)(2,1)} %refs_2_.3, bf16[2,2048,768]{2,1,0:T(8,128)(2,1)} %refs_3_.3, ...), custom_call_target="tpu_custom_call" | custom-call | flops 3019898880 | bytes 18874368 | tf_op jit(solution)/shard_map/pallas_call | solution.py:370
  42.0 4.8 %all-to-all-start = ((bf16[8,40,1024]{2,1,0:T(8,128)(2,1)}), bf16[8,40,1024]{2,1,0:T(8,128)(2,1)}, u32[]{:S(2)}, u32[]{:S(2)}) async-start(bf16[8,40,1024]{2,1,0:T(8,128)(2,1)} %get-tuple-element.86), calls=%async_computation | async-start | bytes 1310720 | tf_op jit(solution)/shard_map/all_to_all | solution.py:410
  46.8 1.5 %collective-permute-start.14 = (bf16[160,768]{1,0:T(8,128)(2,1)}, bf16[160,768]{1,0:T(8,128)(2,1)}, u32[]{:S(2)}, u32[]{:S(2)}) collective-permute-start(bf16[160,768]{1,0:T(8,128)(2,1)} %get-tuple-element.88.refs_3_), channel_id=1, source_target_pairs={{0,8},{8,0},{16,24},{24,16},{1,9},{9,1},{17,25},{25,17},{2,10},{10... | collective-permute-start | bytes 737288 | tf_op jit(solution)/shard_map/ppermute | solution.py:414
  48.3 1.5 %collective-permute-start.15 = (bf16[160,768]{1,0:T(8,128)(2,1)}, bf16[160,768]{1,0:T(8,128)(2,1)}, u32[]{:S(2)}, u32[]{:S(2)}) collective-permute-start(bf16[160,768]{1,0:T(8,128)(2,1)} %get-tuple-element.88.refs_3_), channel_id=1, source_target_pairs={{0,16},{8,24},{16,0},{24,8},{1,17},{9,25},{17,1},{25,9},{2,18},{10... | collective-permute-start | bytes 737288 | tf_op jit(solution)/shard_map/ppermute | solution.py:414
  49.8 0.5 collective-permute-start.16
  50.3 2.8 %shard_map.126 = (bf16[160,2048]{1,0:T(8,128)(2,1)}, bf16[160,512]{1,0:T(8,128)(2,1)}, bf16[160,512]{1,0:T(8,128)(2,1)}, bf16[160,512]{1,0:T(8,128)(2,1)}, bf16[160,512]{1,0:T(8,128)(2,1)}) custom-call(s32[1]{0:T(128)} %bitcast.4.refs_0_.refs_2_, s32[1]{0:T(128)} %bitcast.refs_0_.refs_1_, bf16[40,1024]{1,0:T(8,128)(2,1)} %get-tuple-element.62.refs_2_, ...), custom_call_target="tpu_custom_call" | custom-call | flops 209715200 | bytes 1310720 | tf_op jit(solution)/shard_map/pallas_call | solution.py:370
  53.1 12.1 %shard_map.128 = bf16[8,40,1024]{2,1,0:T(8,128)(2,1)} custom-call(s32[16]{0:T(128)} %refs_0_.7, s32[1]{0:T(128)} %bitcast.refs_0_.refs_1_, bf16[16,2048]{1,0:T(8,128)(2,1)} %refs_2_.3, bf16[2,2048,768]{2,1,0:T(8,128)(2,1)} %refs_3_.3, bf16[2,2048,768]{2,1,0:T(8,128)(2,1)} %refs_4_.3, bf16[2,768,2048]{2,1,0:T(8,128)(2,1)} %refs_5_.7, ...), custom_call_target="tpu_custom_call" | custom-call | flops 3019898880 | bytes 18874368 | tf_op jit(solution)/shard_map/pallas_call | solution.py:370
  65.3 5.1 %all-to-all-start.1 = ((bf16[8,40,1024]{2,1,0:T(8,128)(2,1)}), bf16[8,40,1024]{2,1,0:T(8,128)(2,1)}, u32[]{:S(2)}, u32[]{:S(2)}) async-start(bf16[8,40,1024]{2,1,0:T(8,128)(2,1)} %shard_map.128), calls=%async_computation.1 | async-start | bytes 1310720 | tf_op jit(solution)/shard_map/all_to_all | solution.py:410
  70.4 1.5 %collective-permute-start.17 = (bf16[160,512]{1,0:T(8,128)(2,1)}, bf16[160,512]{1,0:T(8,128)(2,1)}, u32[]{:S(2)}, u32[]{:S(2)}) collective-permute-start(bf16[160,512]{1,0:T(8,128)(2,1)} %get-tuple-element.90), channel_id=1, source_target_pairs={{0,8},{8,0},{16,24},{24,16},{1,9},{9,1},{17,25},{25,17},{2,10},{10... | collective-permute-start | bytes 491528 | tf_op jit(solution)/shard_map/ppermute | solution.py:414
  71.9 1.5 %collective-permute-start.18 = (bf16[160,512]{1,0:T(8,128)(2,1)}, bf16[160,512]{1,0:T(8,128)(2,1)}, u32[]{:S(2)}, u32[]{:S(2)}) collective-permute-start(bf16[160,512]{1,0:T(8,128)(2,1)} %get-tuple-element.91), channel_id=1, source_target_pairs={{0,16},{8,24},{16,0},{24,8},{1,17},{9,25},{17,1},{25,9},{2,18},{10... | collective-permute-start | bytes 491528 | tf_op jit(solution)/shard_map/ppermute | solution.py:414
  73.4 0.5 collective-permute-start.19
  73.9 2.7 %shard_map.125 = bf16[128,2048]{1,0:T(8,128)(2,1)} custom-call(s32[1]{0:T(128)} %bitcast.refs_0_.refs_1_, f32[128,2048]{1,0:T(8,128)} %get-tuple-element.68.refs_1_, bf16[256,320]{1,0:T(8,128)(2,1)} %get-tuple-element.69.refs_2_, bf16[8,40,1024]{2,1,0:T(8,128)(2,1)} %all-to-all-done.refs_3_), custom_call_target="tpu_custom_call" | custom-call | flops 167772160 | bytes 655360 | tf_op jit(solution)/shard_map/pallas_call | solution.py:370
  76.6 1.1 %collective-permute-done.17.refs_8_ = bf16[160,512]{1,0:T(8,128)(2,1)} collective-permute-done((bf16[160,512]{1,0:T(8,128)(2,1)}, bf16[160,512]{1,0:T(8,128)(2,1)}, u32[]{:S(2)}, u32[]{:S(2)}) %collective-permute-start.17) | collective-permute-done | bytes 163872 | tf_op jit(solution)/shard_map/ppermute | solution.py:414
  77.7 4.3 %collective-permute-done.18.refs_9_ = bf16[160,512]{1,0:T(8,128)(2,1)} collective-permute-done((bf16[160,512]{1,0:T(8,128)(2,1)}, bf16[160,512]{1,0:T(8,128)(2,1)}, u32[]{:S(2)}, u32[]{:S(2)}) %collective-permute-start.18) | collective-permute-done | bytes 163872 | tf_op jit(solution)/shard_map/ppermute | solution.py:414
  82.1 3.7 %shard_map.127 = bf16[2,768,512]{2,1,0:T(8,128)(2,1)} custom-call(s32[16]{0:T(128)} %refs_0_.7, s32[1]{0:T(128)} %bitcast.refs_0_.refs_1_, s32[1]{0:T(128)} %bitcast.4.refs_0_.refs_2_, bf16[160,768]{1,0:T(8,128)(2,1)} %get-tuple-element.88.refs_3_, bf16[160,768]{1,0:T(8,128)(2,1)} %collective-permute-done.14.refs_4_, ...), custom_call_target="tpu_custom_call" | custom-call | flops 1006632960 | bytes 1638400 | tf_op jit(solution)/shard_map/pallas_call | solution.py:370
  85.8 2.9 %all-to-all-done.1.refs_3_ = bf16[8,40,1024]{2,1,0:T(8,128)(2,1)} async-done(((bf16[8,40,1024]{2,1,0:T(8,128)(2,1)}), bf16[8,40,1024]{2,1,0:T(8,128)(2,1)}, u32[]{:S(2)}, u32[]{:S(2)}) %all-to-all-start.1) | async-done | bytes 655392 | tf_op jit(solution)/shard_map/all_to_all | solution.py:410
  88.7 2.7 %shard_map.129 = bf16[128,2048]{1,0:T(8,128)(2,1)} custom-call(s32[1]{0:T(128)} %bitcast.refs_0_.refs_1_, f32[128,2048]{1,0:T(8,128)} %get-tuple-element.97.refs_1_, bf16[256,320]{1,0:T(8,128)(2,1)} %get-tuple-element.98.refs_2_, bf16[8,40,1024]{2,1,0:T(8,128)(2,1)} %all-to-all-done.1.refs_3_), custom_call_target="tpu_custom_call" | custom-call | flops 167772160 | bytes 655360 | tf_op jit(solution)/shard_map/pallas_call | solution.py:370
  (21 shorter events, 0.1 us)
Async XLA Ops:
  3.0 6.0 %collective-permute-start = (bf16[40,1024]{1,0:T(8,128)(2,1)}, bf16[40,1024]{1,0:T(8,128)(2,1)}, u32[]{:S(2)}, u32[]{:S(2)}) collective-permute-start(bf16[40,1024]{1,0:T(8,128)(2,1)} %get-tuple-element.54), channel_id=1, source_target_pairs={{0,1},{1,0},{2,3},{3,2},{4,5},{5,4},{6,7},{7,6},{8,9},{9,8},{10,11... | collective-permute-start | bytes 245768 | tf_op jit(solution)/shard_map/ppermute | solution.py:407
  3.5 9.1 %collective-permute-start.1 = (bf16[40,1024]{1,0:T(8,128)(2,1)}, bf16[40,1024]{1,0:T(8,128)(2,1)}, u32[]{:S(2)}, u32[]{:S(2)}) collective-permute-start(bf16[40,1024]{1,0:T(8,128)(2,1)} %get-tuple-element.55), channel_id=1, source_target_pairs={{0,2},{1,3},{2,0},{3,1},{4,6},{5,7},{6,4},{7,5},{8,10},{9,11},{10,... | collective-permute-start | bytes 245768 | tf_op jit(solution)/shard_map/ppermute | solution.py:407
  6.2 8.9 %collective-permute-start.2 = (bf16[40,1024]{1,0:T(8,128)(2,1)}, bf16[40,1024]{1,0:T(8,128)(2,1)}, u32[]{:S(2)}, u32[]{:S(2)}) collective-permute-start(bf16[40,1024]{1,0:T(8,128)(2,1)} %get-tuple-element.56), channel_id=1, source_target_pairs={{0,3},{1,2},{2,1},{3,0},{4,7},{5,6},{6,5},{7,4},{8,11},{9,10},{10,... | collective-permute-start | bytes 245768 | tf_op jit(solution)/shard_map/ppermute | solution.py:407
  6.2 10.1 %collective-permute-start.3 = (bf16[40,1024]{1,0:T(8,128)(2,1)}, bf16[40,1024]{1,0:T(8,128)(2,1)}, u32[]{:S(2)}, u32[]{:S(2)}) collective-permute-start(bf16[40,1024]{1,0:T(8,128)(2,1)} %get-tuple-element.57), channel_id=1, source_target_pairs={{0,4},{1,5},{2,6},{3,7},{4,0},{5,1},{6,2},{7,3},{8,12},{9,13},{10,... | collective-permute-start | bytes 245768 | tf_op jit(solution)/shard_map/ppermute | solution.py:407
  9.0 15.0 %collective-permute-start.4 = (bf16[40,1024]{1,0:T(8,128)(2,1)}, bf16[40,1024]{1,0:T(8,128)(2,1)}, u32[]{:S(2)}, u32[]{:S(2)}) collective-permute-start(bf16[40,1024]{1,0:T(8,128)(2,1)} %get-tuple-element.58), channel_id=1, source_target_pairs={{0,5},{1,4},{2,7},{3,6},{4,1},{5,0},{6,3},{7,2},{8,13},{9,12},{10,... | collective-permute-start | bytes 245768 | tf_op jit(solution)/shard_map/ppermute | solution.py:407
  9.0 15.0 %collective-permute-start.5 = (bf16[40,1024]{1,0:T(8,128)(2,1)}, bf16[40,1024]{1,0:T(8,128)(2,1)}, u32[]{:S(2)}, u32[]{:S(2)}) collective-permute-start(bf16[40,1024]{1,0:T(8,128)(2,1)} %get-tuple-element.59), channel_id=1, source_target_pairs={{0,6},{1,7},{2,4},{3,5},{4,2},{5,3},{6,0},{7,1},{8,14},{9,15},{10,... | collective-permute-start | bytes 245768 | tf_op jit(solution)/shard_map/ppermute | solution.py:407
  12.6 14.9 %collective-permute-start.6 = (bf16[40,1024]{1,0:T(8,128)(2,1)}, bf16[40,1024]{1,0:T(8,128)(2,1)}, u32[]{:S(2)}, u32[]{:S(2)}) collective-permute-start(bf16[40,1024]{1,0:T(8,128)(2,1)} %get-tuple-element.60), channel_id=1, source_target_pairs={{0,7},{1,6},{2,5},{3,4},{4,3},{5,2},{6,1},{7,0},{8,15},{9,14},{10,... | collective-permute-start | bytes 245768 | tf_op jit(solution)/shard_map/ppermute | solution.py:407
  15.1 12.4 %collective-permute-start.7 = (bf16[40,1024]{1,0:T(8,128)(2,1)}, bf16[40,1024]{1,0:T(8,128)(2,1)}, u32[]{:S(2)}, u32[]{:S(2)}) collective-permute-start(bf16[40,1024]{1,0:T(8,128)(2,1)} %get-tuple-element.79), channel_id=1, source_target_pairs={{0,1},{1,0},{2,3},{3,2},{4,5},{5,4},{6,7},{7,6},{8,9},{9,8},{10,11... | collective-permute-start | bytes 245768 | tf_op jit(solution)/shard_map/ppermute | solution.py:407
  16.3 14.9 %collective-permute-start.8 = (bf16[40,1024]{1,0:T(8,128)(2,1)}, bf16[40,1024]{1,0:T(8,128)(2,1)}, u32[]{:S(2)}, u32[]{:S(2)}) collective-permute-start(bf16[40,1024]{1,0:T(8,128)(2,1)} %get-tuple-element.80), channel_id=1, source_target_pairs={{0,2},{1,3},{2,0},{3,1},{4,6},{5,7},{6,4},{7,5},{8,10},{9,11},{10,... | collective-permute-start | bytes 245768 | tf_op jit(solution)/shard_map/ppermute | solution.py:407
  24.0 18.0 %collective-permute-start.9 = (bf16[40,1024]{1,0:T(8,128)(2,1)}, bf16[40,1024]{1,0:T(8,128)(2,1)}, u32[]{:S(2)}, u32[]{:S(2)}) collective-permute-start(bf16[40,1024]{1,0:T(8,128)(2,1)} %get-tuple-element.81), channel_id=1, source_target_pairs={{0,3},{1,2},{2,1},{3,0},{4,7},{5,6},{6,5},{7,4},{8,11},{9,10},{10,... | collective-permute-start | bytes 245768 | tf_op jit(solution)/shard_map/ppermute | solution.py:407
  24.1 17.9 %collective-permute-start.10 = (bf16[40,1024]{1,0:T(8,128)(2,1)}, bf16[40,1024]{1,0:T(8,128)(2,1)}, u32[]{:S(2)}, u32[]{:S(2)}) collective-permute-start(bf16[40,1024]{1,0:T(8,128)(2,1)} %get-tuple-element.82), channel_id=1, source_target_pairs={{0,4},{1,5},{2,6},{3,7},{4,0},{5,1},{6,2},{7,3},{8,12},{9,13},{10,... | collective-permute-start | bytes 245768 | tf_op jit(solution)/shard_map/ppermute | solution.py:407
  27.5 14.4 %collective-permute-start.11 = (bf16[40,1024]{1,0:T(8,128)(2,1)}, bf16[40,1024]{1,0:T(8,128)(2,1)}, u32[]{:S(2)}, u32[]{:S(2)}) collective-permute-start(bf16[40,1024]{1,0:T(8,128)(2,1)} %get-tuple-element.83), channel_id=1, source_target_pairs={{0,5},{1,4},{2,7},{3,6},{4,1},{5,0},{6,3},{7,2},{8,13},{9,12},{10,... | collective-permute-start | bytes 245768 | tf_op jit(solution)/shard_map/ppermute | solution.py:407
  27.5 14.4 %collective-permute-start.12 = (bf16[40,1024]{1,0:T(8,128)(2,1)}, bf16[40,1024]{1,0:T(8,128)(2,1)}, u32[]{:S(2)}, u32[]{:S(2)}) collective-permute-start(bf16[40,1024]{1,0:T(8,128)(2,1)} %get-tuple-element.84), channel_id=1, source_target_pairs={{0,6},{1,7},{2,4},{3,5},{4,2},{5,3},{6,0},{7,1},{8,14},{9,15},{10,... | collective-permute-start | bytes 245768 | tf_op jit(solution)/shard_map/ppermute | solution.py:407
  31.2 10.7 %collective-permute-start.13 = (bf16[40,1024]{1,0:T(8,128)(2,1)}, bf16[40,1024]{1,0:T(8,128)(2,1)}, u32[]{:S(2)}, u32[]{:S(2)}) collective-permute-start(bf16[40,1024]{1,0:T(8,128)(2,1)} %get-tuple-element.85), channel_id=1, source_target_pairs={{0,7},{1,6},{2,5},{3,4},{4,3},{5,2},{6,1},{7,0},{8,15},{9,14},{10,... | collective-permute-start | bytes 245768 | tf_op jit(solution)/shard_map/ppermute | solution.py:407
  42.0 23.3 %all-to-all-start = ((bf16[8,40,1024]{2,1,0:T(8,128)(2,1)}), bf16[8,40,1024]{2,1,0:T(8,128)(2,1)}, u32[]{:S(2)}, u32[]{:S(2)}) async-start(bf16[8,40,1024]{2,1,0:T(8,128)(2,1)} %get-tuple-element.86), calls=%async_computation | async-start | bytes 1310720 | tf_op jit(solution)/shard_map/all_to_all | solution.py:410
  46.8 18.5 %collective-permute-start.14 = (bf16[160,768]{1,0:T(8,128)(2,1)}, bf16[160,768]{1,0:T(8,128)(2,1)}, u32[]{:S(2)}, u32[]{:S(2)}) collective-permute-start(bf16[160,768]{1,0:T(8,128)(2,1)} %get-tuple-element.88.refs_3_), channel_id=1, source_target_pairs={{0,8},{8,0},{16,24},{24,16},{1,9},{9,1},{17,25},{25,17},{2,10},{10... | collective-permute-start | bytes 737288 | tf_op jit(solution)/shard_map/ppermute | solution.py:414
  48.3 17.0 %collective-permute-start.15 = (bf16[160,768]{1,0:T(8,128)(2,1)}, bf16[160,768]{1,0:T(8,128)(2,1)}, u32[]{:S(2)}, u32[]{:S(2)}) collective-permute-start(bf16[160,768]{1,0:T(8,128)(2,1)} %get-tuple-element.88.refs_3_), channel_id=1, source_target_pairs={{0,16},{8,24},{16,0},{24,8},{1,17},{9,25},{17,1},{25,9},{2,18},{10... | collective-permute-start | bytes 737288 | tf_op jit(solution)/shard_map/ppermute | solution.py:414
  49.8 15.5 %collective-permute-start.16 = (bf16[160,768]{1,0:T(8,128)(2,1)}, bf16[160,768]{1,0:T(8,128)(2,1)}, u32[]{:S(2)}, u32[]{:S(2)}) collective-permute-start(bf16[160,768]{1,0:T(8,128)(2,1)} %get-tuple-element.88.refs_3_), channel_id=1, source_target_pairs={{0,24},{8,16},{16,8},{24,0},{1,25},{9,17},{17,9},{25,1},{2,26},{10... | collective-permute-start | bytes 737288 | tf_op jit(solution)/shard_map/ppermute | solution.py:414
  65.3 23.4 %all-to-all-start.1 = ((bf16[8,40,1024]{2,1,0:T(8,128)(2,1)}), bf16[8,40,1024]{2,1,0:T(8,128)(2,1)}, u32[]{:S(2)}, u32[]{:S(2)}) async-start(bf16[8,40,1024]{2,1,0:T(8,128)(2,1)} %shard_map.128), calls=%async_computation.1 | async-start | bytes 1310720 | tf_op jit(solution)/shard_map/all_to_all | solution.py:410
  70.4 7.3 %collective-permute-start.17 = (bf16[160,512]{1,0:T(8,128)(2,1)}, bf16[160,512]{1,0:T(8,128)(2,1)}, u32[]{:S(2)}, u32[]{:S(2)}) collective-permute-start(bf16[160,512]{1,0:T(8,128)(2,1)} %get-tuple-element.90), channel_id=1, source_target_pairs={{0,8},{8,0},{16,24},{24,16},{1,9},{9,1},{17,25},{25,17},{2,10},{10... | collective-permute-start | bytes 491528 | tf_op jit(solution)/shard_map/ppermute | solution.py:414
  71.9 10.2 %collective-permute-start.18 = (bf16[160,512]{1,0:T(8,128)(2,1)}, bf16[160,512]{1,0:T(8,128)(2,1)}, u32[]{:S(2)}, u32[]{:S(2)}) collective-permute-start(bf16[160,512]{1,0:T(8,128)(2,1)} %get-tuple-element.91), channel_id=1, source_target_pairs={{0,16},{8,24},{16,0},{24,8},{1,17},{9,25},{17,1},{25,9},{2,18},{10... | collective-permute-start | bytes 491528 | tf_op jit(solution)/shard_map/ppermute | solution.py:414
  73.4 8.6 %collective-permute-start.19 = (bf16[160,512]{1,0:T(8,128)(2,1)}, bf16[160,512]{1,0:T(8,128)(2,1)}, u32[]{:S(2)}, u32[]{:S(2)}) collective-permute-start(bf16[160,512]{1,0:T(8,128)(2,1)} %get-tuple-element.92), channel_id=1, source_target_pairs={{0,24},{8,16},{16,8},{24,0},{1,25},{9,17},{17,9},{25,1},{2,26},{10... | collective-permute-start | bytes 491528 | tf_op jit(solution)/shard_map/ppermute | solution.py:414

commit v3 on v2

--- a/solution.py
+++ b/solution.py
@@ -14,19 +14,17 @@
 CHUNK = 8
 FF_TILE = 256
 VMEM_LIMIT = 64 * 1024 * 1024 - 65536
-EXPERT_LIMIT = 64 * 1024 * 1024 - 65536
-AHEAD = 4
-TIE_O = True
+AHEAD = 6
+SLOPE = jnp.bfloat16
+TURN = 1
+JOIN = True
+TIE_O = ()
+TIE_S = False
 TIE_L = True
-TIE_P = ()
+TIE_P = (4, 5, 6, 7)
+NEAR = (1, 2, 3)
 TIE_B = "hidden"
-GATHER_HIDDEN = False
-PREPARE_EARLY = True
 TIE_G = True
-WAY_C = "permute"
-WAY_P = "permute"
-WAY_O = "all"
-WAY_B = "all"
 F32 = jnp.float32
 BF16 = jnp.bfloat16
 
@@ -43,7 +41,7 @@
     return lax.broadcasted_iota(jnp.int32, shape, dim)
 
 
-def pair_rows_of(ids, codes, counts_ref, group):
+def places_of(ids, codes, counts_ref):
     count = jnp.zeros_like(ids)
     base = jnp.zeros_like(ids)
     for expert in range(counts_ref.shape[0]):
@@ -52,8 +50,7 @@
         if expert % 2:
             base = jnp.where(hit, counts_ref[expert - 1], base)
     laps = jnp.floor((codes.astype(F32) + 0.5) / count.astype(F32)).astype(jnp.int32)
-    bucket = codes - laps * count
-    return ((ids >> 1) ^ group) * BLOCK_ROWS + base + bucket
+    return ids >> 1, base + codes - laps * count
 
 
 def membership(rows, total, values):
@@ -94,12 +91,14 @@
 
 
 class Blocks:
-    def __init__(self, refs, group):
-        self.refs, self.group = refs, group
+    def __init__(self, refs, n, group):
+        self.refs, self.n, self.group = refs, n, group
 
     def at(self, j):
+        if len(self.refs) == self.n:
+            return self.refs[j]
         if len(self.refs) > 1:
-            return self.refs[j]
+            return self.refs[j // 2].at[(j % 2) ^ (self.group & 1)]
         return self.refs[0].at[self.group ^ j]
 
     def load(self, start, stop):
@@ -146,12 +145,27 @@
 
 def gather_kernel(mean, n, group_ref, counts_ref, ids_ref, codes_ref, weights_ref, x_ref, *outs):
     group = group_ref[0]
-    rows = pair_rows_of(ids_ref[...], codes_ref[...], counts_ref, group)
+    device, inside = places_of(ids_ref[...], codes_ref[...], counts_ref)
+    rows = (device ^ group) * BLOCK_ROWS + inside
     member = membership(rows, n * BLOCK_ROWS, None if mean else weights_ref[...])
     sums = mm(member.astype(BF16), split_halves(x_ref[...]))
     if mean:
         sums = sums / jnp.maximum(jnp.sum(member, axis=1, keepdims=True), 1.0)
-    Blocks(outs, group).store(0, sums)
+    Blocks(outs, n, group).store(0, sums)
+
+
+def gather_pair_kernel(mean, n, group_ref, counts_ref, *refs):
+    sources, outs = (refs[:4], refs[4:8]), refs[8:]
+    group = group_ref[0]
+    core = group & 1
+    for mate, (ids_ref, codes_ref, weights_ref, x_ref) in enumerate(sources):
+        rows = pair_rows(ids_ref, codes_ref, counts_ref, group)
+        member = membership(rows, len(outs) * BLOCK_ROWS, None if mean else weights_ref[...])
+        sums = mm(member.astype(BF16), split_halves(x_ref[...]))
+        if mean:
+            sums = sums / jnp.maximum(jnp.sum(member, axis=1, keepdims=True), 1.0)
+        for d, out in enumerate(outs):
+            out[core ^ mate] = sums[d * BLOCK_ROWS : (d + 1) * BLOCK_ROWS].astype(BF16)
 
 
 def own_scale(scale_ref, group, e):
@@ -170,29 +184,62 @@
     return mm(high, scale, TN) + mm(low, scale, TN)
 
 
-def prepare_kernel(n, counts_ref, group_ref, ids_ref, codes_ref, weights_ref, tok_ref, cot_ref, scale_ref, *outs):
-    base_l_ref, base_g_ref, mix_l_ref, mix_g_ref = outs
-    ids = ids_ref[...]
-    weights = weights_ref[...]
-    gain = gain_of(ids, weights, scale_ref[...])
-    base_l_ref[...] = gain * tok_ref[...].astype(F32)
-    base_g_ref[...] = gain * cot_ref[...].astype(F32)
-    rows = pair_rows_of(ids, codes_ref[...], counts_ref, group_ref[0])
+def pair_rows(ids_ref, codes_ref, counts_ref, group):
+    device, inside = places_of(ids_ref[...], codes_ref[...], counts_ref)
+    away = (device >> 1) ^ (group >> 1)
+    return jnp.where((device & 1) == (group & 1), away * BLOCK_ROWS + inside, -BLOCK_ROWS)
+
+
+def prepare_kernel(n, counts_ref, group_ref, ids_ref, codes_ref, weights_ref, *refs):
+    mate, (mix_g_ref, mix_own_ref, mix_mate_ref) = refs[:-3], refs[-3:]
+    device, inside = places_of(ids_ref[...], codes_ref[...], counts_ref)
+    rows = (device ^ group_ref[0]) * BLOCK_ROWS + inside
     member = membership(rows, n * BLOCK_ROWS, None)
     divisor = jnp.maximum(jnp.sum(member, axis=1, keepdims=True), 1.0)
     mix_g_ref[...] = (member / divisor).T.astype(BF16)
-    mix_l_ref[...] = membership(rows, n * BLOCK_ROWS, weights).T.astype(BF16)
-
-
-def spread_kernel(n, group_ref, base_ref, mix_ref, *refs):
+    for out, (i, c, w) in ((mix_own_ref, (ids_ref, codes_ref, weights_ref)), (mix_mate_ref, mate)):
+        rows = pair_rows(i, c, counts_ref, group_ref[0])
+        out[...] = membership(rows, n // 2 * BLOCK_ROWS, w[...]).T.astype(BF16)
+
+
+def part_kernel(group_ref, mix_ref, *refs):
     blocks, out_ref = refs[:-1], refs[-1]
-    flat = jnp.concatenate(Blocks(blocks, group_ref[0]).load(0, n), axis=0)
+    flat = jnp.concatenate([b[(group_ref[0] & 1) ^ 1] for b in blocks], axis=0)
     back = mm(mix_ref[...], flat)
     tokens, width = out_ref.shape
     half = width // HALVES
     for h in range(HALVES):
-        cols = slice(h * half, (h + 1) * half)
-        out_ref[:, cols] = (base_ref[:, cols] + back[h * tokens : (h + 1) * tokens]).astype(BF16)
+        out_ref[:, h * half : (h + 1) * half] = back[h * tokens : (h + 1) * tokens].astype(BF16)
+
+
+def spread_kernel(copies, n, pair, group_ref, ids_ref, weights_ref, scale_ref, x_ref, mix_ref, *refs):
+    out_hbm, out_ref, sem = refs[-3:]
+    given = refs[:-3]
+    waits = iter(sorted(copies))
+    take = lambda count: [copies[next(waits)].wait() for _ in range(count)]
+    group = group_ref[0]
+    take(3)
+    gain = gain_of(ids_ref[...], weights_ref[...], scale_ref[...])
+    take(1)
+    base = gain * x_ref[...].astype(F32)
+    take(1 + len(given))
+    if pair:
+        part_ref, blocks = given[0], given[1:]
+        base = base + part_ref[...].astype(F32)
+        flat = jnp.concatenate([b[group & 1] for b in blocks], axis=0)
+    else:
+        flat = jnp.concatenate(Blocks(given, n, group).load(0, n), axis=0)
+    tokens, width = out_ref.shape
+    half = width // HALVES
+    sends = []
+    for h in range(HALVES):
+        cols = pl.ds(h * half, half)
+        back = mm(mix_ref[h * tokens : (h + 1) * tokens, :], flat)
+        out_ref[:, h * half : (h + 1) * half] = (base[:, h * half : (h + 1) * half] + back).astype(BF16)
+        sends.append(pltpu.make_async_copy(out_ref.at[:, cols], out_hbm.at[:, cols], sem.at[h]))
+        sends[-1].start()
+    for send in sends:
+        send.wait()
 
 
 class Weights:
@@ -248,7 +295,7 @@
 
 def forward_kernel(n, n_in, n_out, counts_ref, group_ref, scale_ref, wg_hbm, wu_hbm, wd_hbm, *refs):
     group = group_ref[0]
-    blocks, outs = Blocks(refs[:n_in], group), Blocks(refs[n_in : n_in + n_out], group)
+    blocks, outs = Blocks(refs[:n_in], n, group), Blocks(refs[n_in : n_in + n_out], n, group)
     hidden_ref, slope_ref, silu_ref, x_ref, acc_ref, wg_ref, wu_ref, wd_ref, sems = refs[n_in + n_out :]
     weights = Weights((wg_hbm, wu_hbm, wd_hbm), (wg_ref, wu_ref, wd_ref), sems)
     for s in range(AHEAD):
@@ -271,8 +318,8 @@
         slope = up * sg * (1.0 + gate * (1.0 - sg))
         acc_ref[e] += mm(hidden, wd[...])
         hidden_ref[start:stop, cols] = jnp.where(mine, hidden, hidden_ref[start:stop, cols])
-        slope_ref[e, cols, :] = slope.T
-        silu_ref[e, cols, :] = silu.T
+        slope_ref[e, cols, :] = slope.T.astype(SLOPE)
+        silu_ref[e, cols, :] = silu.T.astype(SLOPE)
 
     weights.run(body)
     size = min(n, CHUNK)
@@ -281,46 +328,50 @@
         outs.store(c, pack_windows(parts, n, c, size, counts_ref, group, NN))
 
 
-def unpack_kernel(n, n_in, parts, dp_ref, group_ref, *refs):
-    blocks, pull_ref, shares = Blocks(refs[:n_in], group_ref[0]), refs[n_in], refs[n_in + 1 :]
+def backward_kernel(n, n_in, n_out, parts, counts_ref, group_ref, dp_ref, scale_ref, wg_hbm, wu_hbm, wd_hbm, slope_ref, silu_ref, *refs):
+    group = group_ref[0]
+    blocks, outs = Blocks(refs[:n_in], n, group), Blocks(refs[n_in : n_in + n_out], n, group)
+    refs = refs[n_in + n_out :]
+    shares, (pull_ref, turned_ref, acc_ref, wg_ref, wu_ref, wd_ref, sems) = refs[:parts], refs[parts:]
+    weights = Weights((wg_hbm, wu_hbm, wd_hbm), (wg_ref, wu_ref, wd_ref), sems)
+    for s in range(AHEAD):
+        weights.start(s)
     unpack_all(pull_ref, blocks, n)
+    for e, (start, stop) in enumerate(windows(n)):
+        if TURN == 1:
+            turned_ref[e] = pull_ref[start:stop, :].T
+            scale = jnp.broadcast_to(own_scale(scale_ref, group, e), (8, pull_ref.shape[1])).T[:, :1]
+            acc_ref[e] = -(scale * turned_ref[e].astype(F32))
+        else:
+            pull = pull_ref[start:stop, :].astype(F32)
+            turned_ref[e] = pull.T.astype(BF16)
+            acc_ref[e] = -(own_scale(scale_ref, group, e) * pull).T
     width = pull_ref.shape[1] // parts
     for k, share in enumerate(shares):
         start = pl.multiple_of((dp_ref[0] ^ k) * width, width)
         share[...] = pull_ref[:, pl.ds(start, width)]
 
-
-def backward_kernel(n, n_out, counts_ref, group_ref, scale_ref, wg_hbm, wu_hbm, wd_hbm, pull_ref, slope_ref, silu_ref, *refs):
-    group = group_ref[0]
-    outs = Blocks(refs[:n_out], group)
-    turned_ref, acc_ref, wg_ref, wu_ref, wd_ref, sems = refs[n_out:]
-    weights = Weights((wg_hbm, wu_hbm, wd_hbm), (wg_ref, wu_ref, wd_ref), sems)
-    for s in range(AHEAD):
-        weights.start(s)
-    for e, (start, stop) in enumerate(windows(n)):
-        pull = pull_ref[start:stop, :].astype(F32)
-        turned_ref[e] = pull.T.astype(BF16)
-        acc_ref[e] = -(own_scale(scale_ref, group, e) * pull).T
-
     def body(e, cols, wg, wu, wd):
         d_hidden = mm(wd[...], turned_ref[e])
-        d_gate = (d_hidden * slope_ref[e, cols, :]).astype(BF16)
-        d_up = (d_hidden * silu_ref[e, cols, :]).astype(BF16)
-        acc_ref[e] += mm(wg[...], d_gate) + mm(wu[...], d_up)
+        d_gate = (d_hidden * slope_ref[e, cols, :].astype(F32)).astype(BF16)
+        d_up = (d_hidden * silu_ref[e, cols, :].astype(F32)).astype(BF16)
+        if JOIN:
+            both = jnp.concatenate([wg[...], wu[...]], axis=1)
+            acc_ref[e] += mm(both, jnp.concatenate([d_gate, d_up], axis=0))
+        else:
+            acc_ref[e] += mm(wg[...], d_gate) + mm(wu[...], d_up)
 
     weights.run(body)
     size = min(n, CHUNK)
-    parts = [acc_ref[e].astype(BF16) for e in range(2)]
+    sums = [acc_ref[e].astype(BF16) for e in range(2)]
     for c in range(0, n, size):
-        outs.store(c, pack_windows(parts, n, c, size, counts_ref, group, NT))
-
-
-def grad_kernel(n, parts, counts_ref, group_ref, dp_ref, *refs):
-    if GATHER_HIDDEN:
-        hidden = [refs[0].at[dp_ref[0] ^ k] for k in range(parts)]
-    else:
-        hidden = refs[:parts]
-    shares, out_ref = refs[-1 - parts : -1], refs[-1]
+        outs.store(c, pack_windows(sums, n, c, size, counts_ref, group, NT))
+
+
+def grad_kernel(n, parts, counts_ref, group_ref, *refs):
+    hidden, shares = refs[:parts], refs[parts : 2 * parts]
+    out_hbm, out_ref, sem = refs[2 * parts :]
+    sends = []
     for e in range(2):
         start, stop = windows(n)[e]
         mine = owned(e, start, stop, n, counts_ref, group_ref[0])
@@ -329,6 +380,10 @@
             [jnp.where(mine, s[start:stop, :].astype(F32), 0.0).astype(BF16) for s in shares], axis=0
         )
         out_ref[e] = mm(h_all, pull, TN).astype(BF16)
+        sends.append(pltpu.make_async_copy(out_ref.at[e], out_hbm.at[e], sem.at[e]))
+        sends[-1].start()
+    for send in sends:
+        send.wait()
 
 
 SMEM = pl.BlockSpec(memory_space=pltpu.SMEM)
@@ -336,7 +391,7 @@
 HBM = pl.BlockSpec(memory_space=pltpu.HBM)
 
 
-def call(kernel, ins, outs, flops, nbytes, scratch=(), limit=VMEM_LIMIT):
+def call(kernel, ins, outs, flops, nbytes, scratch=(), lazy=False, out_spec=VMEM):
     arrays, specs, buffers = [], [], []
     for x, way in ins:
         if way in ("copy", "scalars", "stay"):
@@ -346,34 +401,33 @@
         if way == "scalars":
             buffers.append(pltpu.SMEM(x.shape, x.dtype))
         arrays.append(x)
-        specs.append({"smem": SMEM, "vmem": VMEM}.get(way, HBM))
-    ways = [way for _, way in ins]
-    copied = [i for i, way in enumerate(ways) if way in ("copy", "scalars")]
-    if copied:
-        buffers.append(pltpu.SemaphoreType.DMA((len(copied),)))
+        specs.append(SMEM if way == "smem" else HBM)
+    copied = [i for i, (_, way) in enumerate(ins) if way in ("copy", "scalars")]
+    buffers.append(pltpu.SemaphoreType.DMA((max(len(copied), 1),)))
 
     def body(*refs):
         refs = list(refs)
-        if copied:
-            given = refs[len(refs) - len(buffers) : -1]
-            sems = refs[-1]
-            refs = refs[: len(refs) - len(buffers)]
-            copies = [pltpu.make_async_copy(refs[i], given[k], sems.at[k]) for k, i in enumerate(copied)]
-            for copy in copies:
-                copy.start()
-            for copy in copies:
+        given, sems = refs[len(refs) - len(buffers) : -1], refs[-1]
+        refs = refs[: len(refs) - len(buffers)]
+        copies = {i: pltpu.make_async_copy(refs[i], given[k], sems.at[k]) for k, i in enumerate(copied)}
+        for copy in copies.values():
+            copy.start()
+        for k, i in enumerate(copied):
+            refs[i] = given[k]
+        if lazy:
+            kernel(copies, *refs)
+        else:
+            for copy in copies.values():
                 copy.wait()
-            for k, i in enumerate(copied):
-                refs[i] = given[k]
-        kernel(*refs)
+            kernel(*refs)
 
     return pl.pallas_call(
         body,
         out_shape=outs,
         in_specs=specs,
-        out_specs=jax.tree.map(lambda _: VMEM, outs),
+        out_specs=jax.tree.map(lambda _: out_spec, outs),
         scratch_shapes=list(scratch) + buffers,
-        compiler_params=pltpu.CompilerParams(vmem_limit_bytes=limit),
+        compiler_params=pltpu.CompilerParams(vmem_limit_bytes=VMEM_LIMIT),
         cost_estimate=pl.CostEstimate(flops=flops, bytes_accessed=nbytes, transcendentals=0),
     )(*arrays)
 
@@ -396,18 +450,26 @@
     block_bytes = total * width
     picks = ids.shape[0]
 
+    block = (BLOCK_ROWS, half)
+
     def layout(way):
         if way == "permute":
-            return [jax.ShapeDtypeStruct((BLOCK_ROWS, half), BF16)] * n
-        return [jax.ShapeDtypeStruct((n, BLOCK_ROWS, half), BF16)]
+            return [jax.ShapeDtypeStruct(block, BF16)] * n
+        if way == "pair":
+            return [jax.ShapeDtypeStruct((2, *block), BF16)] * (n // 2)
+        return [jax.ShapeDtypeStruct((n, *block), BF16)]
 
     def exchange(way, values):
-        if way == "permute":
-            return [values[0]] + [
-                lax.ppermute(values[k], "expert", [(i, i ^ k) for i in range(n)])
-                for k in sorted(range(1, n))
-            ]
-        return [lax.all_to_all(values[0], "expert", split_axis=0, concat_axis=0, tiled=True)]
+        if way == "all":
+            return [lax.all_to_all(values[0], "expert", split_axis=0, concat_axis=0, tiled=True)]
+        step = n // len(values)
+        return [values[0]] + [
+            lax.ppermute(values[d], "expert", [(i, i ^ (step * d)) for i in range(n)])
+            for d in range(1, len(values))
+        ]
+
+    def from_mate(x):
+        return lax.ppermute(x, "expert", [(i, i ^ 1) for i in range(n)])
 
     def exchange_dp(values):
         return [values[0]] + [
@@ -419,45 +481,34 @@
     copy = lambda *xs: [(x, "copy") for x in xs]
     vmem = lambda xs: [(x, "vmem") for x in xs]
 
+    mate = [from_mate(v).T for v in (expert_ids, bucket_codes, route_weights)]
+
     def gather(mean, way, x):
+        kernel, given = gather_kernel, [ids, codes, weights, x]
+        if way == "pair":
+            kernel, given = gather_pair_kernel, given + mate + [from_mate(x)]
         return call(
-            functools.partial(gather_kernel, mean, n),
-            [place, scalars] + copy(ids, codes, weights, x),
+            functools.partial(kernel, mean, n),
+            [place, scalars] + copy(*given),
             layout(way),
             2 * total * tok_count * width,
             block_bytes,
         )
 
-    base = jax.ShapeDtypeStruct((tok_count, width), F32)
-    mix = jax.ShapeDtypeStruct((HALVES * tok_count, total), BF16)
-    sent_c = gather(True, WAY_C, tokens)
-    got_c = exchange(WAY_C, sent_c)
-    sent_p = gather(False, WAY_P, tie(cotangent, sent_c[0]))
+    sent_c = list(gather(True, "permute", tokens))
+    sent_p = list(gather(False, "pair", tie(cotangent, sent_c[0])))
+    if NEAR:
+        near = [sent_c[k] for k in NEAR]
+        for k, v in zip(NEAR, tie(near, sent_p)):
+            sent_c[k] = v
+    got_c = exchange("permute", sent_c)
     if TIE_P:
-        sent_p = [tie(sent_p[0], [got_c[k] for k in TIE_P])] + list(sent_p[1:])
-    got_p = exchange(WAY_P, sent_p)
-    base_l, base_g, mix_l, mix_g = call(
-        functools.partial(prepare_kernel, n),
-        [scalars, place] + copy(ids, codes, weights, tie(tokens, sent_p[0]), cotangent, comp_scale),
-        [base, base, mix, mix],
-        4 * tok_count * expert_total * width,
-        5 * tok_count * width * 4,
-    )
-
-    def spread(base, mix, got):
-        return call(
-            functools.partial(spread_kernel, n),
-            [place] + copy(base, mix, *got),
-            jax.ShapeDtypeStruct(tokens.shape, BF16),
-            2 * total * tok_count * width,
-            block_bytes,
-        )
-
-    if PREPARE_EARLY:
-        got_c, base_l, base_g, mix_l, mix_g = lax.optimization_barrier((got_c, base_l, base_g, mix_l, mix_g))
+        sent_p = tie(sent_p, [got_c[k] for k in TIE_P])
+    got_p = exchange("pair", sent_p)
+
     weight_bytes = 3 * local * width * ff * 2
     expert_flops = 2 * 3 * rows * local * width * ff
-    out_o, out_b = layout(WAY_O), layout(WAY_B)
+    out_o, out_b = layout("pair"), layout("all")
     stream = [
         pltpu.VMEM(w_gate.shape, BF16),
         pltpu.VMEM(w_up.shape, BF16),
@@ -472,62 +523,89 @@
         out_o
         + [
             jax.ShapeDtypeStruct((rows, ff), BF16),
-            jax.ShapeDtypeStruct((local, ff, most), F32),
-            jax.ShapeDtypeStruct((local, ff, most), F32),
+            jax.ShapeDtypeStruct((local, ff, most), SLOPE),
+            jax.ShapeDtypeStruct((local, ff, most), SLOPE),
         ],
         expert_flops,
         weight_bytes,
         [pltpu.VMEM((rows, width), BF16), pltpu.VMEM((local, most, width), F32)] + stream,
-        EXPERT_LIMIT,
+    )
+    mix = jax.ShapeDtypeStruct((HALVES * tok_count, total), BF16)
+    mix_pair = jax.ShapeDtypeStruct((HALVES * tok_count, total // 2), BF16)
+    mix_g, mix_own, mix_mate = call(
+        functools.partial(prepare_kernel, n),
+        [scalars, place] + copy(tie(ids, results[0]), codes, weights, *mate),
+        [mix, mix_pair, mix_pair],
+        0,
+        3 * tok_count * total * 4,
     )
     sent_o, (hidden, slope, silu) = results[: len(out_o)], results[len(out_o) :]
     if TIE_O:
-        sent_o = tie(list(sent_o), got_p)
-    got_o = exchange(WAY_O, sent_o)
-    if GATHER_HIDDEN:
-        all_hidden = [lax.all_gather(hidden, "dp")]
-    else:
-        all_hidden = exchange_dp([hidden] * parts)
-
-    pull_and_shares = call(
-        functools.partial(unpack_kernel, n, len(got_p), parts),
-        [(dp, "smem"), place] + copy(*got_p),
-        [jax.ShapeDtypeStruct((rows, width), BF16)]
-        + [jax.ShapeDtypeStruct((rows, width // parts), BF16)] * parts,
-        2 * rows * min(n, CHUNK) * BLOCK_ROWS * width,
-        2 * block_bytes,
-    )
-    pull = pull_and_shares[0]
-    all_shares = exchange_dp(pull_and_shares[1:])
-
-    sent_b = call(
-        functools.partial(backward_kernel, n, len(out_b)),
-        fixed + copy(pull, slope, silu),
-        out_b,
+        sent_o = tie(list(sent_o), [got_p[d] for d in TIE_O])
+    got_o = exchange("pair", sent_o)
+    all_hidden = exchange_dp([hidden] * parts)
+
+    share = jax.ShapeDtypeStruct((rows, width // parts), BF16)
+    results = call(
+        functools.partial(backward_kernel, n, len(got_p), len(out_b), parts),
+        fixed[:2] + [(dp, "smem")] + fixed[2:] + copy(slope, silu, *got_p),
+        out_b + [share] * parts,
         expert_flops,
         weight_bytes,
-        [pltpu.VMEM((local, width, most), BF16), pltpu.VMEM((local, width, most), F32)] + stream,
-        EXPERT_LIMIT,
+        [
+            pltpu.VMEM((rows, width), BF16),
+            pltpu.VMEM((local, width, most), BF16),
+            pltpu.VMEM((local, width, most), F32),
+        ]
+        + stream,
     )
+    sent_b, shares = results[: len(out_b)], results[len(out_b) :]
+    all_shares = exchange_dp(shares)
     if TIE_B == "hidden":
-        sent_b = tie(sent_b, all_hidden)
+        sent_b = tie(list(sent_b), (all_hidden, got_o))
     if TIE_B == "both":
         sent_b = tie(sent_b, (all_hidden, all_shares))
-    got_b = exchange(WAY_B, sent_b)
-
-    layer_output = spread(base_l, mix_l, got_o)
+    got_b = exchange("all", sent_b)
+
+    part = call(
+        part_kernel,
+        [place] + copy(mix_mate, *got_o),
+        jax.ShapeDtypeStruct(tokens.shape, BF16),
+        total * tok_count * width,
+        block_bytes,
+    )
+
+    def spread(pair, x, mix, given):
+        out = jax.ShapeDtypeStruct(tokens.shape, BF16)
+        return call(
+            lambda copies, *refs: spread_kernel(copies, n, pair, *refs),
+            [place] + copy(ids, weights, comp_scale, x, mix, *given),
+            out,
+            2 * total * tok_count * width,
+            block_bytes,
+            [pltpu.VMEM(out.shape, BF16), pltpu.SemaphoreType.DMA((HALVES,))],
+            lazy=True,
+            out_spec=HBM,
+        )
+
+    if TIE_S:
+        mix_own = tie(mix_own, all_shares)
+    layer_output = spread(True, tokens, mix_own, [from_mate(part), *got_o])
     if TIE_L:
         all_shares = tie(all_shares, layer_output)
+    grad_shape = jax.ShapeDtypeStruct((local, ff, width // parts), BF16)
     grad_down = call(
         functools.partial(grad_kernel, n, parts),
-        [scalars, place, (dp, "smem")] + copy(*all_hidden, *all_shares),
-        jax.ShapeDtypeStruct((local, ff, width // parts), BF16),
+        [scalars, place] + copy(*all_hidden, *all_shares),
+        grad_shape,
         2 * parts * rows * ff * local * width // parts,
         parts * rows * (ff + width // parts) * 2,
+        [pltpu.VMEM(grad_shape.shape, BF16), pltpu.SemaphoreType.DMA((local,))],
+        out_spec=HBM,
     )
     if TIE_G:
-        base_g = tie(base_g, (layer_output, grad_down))
-    grad_tokens = spread(base_g, mix_g, got_b)
+        mix_g = tie(mix_g, (layer_output, grad_down))
+    grad_tokens = spread(False, cotangent, mix_g, got_b)
     return (layer_output, grad_tokens, grad_down)
 
 

time: 92 us -> 84.1 us (0.914)
  starting transfers between devices: 39.3 us -> 32.4 us
  Pallas kernels: 42.9 us -> 40.9 us
  waiting for transfers between devices: 8.38 us -> 9.47 us
    all_to_all x2 -> x1, starting transfers between devices: 9.93 us -> 4.4 us  [exchange(): lax.all_to_all(values[0], 'expert', split_axis=0, concat_axis=0, tiled=True)]
    ppermute x14 -> x18, waiting for transfers between devices: 0.04 us -> 4.13 us  [the longest x13 3.12 us: exchange(): lax.ppermute(values[d], 'expert', [(i, i ^ step * d) for i in range(n)])]
    all_to_all x2 -> x1, waiting for transfers between devices: 2.89 us -> 0.01 us  [exchange(): lax.all_to_all(values[0], 'expert', split_axis=0, concat_axis=0, tiled=True)]
    pallas_call x9, Pallas kernels: 42.9 us -> 40.9 us  [call(): pl.pallas_call(body, out_shape=outs, in_specs=specs, out_specs=jax.tree.m...]
    ppermute x14 -> x18, starting transfers between devices: 22.4 us -> 20.7 us  [the longest x13 19.3 us: exchange(): lax.ppermute(values[d], 'expert', [(i, i ^ step * d) for i in range(n)])]
  transfers between devices with their start and end apart: 22 -> 25, of which waited for: 3 -> 5; matrix products, arithmetic and copies ran while one was open for 0% -> 0% of each run, Pallas kernels for 41% -> 43%
where the time goes in v3:
time: 84.1 us; the launch traced here: 83.7 us
  Pallas kernels  40.9 us (49%)
  starting transfers between devices  32.4 us (39%)
  waiting for transfers between devices  9.47 us (11%)
  between operations  0.95 us (1%)
    pallas_call x9, Pallas kernels, call(): pl.pallas_call(body, out_shape=outs, in_specs=specs, out_specs=jax.tree.m...  40.9 us
    ppermute x13, starting transfers between devices, exchange(): lax.ppermute(values[d], 'expert', [(i, i ^ step * d) for i in range(n)])  19.3 us
    ppermute x6, starting transfers between devices, exchange_dp(): lax.ppermute(values[k], 'dp', [(i, i ^ k) for i in range(parts)])  7.27 us
    ppermute x6, waiting for transfers between devices, exchange_dp(): lax.ppermute(values[k], 'dp', [(i, i ^ k) for i in range(parts)])  5.34 us
    all_to_all x1, starting transfers between devices, exchange(): lax.all_to_all(values[0], 'expert', split_axis=0, concat_axis=0, tiled=True)  4.4 us
    ppermute x13, waiting for transfers between devices, exchange(): lax.ppermute(values[d], 'expert', [(i, i ^ step * d) for i in range(n)])  3.12 us
  transfers between devices with their start and end apart: 25, of which 5 were waited for; matrix products, arithmetic and copies ran while one was open for 0% of the time, Pallas kernels for 43%

profile of v3, /device:TPU:0, one launch (start us, length us, event | category | flops | bytes accessed | tf_op | source)
XLA Modules:
  0.0 83.7 jit_solution(533387648862663349)
XLA Ops:
  0.6 2.3 %shard_map.121 = (bf16[40,1024]{1,0:T(8,128)(2,1)}, bf16[40,1024]{1,0:T(8,128)(2,1)}, bf16[40,1024]{1,0:T(8,128)(2,1)}, bf16[40,1024]{1,0:T(8,128)(2,1)}, bf16[4...) custom-call(s32[1]{0:T(128)} %bitcast.refs_0_.refs_1_, ...), custom_call_target="tpu_custom_call" | custom-call | flops 167772160 | bytes 655360 | tf_op jit(solution)/shard_map/pallas_call | solution.py:424
  3.0 0.5 collective-permute-start.3
  3.5 4.7 %collective-permute-start.10 = (bf16[40,1024]{1,0:T(8,128)(2,1)}, bf16[40,1024]{1,0:T(8,128)(2,1)}, u32[]{:S(2)}, u32[]{:S(2)}) collective-permute-start(bf16[40,1024]{1,0:T(8,128)(2,1)} %get-tuple-element.60), channel_id=1, source_target_pairs={{0,7},{1,6},{2,5},{3,4},{4,3},{5,2},{6,1},{7,0},{8,15},{9,14},{10,... | collective-permute-start | bytes 245768 | tf_op jit(solution)/shard_map/ppermute | solution.py:467
  8.3 0.4 collective-permute-start.1
  8.8 1.0 %collective-permute-done = s32[128,8]{0,1:T(8,128)} collective-permute-done((s32[128,8]{0,1:T(8,128)}, s32[128,8]{0,1:T(8,128)}, u32[]{:S(2)}, u32[]{:S(2)}) %collective-permute-start) | collective-permute-done | bytes 4128 | tf_op jit(solution)/shard_map/ppermute | solution.py:472
  9.9 2.9 %collective-permute-start.8 = (bf16[40,1024]{1,0:T(8,128)(2,1)}, bf16[40,1024]{1,0:T(8,128)(2,1)}, u32[]{:S(2)}, u32[]{:S(2)}) collective-permute-start(bf16[40,1024]{1,0:T(8,128)(2,1)} %get-tuple-element.58), channel_id=1, source_target_pairs={{0,5},{1,4},{2,7},{3,6},{4,1},{5,0},{6,3},{7,2},{8,13},{9,12},{10,... | collective-permute-start | bytes 245768 | tf_op jit(solution)/shard_map/ppermute | solution.py:467
  13.2 2.7 %shard_map.122 = (bf16[2,40,1024]{2,1,0:T(8,128)(2,1)}, bf16[2,40,1024]{2,1,0:T(8,128)(2,1)}, bf16[2,40,1024]{2,1,0:T(8,128)(2,1)}, bf16[2,40,1024]{2,1,0:T(8,128)(2,1)}) custom-call(s32[1]{0:T(128)} %bitcast.refs_0_.refs_1_, s32[16]{0:T(128)} %refs_0_.7, s32[8,128]{1,0:T(8,128)} %bitcast.9, s32[8,128]{1,0:T(8,128)} %bitcast.19, f32[8,128]{1,0:T(8,128)} %bitcast.14, ...), custom_call_target="tpu_custom_call" | custom-call | flops 167772160 | bytes 655360 | tf_op jit(solution)/shard_map/pallas_call | solution.py:424
  16.0 1.6 %collective-permute-start.5 = (bf16[40,1024]{1,0:T(8,128)(2,1)}, bf16[40,1024]{1,0:T(8,128)(2,1)}, u32[]{:S(2)}, u32[]{:S(2)}) collective-permute-start(bf16[40,1024]{1,0:T(8,128)(2,1)} %get-tuple-element.55), channel_id=1, source_target_pairs={{0,2},{1,3},{2,0},{3,1},{4,6},{5,7},{6,4},{7,5},{8,10},{9,11},{10,... | collective-permute-start | bytes 245768 | tf_op jit(solution)/shard_map/ppermute | solution.py:467
  17.6 2.4 %collective-permute-done.7.refs_10_ = bf16[40,1024]{1,0:T(8,128)(2,1)} collective-permute-done((bf16[40,1024]{1,0:T(8,128)(2,1)}, bf16[40,1024]{1,0:T(8,128)(2,1)}, u32[]{:S(2)}, u32[]{:S(2)}) %collective-permute-start.7) | collective-permute-done | bytes 81952 | tf_op jit(solution)/shard_map/ppermute | solution.py:467
  20.1 0.6 collective-permute-done.8.refs_11_
  20.7 2.8 %collective-permute-start.18 = (bf16[2,40,1024]{2,1,0:T(8,128)(2,1)}, bf16[2,40,1024]{2,1,0:T(8,128)(2,1)}, u32[]{:S(2)}, u32[]{:S(2)}) collective-permute-start(bf16[2,40,1024]{2,1,0:T(8,128)(2,1)} %get-tuple-element.73), channel_id=1, source_target_pairs={{0,2},{1,3},{2,0},{3,1},{4,6},{5,7},{6,4},{7,5},{8,10},{9,11},{10,... | collective-permute-start | bytes 491528 | tf_op jit(solution)/shard_map/ppermute | solution.py:467
  23.5 1.0 %collective-permute-start.19 = (bf16[2,40,1024]{2,1,0:T(8,128)(2,1)}, bf16[2,40,1024]{2,1,0:T(8,128)(2,1)}, u32[]{:S(2)}, u32[]{:S(2)}) collective-permute-start(bf16[2,40,1024]{2,1,0:T(8,128)(2,1)} %get-tuple-element.74), channel_id=1, source_target_pairs={{0,4},{1,5},{2,6},{3,7},{4,0},{5,1},{6,2},{7,3},{8,12},{9,13},{10,... | collective-permute-start | bytes 491528 | tf_op jit(solution)/shard_map/ppermute | solution.py:467
  24.5 1.5 %collective-permute-start.20 = (bf16[2,40,1024]{2,1,0:T(8,128)(2,1)}, bf16[2,40,1024]{2,1,0:T(8,128)(2,1)}, u32[]{:S(2)}, u32[]{:S(2)}) collective-permute-start(bf16[2,40,1024]{2,1,0:T(8,128)(2,1)} %get-tuple-element.75), channel_id=1, source_target_pairs={{0,6},{1,7},{2,4},{3,5},{4,2},{5,3},{6,0},{7,1},{8,14},{9,15},{10,... | collective-permute-start | bytes 491528 | tf_op jit(solution)/shard_map/ppermute | solution.py:467
  26.0 10.5 %shard_map.123 = (bf16[2,40,1024]{2,1,0:T(8,128)(2,1)}, bf16[2,40,1024]{2,1,0:T(8,128)(2,1)}, bf16[2,40,1024]{2,1,0:T(8,128)(2,1)}, bf16[2,40,1024]{2,1,0:T(8,12...) custom-call(s32[16]{0:T(128)} %refs_0_.7, s32[1]{0:T(128)} %bitcast.refs_0_.refs_1_, ...), custom_call_target="tpu_custom_call" | custom-call | flops 3019898880 | bytes 18874368 | tf_op jit(solution)/shard_map/pallas_call | solution.py:424
  36.5 1.1 %collective-permute-start.11 = (bf16[2,40,1024]{2,1,0:T(8,128)(2,1)}, bf16[2,40,1024]{2,1,0:T(8,128)(2,1)}, u32[]{:S(2)}, u32[]{:S(2)}) collective-permute-start(bf16[2,40,1024]{2,1,0:T(8,128)(2,1)} %get-tuple-element.65), channel_id=1, source_target_pairs={{0,2},{1,3},{2,0},{3,1},{4,6},{5,7},{6,4},{7,5},{8,10},{9,11},{10,... | collective-permute-start | bytes 491528 | tf_op jit(solution)/shard_map/ppermute | solution.py:467
  37.6 1.5 %collective-permute-start.15 = (bf16[160,768]{1,0:T(8,128)(2,1)}, bf16[160,768]{1,0:T(8,128)(2,1)}, u32[]{:S(2)}, u32[]{:S(2)}) collective-permute-start(bf16[160,768]{1,0:T(8,128)(2,1)} %get-tuple-element.69.refs_2_), channel_id=1, source_target_pairs={{0,8},{8,0},{16,24},{24,16},{1,9},{9,1},{17,25},{25,17},{2,10},{10... | collective-permute-start | bytes 737288 | tf_op jit(solution)/shard_map/ppermute | solution.py:476
  39.0 1.5 %collective-permute-start.16 = (bf16[160,768]{1,0:T(8,128)(2,1)}, bf16[160,768]{1,0:T(8,128)(2,1)}, u32[]{:S(2)}, u32[]{:S(2)}) collective-permute-start(bf16[160,768]{1,0:T(8,128)(2,1)} %get-tuple-element.69.refs_2_), channel_id=1, source_target_pairs={{0,16},{8,24},{16,0},{24,8},{1,17},{9,25},{17,1},{25,9},{2,18},{10... | collective-permute-start | bytes 737288 | tf_op jit(solution)/shard_map/ppermute | solution.py:476
  40.6 0.8 collective-permute-start.17
  41.4 1.6 %collective-permute-start.12 = (bf16[2,40,1024]{2,1,0:T(8,128)(2,1)}, bf16[2,40,1024]{2,1,0:T(8,128)(2,1)}, u32[]{:S(2)}, u32[]{:S(2)}) collective-permute-start(bf16[2,40,1024]{2,1,0:T(8,128)(2,1)} %get-tuple-element.66), channel_id=1, source_target_pairs={{0,4},{1,5},{2,6},{3,7},{4,0},{5,1},{6,2},{7,3},{8,12},{9,13},{10,... | collective-permute-start | bytes 491528 | tf_op jit(solution)/shard_map/ppermute | solution.py:467
  43.0 1.6 %collective-permute-start.13 = (bf16[2,40,1024]{2,1,0:T(8,128)(2,1)}, bf16[2,40,1024]{2,1,0:T(8,128)(2,1)}, u32[]{:S(2)}, u32[]{:S(2)}) collective-permute-start(bf16[2,40,1024]{2,1,0:T(8,128)(2,1)} %get-tuple-element.67), channel_id=1, source_target_pairs={{0,6},{1,7},{2,4},{3,5},{4,2},{5,3},{6,0},{7,1},{8,14},{9,15},{10,... | collective-permute-start | bytes 491528 | tf_op jit(solution)/shard_map/ppermute | solution.py:467
  44.6 12.0 %shard_map.127 = (bf16[8,40,1024]{2,1,0:T(8,128)(2,1)}, bf16[160,512]{1,0:T(8,128)(2,1)}, bf16[160,512]{1,0:T(8,128)(2,1)}, bf16[160,512]{1,0:T(8,128)(2,1)}, bf16[160,512]{1,0:T(8,128)(2,1)}) custom-call(s32[16]{0:T(128)} %refs_0_.7, s32[1]{0:T(128)} %bitcast.refs_0_.refs_1_, s32[1]{0:T(128)} %bitcast.7.refs_2_, bf16[16,2048]{1,0:T(8,128)(2,1)} %refs_3_.7, ...), custom_call_target="tpu_custom_call" | custom-call | flops 3019898880 | bytes 18874368 | tf_op jit(solution)/shard_map/pallas_call | solution.py:424
  56.6 4.4 %all-to-all-start = ((bf16[8,40,1024]{2,1,0:T(8,128)(2,1)}), bf16[8,40,1024]{2,1,0:T(8,128)(2,1)}, u32[]{:S(2)}, u32[]{:S(2)}) async-start(bf16[8,40,1024]{2,1,0:T(8,128)(2,1)} %get-tuple-element.86), calls=%async_computation | async-start | bytes 1310720 | tf_op jit(solution)/shard_map/all_to_all | solution.py:464
  61.1 2.2 %shard_map.124 = (bf16[256,320]{1,0:T(8,128)(2,1)}, bf16[256,160]{1,0:T(8,128)(2,1)}, bf16[256,160]{1,0:T(8,128)(2,1)}) custom-call(s32[16]{0:T(128)} %refs_0_.7, s32[1]{0:T(128)} %bitcast.refs_0_.refs_1_, s32[8,128]{1,0:T(8,128)} %bitcast.10, s32[8,128]{1,0:T(8,128)} %bitcast.20, f32[8,128]{1,0:T(8,128)} %bitcast.15, s32[8,128]{1,0:T(8,128)} %bitcast.4.refs_6_.refs_5_, ...), custom_call_target="tpu_custom_call" | custom-call | bytes 491520 | tf_op jit(solution)/shard_map/pallas_call | solution.py:424
  63.2 2.4 %shard_map.125 = bf16[128,2048]{1,0:T(8,128)(2,1)} custom-call(s32[1]{0:T(128)} %bitcast.refs_0_.refs_1_, bf16[256,160]{1,0:T(8,128)(2,1)} %get-tuple-element.64.refs_1_, bf16[2,40,1024]{2,1,0:T(8,128)(2,1)} %get-tuple-element.61.refs_2_.refs_7_, bf16[2,40,1024]{2,1,0:T(8,128)(2,1)} %collective-permute-done.11.refs_3_.refs_8_, ...), custom_call_target="tpu_custom_call" | custom-call | flops 83886080 | bytes 655360 | tf_op jit(solution)/shard_map/pallas_call | solution.py:424
  65.8 1.5 %collective-permute-start.21 = (bf16[160,512]{1,0:T(8,128)(2,1)}, bf16[160,512]{1,0:T(8,128)(2,1)}, u32[]{:S(2)}, u32[]{:S(2)}) collective-permute-start(bf16[160,512]{1,0:T(8,128)(2,1)} %get-tuple-element.77), channel_id=1, source_target_pairs={{0,8},{8,0},{16,24},{24,16},{1,9},{9,1},{17,25},{25,17},{2,10},{10... | collective-permute-start | bytes 491528 | tf_op jit(solution)/shard_map/ppermute | solution.py:476
  67.3 1.5 %collective-permute-start.22 = (bf16[160,512]{1,0:T(8,128)(2,1)}, bf16[160,512]{1,0:T(8,128)(2,1)}, u32[]{:S(2)}, u32[]{:S(2)}) collective-permute-start(bf16[160,512]{1,0:T(8,128)(2,1)} %get-tuple-element.78), channel_id=1, source_target_pairs={{0,16},{8,24},{16,0},{24,8},{1,17},{9,25},{17,1},{25,9},{2,18},{10... | collective-permute-start | bytes 491528 | tf_op jit(solution)/shard_map/ppermute | solution.py:476
  68.8 0.5 collective-permute-start.23
  69.3 2.6 %shard_map.126 = bf16[128,2048]{1,0:T(8,128)(2,1)} custom-call(s32[1]{0:T(128)} %bitcast.refs_0_.refs_1_, s32[8,128]{1,0:T(8,128)} %bitcast.11, f32[8,128]{1,0:T(8,128)} %bitcast.16, bf16[16,2048]{1,0:T(8,128)(2,1)} %refs_3_.7, bf16[128,2048]{1,0:T(8,128)(2,1)} %refs_4_.5, bf16[256,160]{1,0:T(8,128)(2,1)} %get-tuple-element.63.refs_5_, ...), custom_call_target="tpu_custom_call" | custom-call | flops 167772160 | bytes 655360 | tf_op jit(solution)/shard_map/pallas_call | solution.py:424
  72.0 1.2 %collective-permute-done.21.refs_7_ = bf16[160,512]{1,0:T(8,128)(2,1)} collective-permute-done((bf16[160,512]{1,0:T(8,128)(2,1)}, bf16[160,512]{1,0:T(8,128)(2,1)}, u32[]{:S(2)}, u32[]{:S(2)}) %collective-permute-start.21) | collective-permute-done | bytes 163872 | tf_op jit(solution)/shard_map/ppermute | solution.py:476
  73.2 4.1 %collective-permute-done.22.refs_8_ = bf16[160,512]{1,0:T(8,128)(2,1)} collective-permute-done((bf16[160,512]{1,0:T(8,128)(2,1)}, bf16[160,512]{1,0:T(8,128)(2,1)}, u32[]{:S(2)}, u32[]{:S(2)}) %collective-permute-start.22) | collective-permute-done | bytes 163872 | tf_op jit(solution)/shard_map/ppermute | solution.py:476
  77.3 3.5 %shard_map.128 = bf16[2,768,512]{2,1,0:T(8,128)(2,1)} custom-call(s32[16]{0:T(128)} %refs_0_.7, s32[1]{0:T(128)} %bitcast.refs_0_.refs_1_, bf16[160,768]{1,0:T(8,128)(2,1)} %get-tuple-element.69.refs_2_, bf16[160,768]{1,0:T(8,128)(2,1)} %collective-permute-done.15.refs_3_, bf16[160,768]{1,0:T(8,128)(2,1)} %collective-permute-done.16.refs_4_, ...), custom_call_target="tpu_custom_call" | custom-call | flops 1006632960 | bytes 1638400 | tf_op jit(solution)/shard_map/pallas_call | solution.py:424
  80.8 2.7 %shard_map.129 = bf16[128,2048]{1,0:T(8,128)(2,1)} custom-call(s32[1]{0:T(128)} %bitcast.refs_0_.refs_1_, s32[8,128]{1,0:T(8,128)} %bitcast.12, f32[8,128]{1,0:T(8,128)} %bitcast.17, bf16[16,2048]{1,0:T(8,128)(2,1)} %refs_3_.7, bf16[128,2048]{1,0:T(8,128)(2,1)} %refs_4_.7, bf16[256,320]{1,0:T(8,128)(2,1)} %get-tuple-element.84.refs_5_, ...), custom_call_target="tpu_custom_call" | custom-call | flops 167772160 | bytes 655360 | tf_op jit(solution)/shard_map/pallas_call | solution.py:424
  (27 shorter events, 1.0 us)
Async XLA Ops:
  3.0 10.2 %collective-permute-start.3 = (bf16[128,2048]{1,0:T(8,128)(2,1)}, bf16[128,2048]{1,0:T(8,128)(2,1)}, u32[]{:S(2)}, u32[]{:S(2)}) collective-permute-start(bf16[128,2048]{1,0:T(8,128)(2,1)} %refs_4_.7), channel_id=1, source_target_pairs={{0,1},{1,0},{2,3},{3,2},{4,5},{5,4},{6,7},{7,6},{8,9},{9,8},{10,11... | collective-permute-start | bytes 1572872 | tf_op jit(solution)/shard_map/ppermute | solution.py:472
  3.5 12.5 %collective-permute-start.10 = (bf16[40,1024]{1,0:T(8,128)(2,1)}, bf16[40,1024]{1,0:T(8,128)(2,1)}, u32[]{:S(2)}, u32[]{:S(2)}) collective-permute-start(bf16[40,1024]{1,0:T(8,128)(2,1)} %get-tuple-element.60), channel_id=1, source_target_pairs={{0,7},{1,6},{2,5},{3,4},{4,3},{5,2},{6,1},{7,0},{8,15},{9,14},{10,... | collective-permute-start | bytes 245768 | tf_op jit(solution)/shard_map/ppermute | solution.py:467
  8.2 11.8 %collective-permute-start.7 = (bf16[40,1024]{1,0:T(8,128)(2,1)}, bf16[40,1024]{1,0:T(8,128)(2,1)}, u32[]{:S(2)}, u32[]{:S(2)}) collective-permute-start(bf16[40,1024]{1,0:T(8,128)(2,1)} %get-tuple-element.57), channel_id=1, source_target_pairs={{0,4},{1,5},{2,6},{3,7},{4,0},{5,1},{6,2},{7,3},{8,12},{9,13},{10,... | collective-permute-start | bytes 245768 | tf_op jit(solution)/shard_map/ppermute | solution.py:467
  8.3 1.5 %collective-permute-start = (s32[128,8]{0,1:T(8,128)}, s32[128,8]{0,1:T(8,128)}, u32[]{:S(2)}, u32[]{:S(2)}) collective-permute-start(s32[128,8]{0,1:T(8,128)} %param.11), channel_id=1, source_target_pairs={{0,1},{1,0},{2,3},{3,2},{4,5},{5,4},{6,7},{7,6},{8,9},{9,8},{10,11... | collective-permute-start | bytes 12296 | tf_op jit(solution)/shard_map/ppermute | solution.py:472
  8.3 1.6 %collective-permute-start.1 = (s32[128,8]{0,1:T(8,128)}, s32[128,8]{0,1:T(8,128)}, u32[]{:S(2)}, u32[]{:S(2)}) collective-permute-start(s32[128,8]{0,1:T(8,128)} %param.12), channel_id=1, source_target_pairs={{0,1},{1,0},{2,3},{3,2},{4,5},{5,4},{6,7},{7,6},{8,9},{9,8},{10,11... | collective-permute-start | bytes 12296 | tf_op jit(solution)/shard_map/ppermute | solution.py:472
  9.8 3.0 %collective-permute-start.2 = (f32[128,8]{0,1:T(8,128)}, f32[128,8]{0,1:T(8,128)}, u32[]{:S(2)}, u32[]{:S(2)}) collective-permute-start(f32[128,8]{0,1:T(8,128)} %param.13), channel_id=1, source_target_pairs={{0,1},{1,0},{2,3},{3,2},{4,5},{5,4},{6,7},{7,6},{8,9},{9,8},{10,11... | collective-permute-start | bytes 12296 | tf_op jit(solution)/shard_map/ppermute | solution.py:472
  9.9 10.8 %collective-permute-start.8 = (bf16[40,1024]{1,0:T(8,128)(2,1)}, bf16[40,1024]{1,0:T(8,128)(2,1)}, u32[]{:S(2)}, u32[]{:S(2)}) collective-permute-start(bf16[40,1024]{1,0:T(8,128)(2,1)} %get-tuple-element.58), channel_id=1, source_target_pairs={{0,5},{1,4},{2,7},{3,6},{4,1},{5,0},{6,3},{7,2},{8,13},{9,12},{10,... | collective-permute-start | bytes 245768 | tf_op jit(solution)/shard_map/ppermute | solution.py:467
  12.8 7.9 %collective-permute-start.9 = (bf16[40,1024]{1,0:T(8,128)(2,1)}, bf16[40,1024]{1,0:T(8,128)(2,1)}, u32[]{:S(2)}, u32[]{:S(2)}) collective-permute-start(bf16[40,1024]{1,0:T(8,128)(2,1)} %get-tuple-element.59), channel_id=1, source_target_pairs={{0,6},{1,7},{2,4},{3,5},{4,2},{5,3},{6,0},{7,1},{8,14},{9,15},{10,... | collective-permute-start | bytes 245768 | tf_op jit(solution)/shard_map/ppermute | solution.py:467
  15.9 8.6 %collective-permute-start.4 = (bf16[40,1024]{1,0:T(8,128)(2,1)}, bf16[40,1024]{1,0:T(8,128)(2,1)}, u32[]{:S(2)}, u32[]{:S(2)}) collective-permute-start(bf16[40,1024]{1,0:T(8,128)(2,1)} %get-tuple-element.54), channel_id=1, source_target_pairs={{0,1},{1,0},{2,3},{3,2},{4,5},{5,4},{6,7},{7,6},{8,9},{9,8},{10,11... | collective-permute-start | bytes 245768 | tf_op jit(solution)/shard_map/ppermute | solution.py:467
  16.0 10.0 %collective-permute-start.5 = (bf16[40,1024]{1,0:T(8,128)(2,1)}, bf16[40,1024]{1,0:T(8,128)(2,1)}, u32[]{:S(2)}, u32[]{:S(2)}) collective-permute-start(bf16[40,1024]{1,0:T(8,128)(2,1)} %get-tuple-element.55), channel_id=1, source_target_pairs={{0,2},{1,3},{2,0},{3,1},{4,6},{5,7},{6,4},{7,5},{8,10},{9,11},{10,... | collective-permute-start | bytes 245768 | tf_op jit(solution)/shard_map/ppermute | solution.py:467
  20.1 5.9 %collective-permute-start.6 = (bf16[40,1024]{1,0:T(8,128)(2,1)}, bf16[40,1024]{1,0:T(8,128)(2,1)}, u32[]{:S(2)}, u32[]{:S(2)}) collective-permute-start(bf16[40,1024]{1,0:T(8,128)(2,1)} %get-tuple-element.56), channel_id=1, source_target_pairs={{0,3},{1,2},{2,1},{3,0},{4,7},{5,6},{6,5},{7,4},{8,11},{9,10},{10,... | collective-permute-start | bytes 245768 | tf_op jit(solution)/shard_map/ppermute | solution.py:467
  20.7 18.3 %collective-permute-start.18 = (bf16[2,40,1024]{2,1,0:T(8,128)(2,1)}, bf16[2,40,1024]{2,1,0:T(8,128)(2,1)}, u32[]{:S(2)}, u32[]{:S(2)}) collective-permute-start(bf16[2,40,1024]{2,1,0:T(8,128)(2,1)} %get-tuple-element.73), channel_id=1, source_target_pairs={{0,2},{1,3},{2,0},{3,1},{4,6},{5,7},{6,4},{7,5},{8,10},{9,11},{10,... | collective-permute-start | bytes 491528 | tf_op jit(solution)/shard_map/ppermute | solution.py:467
  23.5 17.1 %collective-permute-start.19 = (bf16[2,40,1024]{2,1,0:T(8,128)(2,1)}, bf16[2,40,1024]{2,1,0:T(8,128)(2,1)}, u32[]{:S(2)}, u32[]{:S(2)}) collective-permute-start(bf16[2,40,1024]{2,1,0:T(8,128)(2,1)} %get-tuple-element.74), channel_id=1, source_target_pairs={{0,4},{1,5},{2,6},{3,7},{4,0},{5,1},{6,2},{7,3},{8,12},{9,13},{10,... | collective-permute-start | bytes 491528 | tf_op jit(solution)/shard_map/ppermute | solution.py:467
  24.5 16.8 %collective-permute-start.20 = (bf16[2,40,1024]{2,1,0:T(8,128)(2,1)}, bf16[2,40,1024]{2,1,0:T(8,128)(2,1)}, u32[]{:S(2)}, u32[]{:S(2)}) collective-permute-start(bf16[2,40,1024]{2,1,0:T(8,128)(2,1)} %get-tuple-element.75), channel_id=1, source_target_pairs={{0,6},{1,7},{2,4},{3,5},{4,2},{5,3},{6,0},{7,1},{8,14},{9,15},{10,... | collective-permute-start | bytes 491528 | tf_op jit(solution)/shard_map/ppermute | solution.py:467
  36.5 6.5 %collective-permute-start.11 = (bf16[2,40,1024]{2,1,0:T(8,128)(2,1)}, bf16[2,40,1024]{2,1,0:T(8,128)(2,1)}, u32[]{:S(2)}, u32[]{:S(2)}) collective-permute-start(bf16[2,40,1024]{2,1,0:T(8,128)(2,1)} %get-tuple-element.65), channel_id=1, source_target_pairs={{0,2},{1,3},{2,0},{3,1},{4,6},{5,7},{6,4},{7,5},{8,10},{9,11},{10,... | collective-permute-start | bytes 491528 | tf_op jit(solution)/shard_map/ppermute | solution.py:467
  37.6 19.1 %collective-permute-start.15 = (bf16[160,768]{1,0:T(8,128)(2,1)}, bf16[160,768]{1,0:T(8,128)(2,1)}, u32[]{:S(2)}, u32[]{:S(2)}) collective-permute-start(bf16[160,768]{1,0:T(8,128)(2,1)} %get-tuple-element.69.refs_2_), channel_id=1, source_target_pairs={{0,8},{8,0},{16,24},{24,16},{1,9},{9,1},{17,25},{25,17},{2,10},{10... | collective-permute-start | bytes 737288 | tf_op jit(solution)/shard_map/ppermute | solution.py:476
  39.0 17.6 %collective-permute-start.16 = (bf16[160,768]{1,0:T(8,128)(2,1)}, bf16[160,768]{1,0:T(8,128)(2,1)}, u32[]{:S(2)}, u32[]{:S(2)}) collective-permute-start(bf16[160,768]{1,0:T(8,128)(2,1)} %get-tuple-element.69.refs_2_), channel_id=1, source_target_pairs={{0,16},{8,24},{16,0},{24,8},{1,17},{9,25},{17,1},{25,9},{2,18},{10... | collective-permute-start | bytes 737288 | tf_op jit(solution)/shard_map/ppermute | solution.py:476
  40.6 16.1 %collective-permute-start.17 = (bf16[160,768]{1,0:T(8,128)(2,1)}, bf16[160,768]{1,0:T(8,128)(2,1)}, u32[]{:S(2)}, u32[]{:S(2)}) collective-permute-start(bf16[160,768]{1,0:T(8,128)(2,1)} %get-tuple-element.69.refs_2_), channel_id=1, source_target_pairs={{0,24},{8,16},{16,8},{24,0},{1,25},{9,17},{17,9},{25,1},{2,26},{10... | collective-permute-start | bytes 737288 | tf_op jit(solution)/shard_map/ppermute | solution.py:476
  41.4 15.2 %collective-permute-start.12 = (bf16[2,40,1024]{2,1,0:T(8,128)(2,1)}, bf16[2,40,1024]{2,1,0:T(8,128)(2,1)}, u32[]{:S(2)}, u32[]{:S(2)}) collective-permute-start(bf16[2,40,1024]{2,1,0:T(8,128)(2,1)} %get-tuple-element.66), channel_id=1, source_target_pairs={{0,4},{1,5},{2,6},{3,7},{4,0},{5,1},{6,2},{7,3},{8,12},{9,13},{10,... | collective-permute-start | bytes 491528 | tf_op jit(solution)/shard_map/ppermute | solution.py:467
  43.0 13.6 %collective-permute-start.13 = (bf16[2,40,1024]{2,1,0:T(8,128)(2,1)}, bf16[2,40,1024]{2,1,0:T(8,128)(2,1)}, u32[]{:S(2)}, u32[]{:S(2)}) collective-permute-start(bf16[2,40,1024]{2,1,0:T(8,128)(2,1)} %get-tuple-element.67), channel_id=1, source_target_pairs={{0,6},{1,7},{2,4},{3,5},{4,2},{5,3},{6,0},{7,1},{8,14},{9,15},{10,... | collective-permute-start | bytes 491528 | tf_op jit(solution)/shard_map/ppermute | solution.py:467
  56.6 24.1 %all-to-all-start = ((bf16[8,40,1024]{2,1,0:T(8,128)(2,1)}), bf16[8,40,1024]{2,1,0:T(8,128)(2,1)}, u32[]{:S(2)}, u32[]{:S(2)}) async-start(bf16[8,40,1024]{2,1,0:T(8,128)(2,1)} %get-tuple-element.86), calls=%async_computation | async-start | bytes 1310720 | tf_op jit(solution)/shard_map/all_to_all | solution.py:464
  65.6 3.7 %collective-permute-start.14 = (bf16[128,2048]{1,0:T(8,128)(2,1)}, bf16[128,2048]{1,0:T(8,128)(2,1)}, u32[]{:S(2)}, u32[]{:S(2)}) collective-permute-start(bf16[128,2048]{1,0:T(8,128)(2,1)} %shard_map.125), channel_id=1, source_target_pairs={{0,1},{1,0},{2,3},{3,2},{4,5},{5,4},{6,7},{7,6},{8,9},{9,8},{10,11... | collective-permute-start | bytes 1572872 | tf_op jit(solution)/shard_map/ppermute | solution.py:472
  65.8 7.3 %collective-permute-start.21 = (bf16[160,512]{1,0:T(8,128)(2,1)}, bf16[160,512]{1,0:T(8,128)(2,1)}, u32[]{:S(2)}, u32[]{:S(2)}) collective-permute-start(bf16[160,512]{1,0:T(8,128)(2,1)} %get-tuple-element.77), channel_id=1, source_target_pairs={{0,8},{8,0},{16,24},{24,16},{1,9},{9,1},{17,25},{25,17},{2,10},{10... | collective-permute-start | bytes 491528 | tf_op jit(solution)/shard_map/ppermute | solution.py:476
  67.3 10.0 %collective-permute-start.22 = (bf16[160,512]{1,0:T(8,128)(2,1)}, bf16[160,512]{1,0:T(8,128)(2,1)}, u32[]{:S(2)}, u32[]{:S(2)}) collective-permute-start(bf16[160,512]{1,0:T(8,128)(2,1)} %get-tuple-element.78), channel_id=1, source_target_pairs={{0,16},{8,24},{16,0},{24,8},{1,17},{9,25},{17,1},{25,9},{2,18},{10... | collective-permute-start | bytes 491528 | tf_op jit(solution)/shard_map/ppermute | solution.py:476
  68.8 8.5 %collective-permute-start.23 = (bf16[160,512]{1,0:T(8,128)(2,1)}, bf16[160,512]{1,0:T(8,128)(2,1)}, u32[]{:S(2)}, u32[]{:S(2)}) collective-permute-start(bf16[160,512]{1,0:T(8,128)(2,1)} %get-tuple-element.79), channel_id=1, source_target_pairs={{0,24},{8,16},{16,8},{24,0},{1,25},{9,17},{17,9},{25,1},{2,26},{10... | collective-permute-start | bytes 491528 | tf_op jit(solution)/shard_map/ppermute | solution.py:476

commit v4 on v3

--- a/solution.py
+++ b/solution.py
@@ -19,10 +19,14 @@
 TURN = 1
 JOIN = True
 TIE_O = ()
-TIE_S = False
+TIE_S = True
 TIE_L = True
-TIE_P = (4, 5, 6, 7)
-NEAR = (1, 2, 3)
+TIE_P = (4,5)
+NEAR = (1,)
+ORDER_C = ()
+MATE_FIRST = ()
+CHEAP = 1000000
+FIRST_P = False
 TIE_B = "hidden"
 TIE_G = True
 F32 = jnp.float32
@@ -80,14 +84,13 @@
 def unpack_rows(blocks):
     flat = jnp.concatenate(blocks, axis=0)
     count = len(blocks)
-    shape = (count * PAIR_ROWS, count * BLOCK_ROWS)
+    rows = count * PAIR_ROWS
+    shape = (rows, count * BLOCK_ROWS)
     place = row_places(iota(shape, 0), count)
     col = iota(shape, 1)
-    out = []
-    for half in range(HALVES):
-        pick = (col == place + half * PAIR_ROWS).astype(F32).astype(BF16)
-        out.append(mm(pick, flat).astype(BF16))
-    return jnp.concatenate(out, axis=1)
+    picks = [(col == place + half * PAIR_ROWS).astype(F32) for half in range(HALVES)]
+    out = mm(jnp.concatenate(picks, axis=0).astype(BF16), flat).astype(BF16)
+    return jnp.concatenate([out[h * rows : (h + 1) * rows] for h in range(HALVES)], axis=1)
 
 
 class Blocks:
@@ -110,7 +113,8 @@
 
 
 def pack_windows(parts, n, c, size, counts_ref, group, dims):
-    total = None
+    picks, pieces = [], []
+    half = parts[0].shape[1 if dims == NN else 0] // HALVES
     for e, (x, (start, stop)) in enumerate(zip(parts, windows(n))):
         shape = (size * BLOCK_ROWS, stop - start)
         row = iota(shape, 0)
@@ -122,15 +126,11 @@
         if n > size:
             block = index - inside * n
             place = jnp.where((block >= c) & (block < c + size), place, -BLOCK_ROWS * n)
-        picks = [(row == place + h * PAIR_ROWS).astype(F32).astype(BF16) for h in range(HALVES)]
-        part = None
-        half = x.shape[1 if dims == NN else 0] // HALVES
-        for h, pick in enumerate(picks):
-            piece = x[:, h * half : (h + 1) * half] if dims == NN else x[h * half : (h + 1) * half, :]
-            product = mm(pick, piece, dims)
-            part = product if part is None else part + product
-        total = part if total is None else total + part
-    return total
+        for h in range(HALVES):
+            picks.append((row == place + h * PAIR_ROWS).astype(F32).astype(BF16))
+            span = slice(h * half, (h + 1) * half)
+            pieces.append(x[:, span] if dims == NN else x[span, :])
+    return mm(jnp.concatenate(picks, axis=1), jnp.concatenate(pieces, axis=0 if dims == NN else 1), dims)
 
 
 def windows(n):
@@ -463,10 +463,10 @@
         if way == "all":
             return [lax.all_to_all(values[0], "expert", split_axis=0, concat_axis=0, tiled=True)]
         step = n // len(values)
-        return [values[0]] + [
-            lax.ppermute(values[d], "expert", [(i, i ^ (step * d)) for i in range(n)])
-            for d in range(1, len(values))
-        ]
+        got = {0: values[0]}
+        for d in sorted(range(1, len(values)), key=lambda d: (d not in ORDER_C, ORDER_C.index(d) if d in ORDER_C else d)):
+            got[d] = lax.ppermute(values[d], "expert", [(i, i ^ (step * d)) for i in range(n)])
+        return [got[d] for d in range(len(values))]
 
     def from_mate(x):
         return lax.ppermute(x, "expert", [(i, i ^ 1) for i in range(n)])
@@ -501,10 +501,19 @@
         near = [sent_c[k] for k in NEAR]
         for k, v in zip(NEAR, tie(near, sent_p)):
             sent_c[k] = v
+    if MATE_FIRST:
+        for k, v in zip(MATE_FIRST, tie([sent_c[k] for k in MATE_FIRST], mate[0])):
+            sent_c[k] = v
     got_c = exchange("permute", sent_c)
-    if TIE_P:
+    if FIRST_P:
+        early = lax.ppermute(sent_p[1], "expert", [(i, i ^ 2) for i in range(n)])
+        late = tie(sent_p[2:], ([got_c[k] for k in TIE_P], early))
+        got_p = [sent_p[0], early] + [
+            lax.ppermute(v, "expert", [(i, i ^ (2 * d)) for i in range(n)]) for d, v in enumerate(late, 2)
+        ]
+    else:
         sent_p = tie(sent_p, [got_c[k] for k in TIE_P])
-    got_p = exchange("pair", sent_p)
+        got_p = exchange("pair", sent_p)
 
     weight_bytes = 3 * local * width * ff * 2
     expert_flops = 2 * 3 * rows * local * width * ff
@@ -537,7 +546,7 @@
         [scalars, place] + copy(tie(ids, results[0]), codes, weights, *mate),
         [mix, mix_pair, mix_pair],
         0,
-        3 * tok_count * total * 4,
+        3 * tok_count * total * 4 // CHEAP,
     )
     sent_o, (hidden, slope, silu) = results[: len(out_o)], results[len(out_o) :]
     if TIE_O:
@@ -571,8 +580,8 @@
         part_kernel,
         [place] + copy(mix_mate, *got_o),
         jax.ShapeDtypeStruct(tokens.shape, BF16),
-        total * tok_count * width,
-        block_bytes,
+        total * tok_count * width // CHEAP,
+        block_bytes // CHEAP,
     )
 
     def spread(pair, x, mix, given):
@@ -581,17 +590,18 @@
             lambda copies, *refs: spread_kernel(copies, n, pair, *refs),
             [place] + copy(ids, weights, comp_scale, x, mix, *given),
             out,
-            2 * total * tok_count * width,
-            block_bytes,
+            2 * total * tok_count * width // CHEAP,
+            block_bytes // CHEAP,
             [pltpu.VMEM(out.shape, BF16), pltpu.SemaphoreType.DMA((HALVES,))],
             lazy=True,
             out_spec=HBM,
         )
 
     if TIE_S:
-        mix_own = tie(mix_own, all_shares)
-    layer_output = spread(True, tokens, mix_own, [from_mate(part), *got_o])
-    if TIE_L:
+        part = tie(part, all_shares)
+    part = from_mate(part)
+    if not TIE_S:
+        layer_output = spread(True, tokens, mix_own, [part, *got_o])
         all_shares = tie(all_shares, layer_output)
     grad_shape = jax.ShapeDtypeStruct((local, ff, width // parts), BF16)
     grad_down = call(
@@ -603,6 +613,8 @@
         [pltpu.VMEM(grad_shape.shape, BF16), pltpu.SemaphoreType.DMA((local,))],
         out_spec=HBM,
     )
+    if TIE_S:
+        layer_output = spread(True, tokens, tie(mix_own, grad_down), [part, *got_o])
     if TIE_G:
         mix_g = tie(mix_g, (layer_output, grad_down))
     grad_tokens = spread(False, cotangent, mix_g, got_b)

time: 84.1 us -> 81.8 us (0.973)
  waiting for transfers between devices: 9.47 us -> 4.83 us
  starting transfers between devices: 32.4 us -> 35.3 us
    ppermute x13, starting transfers between devices: 19.3 us -> 22.7 us  [exchange(): lax.ppermute(values[d], 'expert', [(i, i ^ step * d) for i in range(n)])]
    ppermute x13, waiting for transfers between devices: 3.12 us -> 0.03 us  [exchange(): lax.ppermute(values[d], 'expert', [(i, i ^ step * d) for i in range(n)])]
    ppermute x6, waiting for transfers between devices: 5.34 us -> 3.27 us  [exchange_dp(): lax.ppermute(values[k], 'dp', [(i, i ^ k) for i in range(parts)])]
  transfers between devices with their start and end apart: 25 -> 25, of which waited for: 5 -> 3; matrix products, arithmetic and copies ran while one was open for 0% -> 0% of each run, Pallas kernels for 43% -> 43%
where the time goes in v4:
time: 81.8 us; the launch traced here: 81.3 us
  Pallas kernels  40.2 us (49%)
  starting transfers between devices  35.3 us (43%)
  waiting for transfers between devices  4.83 us (6%)
  between operations  0.95 us (1%)
    pallas_call x9, Pallas kernels, call(): pl.pallas_call(body, out_shape=outs, in_specs=specs, out_specs=jax.tree.m...  40.2 us
    ppermute x13, starting transfers between devices, exchange(): lax.ppermute(values[d], 'expert', [(i, i ^ step * d) for i in range(n)])  22.7 us
    ppermute x6, starting transfers between devices, exchange_dp(): lax.ppermute(values[k], 'dp', [(i, i ^ k) for i in range(parts)])  7.04 us
    all_to_all x1, starting transfers between devices, exchange(): lax.all_to_all(values[0], 'expert', split_axis=0, concat_axis=0, tiled=True)  4.4 us
    ppermute x6, waiting for transfers between devices, exchange_dp(): lax.ppermute(values[k], 'dp', [(i, i ^ k) for i in range(parts)])  3.27 us
  transfers between devices with their start and end apart: 25, of which 3 were waited for; matrix products, arithmetic and copies ran while one was open for 0% of the time, Pallas kernels for 43%

profile of v4, /device:TPU:0, one launch (start us, length us, event | category | flops | bytes accessed | tf_op | source)
XLA Modules:
  0.0 81.3 jit_solution(17418584664323874003)
XLA Ops:
  0.6 2.4 %shard_map.121 = (bf16[40,1024]{1,0:T(8,128)(2,1)}, bf16[40,1024]{1,0:T(8,128)(2,1)}, bf16[40,1024]{1,0:T(8,128)(2,1)}, bf16[40,1024]{1,0:T(8,128)(2,1)}, bf16[4...) custom-call(s32[1]{0:T(128)} %bitcast.refs_0_.refs_1_, ...), custom_call_target="tpu_custom_call" | custom-call | flops 167772160 | bytes 655360 | tf_op jit(solution)/shard_map/pallas_call | solution.py:424
  3.0 0.5 collective-permute-start.3
  3.5 3.7 %collective-permute-start.7 = (bf16[40,1024]{1,0:T(8,128)(2,1)}, bf16[40,1024]{1,0:T(8,128)(2,1)}, u32[]{:S(2)}, u32[]{:S(2)}) collective-permute-start(bf16[40,1024]{1,0:T(8,128)(2,1)} %get-tuple-element.51), channel_id=1, source_target_pairs={{0,4},{1,5},{2,6},{3,7},{4,0},{5,1},{6,2},{7,3},{8,12},{9,13},{10,... | collective-permute-start | bytes 245768 | tf_op jit(solution)/shard_map/ppermute | solution.py:468
  7.4 0.4 collective-permute-start.1
  7.8 1.0 %collective-permute-done = s32[128,8]{0,1:T(8,128)} collective-permute-done((s32[128,8]{0,1:T(8,128)}, s32[128,8]{0,1:T(8,128)}, u32[]{:S(2)}, u32[]{:S(2)}) %collective-permute-start) | collective-permute-done | bytes 4128 | tf_op jit(solution)/shard_map/ppermute | solution.py:472
  8.9 1.8 %collective-permute-start.5 = (bf16[40,1024]{1,0:T(8,128)(2,1)}, bf16[40,1024]{1,0:T(8,128)(2,1)}, u32[]{:S(2)}, u32[]{:S(2)}) collective-permute-start(bf16[40,1024]{1,0:T(8,128)(2,1)} %get-tuple-element.49), channel_id=1, source_target_pairs={{0,2},{1,3},{2,0},{3,1},{4,6},{5,7},{6,4},{7,5},{8,10},{9,11},{10,... | collective-permute-start | bytes 245768 | tf_op jit(solution)/shard_map/ppermute | solution.py:468
  10.7 1.1 %collective-permute-start.6 = (bf16[40,1024]{1,0:T(8,128)(2,1)}, bf16[40,1024]{1,0:T(8,128)(2,1)}, u32[]{:S(2)}, u32[]{:S(2)}) collective-permute-start(bf16[40,1024]{1,0:T(8,128)(2,1)} %get-tuple-element.50), channel_id=1, source_target_pairs={{0,3},{1,2},{2,1},{3,0},{4,7},{5,6},{6,5},{7,4},{8,11},{9,10},{10,... | collective-permute-start | bytes 245768 | tf_op jit(solution)/shard_map/ppermute | solution.py:468
  11.8 2.5 %collective-permute-start.9 = (bf16[40,1024]{1,0:T(8,128)(2,1)}, bf16[40,1024]{1,0:T(8,128)(2,1)}, u32[]{:S(2)}, u32[]{:S(2)}) collective-permute-start(bf16[40,1024]{1,0:T(8,128)(2,1)} %get-tuple-element.53), channel_id=1, source_target_pairs={{0,6},{1,7},{2,4},{3,5},{4,2},{5,3},{6,0},{7,1},{8,14},{9,15},{10,... | collective-permute-start | bytes 245768 | tf_op jit(solution)/shard_map/ppermute | solution.py:468
  14.3 2.7 %shard_map.122 = (bf16[2,40,1024]{2,1,0:T(8,128)(2,1)}, bf16[2,40,1024]{2,1,0:T(8,128)(2,1)}, bf16[2,40,1024]{2,1,0:T(8,128)(2,1)}, bf16[2,40,1024]{2,1,0:T(8,128)(2,1)}) custom-call(s32[1]{0:T(128)} %bitcast.refs_0_.refs_1_, s32[16]{0:T(128)} %refs_0_.7, s32[8,128]{1,0:T(8,128)} %bitcast.9, s32[8,128]{1,0:T(8,128)} %bitcast.19, f32[8,128]{1,0:T(8,128)} %bitcast.14, ...), custom_call_target="tpu_custom_call" | custom-call | flops 167772160 | bytes 655360 | tf_op jit(solution)/shard_map/pallas_call | solution.py:424
  17.0 0.9 %collective-permute-start.10 = (bf16[40,1024]{1,0:T(8,128)(2,1)}, bf16[40,1024]{1,0:T(8,128)(2,1)}, u32[]{:S(2)}, u32[]{:S(2)}) collective-permute-start(bf16[40,1024]{1,0:T(8,128)(2,1)} %get-tuple-element.54), channel_id=1, source_target_pairs={{0,7},{1,6},{2,5},{3,4},{4,3},{5,2},{6,1},{7,0},{8,15},{9,14},{10,... | collective-permute-start | bytes 245768 | tf_op jit(solution)/shard_map/ppermute | solution.py:468
  17.9 0.6 collective-permute-start.4
  18.5 6.0 %collective-permute-start.15 = (bf16[2,40,1024]{2,1,0:T(8,128)(2,1)}, bf16[2,40,1024]{2,1,0:T(8,128)(2,1)}, u32[]{:S(2)}, u32[]{:S(2)}) collective-permute-start(bf16[2,40,1024]{2,1,0:T(8,128)(2,1)} %get-tuple-element.63), channel_id=1, source_target_pairs={{0,4},{1,5},{2,6},{3,7},{4,0},{5,1},{6,2},{7,3},{8,12},{9,13},{10,... | collective-permute-start | bytes 491528 | tf_op jit(solution)/shard_map/ppermute | solution.py:468
  24.6 1.4 %collective-permute-start.16 = (bf16[2,40,1024]{2,1,0:T(8,128)(2,1)}, bf16[2,40,1024]{2,1,0:T(8,128)(2,1)}, u32[]{:S(2)}, u32[]{:S(2)}) collective-permute-start(bf16[2,40,1024]{2,1,0:T(8,128)(2,1)} %get-tuple-element.64), channel_id=1, source_target_pairs={{0,6},{1,7},{2,4},{3,5},{4,2},{5,3},{6,0},{7,1},{8,14},{9,15},{10,... | collective-permute-start | bytes 491528 | tf_op jit(solution)/shard_map/ppermute | solution.py:468
  26.0 10.1 %shard_map.123 = (bf16[2,40,1024]{2,1,0:T(8,128)(2,1)}, bf16[2,40,1024]{2,1,0:T(8,128)(2,1)}, bf16[2,40,1024]{2,1,0:T(8,128)(2,1)}, bf16[2,40,1024]{2,1,0:T(8,12...) custom-call(s32[16]{0:T(128)} %refs_0_.7, s32[1]{0:T(128)} %bitcast.refs_0_.refs_1_, ...), custom_call_target="tpu_custom_call" | custom-call | flops 3019898880 | bytes 18874368 | tf_op jit(solution)/shard_map/pallas_call | solution.py:424
  36.2 0.7 collective-permute-start.20
  36.8 2.5 %collective-permute-start.13 = (bf16[160,768]{1,0:T(8,128)(2,1)}, bf16[160,768]{1,0:T(8,128)(2,1)}, u32[]{:S(2)}, u32[]{:S(2)}) collective-permute-start(bf16[160,768]{1,0:T(8,128)(2,1)} %get-tuple-element.58.refs_2_), channel_id=1, source_target_pairs={{0,24},{8,16},{16,8},{24,0},{1,25},{9,17},{17,9},{25,1},{2,26},{10... | collective-permute-start | bytes 737288 | tf_op jit(solution)/shard_map/ppermute | solution.py:476
  39.3 0.5 collective-permute-start.12
  39.8 0.5 collective-permute-start.11
  40.3 2.4 %collective-permute-start.21 = (bf16[2,40,1024]{2,1,0:T(8,128)(2,1)}, bf16[2,40,1024]{2,1,0:T(8,128)(2,1)}, u32[]{:S(2)}, u32[]{:S(2)}) collective-permute-start(bf16[2,40,1024]{2,1,0:T(8,128)(2,1)} %get-tuple-element.72), channel_id=1, source_target_pairs={{0,4},{1,5},{2,6},{3,7},{4,0},{5,1},{6,2},{7,3},{8,12},{9,13},{10,... | collective-permute-start | bytes 491528 | tf_op jit(solution)/shard_map/ppermute | solution.py:468
  42.7 1.6 %collective-permute-start.22 = (bf16[2,40,1024]{2,1,0:T(8,128)(2,1)}, bf16[2,40,1024]{2,1,0:T(8,128)(2,1)}, u32[]{:S(2)}, u32[]{:S(2)}) collective-permute-start(bf16[2,40,1024]{2,1,0:T(8,128)(2,1)} %get-tuple-element.73), channel_id=1, source_target_pairs={{0,6},{1,7},{2,4},{3,5},{4,2},{5,3},{6,0},{7,1},{8,14},{9,15},{10,... | collective-permute-start | bytes 491528 | tf_op jit(solution)/shard_map/ppermute | solution.py:468
  44.2 11.8 %shard_map.125 = (bf16[8,40,1024]{2,1,0:T(8,128)(2,1)}, bf16[160,512]{1,0:T(8,128)(2,1)}, bf16[160,512]{1,0:T(8,128)(2,1)}, bf16[160,512]{1,0:T(8,128)(2,1)}, bf16[160,512]{1,0:T(8,128)(2,1)}) custom-call(s32[16]{0:T(128)} %refs_0_.7, s32[1]{0:T(128)} %bitcast.refs_0_.refs_1_, s32[1]{0:T(128)} %bitcast.7.refs_2_, bf16[16,2048]{1,0:T(8,128)(2,1)} %refs_3_.7, ...), custom_call_target="tpu_custom_call" | custom-call | flops 3019898880 | bytes 18874368 | tf_op jit(solution)/shard_map/pallas_call | solution.py:424
  56.1 4.4 %all-to-all-start = ((bf16[8,40,1024]{2,1,0:T(8,128)(2,1)}), bf16[8,40,1024]{2,1,0:T(8,128)(2,1)}, u32[]{:S(2)}, u32[]{:S(2)}) async-start(bf16[8,40,1024]{2,1,0:T(8,128)(2,1)} %get-tuple-element.78), calls=%async_computation | async-start | bytes 1310720 | tf_op jit(solution)/shard_map/all_to_all | solution.py:464
  60.5 1.5 %collective-permute-start.17 = (bf16[160,512]{1,0:T(8,128)(2,1)}, bf16[160,512]{1,0:T(8,128)(2,1)}, u32[]{:S(2)}, u32[]{:S(2)}) collective-permute-start(bf16[160,512]{1,0:T(8,128)(2,1)} %get-tuple-element.66), channel_id=1, source_target_pairs={{0,8},{8,0},{16,24},{24,16},{1,9},{9,1},{17,25},{25,17},{2,10},{10... | collective-permute-start | bytes 491528 | tf_op jit(solution)/shard_map/ppermute | solution.py:476
  62.0 1.5 %collective-permute-start.18 = (bf16[160,512]{1,0:T(8,128)(2,1)}, bf16[160,512]{1,0:T(8,128)(2,1)}, u32[]{:S(2)}, u32[]{:S(2)}) collective-permute-start(bf16[160,512]{1,0:T(8,128)(2,1)} %get-tuple-element.67), channel_id=1, source_target_pairs={{0,16},{8,24},{16,0},{24,8},{1,17},{9,25},{17,1},{25,9},{2,18},{10... | collective-permute-start | bytes 491528 | tf_op jit(solution)/shard_map/ppermute | solution.py:476
  63.5 0.5 collective-permute-start.19
  64.0 2.1 %shard_map.124 = (bf16[256,320]{1,0:T(8,128)(2,1)}, bf16[256,160]{1,0:T(8,128)(2,1)}, bf16[256,160]{1,0:T(8,128)(2,1)}) custom-call(s32[16]{0:T(128)} %refs_0_.7, s32[1]{0:T(128)} %bitcast.refs_0_.refs_1_, s32[8,128]{1,0:T(8,128)} %bitcast.10, s32[8,128]{1,0:T(8,128)} %bitcast.20, f32[8,128]{1,0:T(8,128)} %bitcast.15, s32[8,128]{1,0:T(8,128)} %bitcast.4.refs_6_.refs_5_, ...), custom_call_target="tpu_custom_call" | custom-call | tf_op jit(solution)/shard_map/pallas_call | solution.py:424
  66.2 2.4 %shard_map.127 = bf16[128,2048]{1,0:T(8,128)(2,1)} custom-call(s32[1]{0:T(128)} %bitcast.refs_0_.refs_1_, bf16[256,160]{1,0:T(8,128)(2,1)} %get-tuple-element.70.refs_1_, bf16[2,40,1024]{2,1,0:T(8,128)(2,1)} %get-tuple-element.55.refs_2_.refs_7_, bf16[2,40,1024]{2,1,0:T(8,128)(2,1)} %collective-permute-done.20.refs_3_.refs_8_, ...), custom_call_target="tpu_custom_call" | custom-call | flops 83 | tf_op jit(solution)/shard_map/pallas_call | solution.py:424
  68.5 3.3 %collective-permute-done.18.refs_8_ = bf16[160,512]{1,0:T(8,128)(2,1)} collective-permute-done((bf16[160,512]{1,0:T(8,128)(2,1)}, bf16[160,512]{1,0:T(8,128)(2,1)}, u32[]{:S(2)}, u32[]{:S(2)}) %collective-permute-start.18) | collective-permute-done | bytes 163872 | tf_op jit(solution)/shard_map/ppermute | solution.py:476
  71.8 3.5 %shard_map.126 = bf16[2,768,512]{2,1,0:T(8,128)(2,1)} custom-call(s32[16]{0:T(128)} %refs_0_.7, s32[1]{0:T(128)} %bitcast.refs_0_.refs_1_, bf16[160,768]{1,0:T(8,128)(2,1)} %get-tuple-element.58.refs_2_, bf16[160,768]{1,0:T(8,128)(2,1)} %collective-permute-done.11.refs_3_, bf16[160,768]{1,0:T(8,128)(2,1)} %collective-permute-done.12.refs_4_, ...), custom_call_target="tpu_custom_call" | custom-call | flops 1006632960 | bytes 1638400 | tf_op jit(solution)/shard_map/pallas_call | solution.py:424
  75.3 2.6 %shard_map.128 = bf16[128,2048]{1,0:T(8,128)(2,1)} custom-call(s32[1]{0:T(128)} %bitcast.refs_0_.refs_1_, s32[8,128]{1,0:T(8,128)} %bitcast.11, f32[8,128]{1,0:T(8,128)} %bitcast.16, bf16[16,2048]{1,0:T(8,128)(2,1)} %refs_3_.7, bf16[128,2048]{1,0:T(8,128)(2,1)} %refs_4_.6, bf16[256,160]{1,0:T(8,128)(2,1)} %get-tuple-element.69.refs_5_, ...), custom_call_target="tpu_custom_call" | custom-call | flops 167 | tf_op jit(solution)/shard_map/pallas_call | solution.py:424
  77.9 0.5 all-to-all-done.refs_6_
  78.5 2.7 %shard_map.129 = bf16[128,2048]{1,0:T(8,128)(2,1)} custom-call(s32[1]{0:T(128)} %bitcast.refs_0_.refs_1_, s32[8,128]{1,0:T(8,128)} %bitcast.12, f32[8,128]{1,0:T(8,128)} %bitcast.17, bf16[16,2048]{1,0:T(8,128)(2,1)} %refs_3_.7, bf16[128,2048]{1,0:T(8,128)(2,1)} %refs_4_.7, bf16[256,320]{1,0:T(8,128)(2,1)} %get-tuple-element.76.refs_5_, ...), custom_call_target="tpu_custom_call" | custom-call | flops 167 | tf_op jit(solution)/shard_map/pallas_call | solution.py:424
  (27 shorter events, 0.4 us)
Async XLA Ops:
  3.0 8.8 %collective-permute-start.3 = (bf16[128,2048]{1,0:T(8,128)(2,1)}, bf16[128,2048]{1,0:T(8,128)(2,1)}, u32[]{:S(2)}, u32[]{:S(2)}) collective-permute-start(bf16[128,2048]{1,0:T(8,128)(2,1)} %refs_4_.7), channel_id=1, source_target_pairs={{0,1},{1,0},{2,3},{3,2},{4,5},{5,4},{6,7},{7,6},{8,9},{9,8},{10,11... | collective-permute-start | bytes 1572872 | tf_op jit(solution)/shard_map/ppermute | solution.py:472
  3.5 13.5 %collective-permute-start.7 = (bf16[40,1024]{1,0:T(8,128)(2,1)}, bf16[40,1024]{1,0:T(8,128)(2,1)}, u32[]{:S(2)}, u32[]{:S(2)}) collective-permute-start(bf16[40,1024]{1,0:T(8,128)(2,1)} %get-tuple-element.51), channel_id=1, source_target_pairs={{0,4},{1,5},{2,6},{3,7},{4,0},{5,1},{6,2},{7,3},{8,12},{9,13},{10,... | collective-permute-start | bytes 245768 | tf_op jit(solution)/shard_map/ppermute | solution.py:468
  7.2 10.7 %collective-permute-start.8 = (bf16[40,1024]{1,0:T(8,128)(2,1)}, bf16[40,1024]{1,0:T(8,128)(2,1)}, u32[]{:S(2)}, u32[]{:S(2)}) collective-permute-start(bf16[40,1024]{1,0:T(8,128)(2,1)} %get-tuple-element.52), channel_id=1, source_target_pairs={{0,5},{1,4},{2,7},{3,6},{4,1},{5,0},{6,3},{7,2},{8,13},{9,12},{10,... | collective-permute-start | bytes 245768 | tf_op jit(solution)/shard_map/ppermute | solution.py:468
  7.3 1.5 %collective-permute-start = (s32[128,8]{0,1:T(8,128)}, s32[128,8]{0,1:T(8,128)}, u32[]{:S(2)}, u32[]{:S(2)}) collective-permute-start(s32[128,8]{0,1:T(8,128)} %param.11), channel_id=1, source_target_pairs={{0,1},{1,0},{2,3},{3,2},{4,5},{5,4},{6,7},{7,6},{8,9},{9,8},{10,11... | collective-permute-start | bytes 12296 | tf_op jit(solution)/shard_map/ppermute | solution.py:472
  7.4 1.5 %collective-permute-start.1 = (s32[128,8]{0,1:T(8,128)}, s32[128,8]{0,1:T(8,128)}, u32[]{:S(2)}, u32[]{:S(2)}) collective-permute-start(s32[128,8]{0,1:T(8,128)} %param.12), channel_id=1, source_target_pairs={{0,1},{1,0},{2,3},{3,2},{4,5},{5,4},{6,7},{7,6},{8,9},{9,8},{10,11... | collective-permute-start | bytes 12296 | tf_op jit(solution)/shard_map/ppermute | solution.py:472
  8.8 2.0 %collective-permute-start.2 = (f32[128,8]{0,1:T(8,128)}, f32[128,8]{0,1:T(8,128)}, u32[]{:S(2)}, u32[]{:S(2)}) collective-permute-start(f32[128,8]{0,1:T(8,128)} %param.13), channel_id=1, source_target_pairs={{0,1},{1,0},{2,3},{3,2},{4,5},{5,4},{6,7},{7,6},{8,9},{9,8},{10,11... | collective-permute-start | bytes 12296 | tf_op jit(solution)/shard_map/ppermute | solution.py:472
  8.9 9.6 %collective-permute-start.5 = (bf16[40,1024]{1,0:T(8,128)(2,1)}, bf16[40,1024]{1,0:T(8,128)(2,1)}, u32[]{:S(2)}, u32[]{:S(2)}) collective-permute-start(bf16[40,1024]{1,0:T(8,128)(2,1)} %get-tuple-element.49), channel_id=1, source_target_pairs={{0,2},{1,3},{2,0},{3,1},{4,6},{5,7},{6,4},{7,5},{8,10},{9,11},{10,... | collective-permute-start | bytes 245768 | tf_op jit(solution)/shard_map/ppermute | solution.py:468
  10.7 7.8 %collective-permute-start.6 = (bf16[40,1024]{1,0:T(8,128)(2,1)}, bf16[40,1024]{1,0:T(8,128)(2,1)}, u32[]{:S(2)}, u32[]{:S(2)}) collective-permute-start(bf16[40,1024]{1,0:T(8,128)(2,1)} %get-tuple-element.50), channel_id=1, source_target_pairs={{0,3},{1,2},{2,1},{3,0},{4,7},{5,6},{6,5},{7,4},{8,11},{9,10},{10,... | collective-permute-start | bytes 245768 | tf_op jit(solution)/shard_map/ppermute | solution.py:468
  11.8 12.7 %collective-permute-start.9 = (bf16[40,1024]{1,0:T(8,128)(2,1)}, bf16[40,1024]{1,0:T(8,128)(2,1)}, u32[]{:S(2)}, u32[]{:S(2)}) collective-permute-start(bf16[40,1024]{1,0:T(8,128)(2,1)} %get-tuple-element.53), channel_id=1, source_target_pairs={{0,6},{1,7},{2,4},{3,5},{4,2},{5,3},{6,0},{7,1},{8,14},{9,15},{10,... | collective-permute-start | bytes 245768 | tf_op jit(solution)/shard_map/ppermute | solution.py:468
  17.0 9.0 %collective-permute-start.10 = (bf16[40,1024]{1,0:T(8,128)(2,1)}, bf16[40,1024]{1,0:T(8,128)(2,1)}, u32[]{:S(2)}, u32[]{:S(2)}) collective-permute-start(bf16[40,1024]{1,0:T(8,128)(2,1)} %get-tuple-element.54), channel_id=1, source_target_pairs={{0,7},{1,6},{2,5},{3,4},{4,3},{5,2},{6,1},{7,0},{8,15},{9,14},{10,... | collective-permute-start | bytes 245768 | tf_op jit(solution)/shard_map/ppermute | solution.py:468
  17.9 8.1 %collective-permute-start.4 = (bf16[40,1024]{1,0:T(8,128)(2,1)}, bf16[40,1024]{1,0:T(8,128)(2,1)}, u32[]{:S(2)}, u32[]{:S(2)}) collective-permute-start(bf16[40,1024]{1,0:T(8,128)(2,1)} %get-tuple-element.48), channel_id=1, source_target_pairs={{0,1},{1,0},{2,3},{3,2},{4,5},{5,4},{6,7},{7,6},{8,9},{9,8},{10,11... | collective-permute-start | bytes 245768 | tf_op jit(solution)/shard_map/ppermute | solution.py:468
  18.5 20.7 %collective-permute-start.14 = (bf16[2,40,1024]{2,1,0:T(8,128)(2,1)}, bf16[2,40,1024]{2,1,0:T(8,128)(2,1)}, u32[]{:S(2)}, u32[]{:S(2)}) collective-permute-start(bf16[2,40,1024]{2,1,0:T(8,128)(2,1)} %get-tuple-element.62), channel_id=1, source_target_pairs={{0,2},{1,3},{2,0},{3,1},{4,6},{5,7},{6,4},{7,5},{8,10},{9,11},{10,... | collective-permute-start | bytes 491528 | tf_op jit(solution)/shard_map/ppermute | solution.py:468
  18.5 21.2 %collective-permute-start.15 = (bf16[2,40,1024]{2,1,0:T(8,128)(2,1)}, bf16[2,40,1024]{2,1,0:T(8,128)(2,1)}, u32[]{:S(2)}, u32[]{:S(2)}) collective-permute-start(bf16[2,40,1024]{2,1,0:T(8,128)(2,1)} %get-tuple-element.63), channel_id=1, source_target_pairs={{0,4},{1,5},{2,6},{3,7},{4,0},{5,1},{6,2},{7,3},{8,12},{9,13},{10,... | collective-permute-start | bytes 491528 | tf_op jit(solution)/shard_map/ppermute | solution.py:468
  24.6 15.8 %collective-permute-start.16 = (bf16[2,40,1024]{2,1,0:T(8,128)(2,1)}, bf16[2,40,1024]{2,1,0:T(8,128)(2,1)}, u32[]{:S(2)}, u32[]{:S(2)}) collective-permute-start(bf16[2,40,1024]{2,1,0:T(8,128)(2,1)} %get-tuple-element.64), channel_id=1, source_target_pairs={{0,6},{1,7},{2,4},{3,5},{4,2},{5,3},{6,0},{7,1},{8,14},{9,15},{10,... | collective-permute-start | bytes 491528 | tf_op jit(solution)/shard_map/ppermute | solution.py:468
  36.2 6.5 %collective-permute-start.20 = (bf16[2,40,1024]{2,1,0:T(8,128)(2,1)}, bf16[2,40,1024]{2,1,0:T(8,128)(2,1)}, u32[]{:S(2)}, u32[]{:S(2)}) collective-permute-start(bf16[2,40,1024]{2,1,0:T(8,128)(2,1)} %get-tuple-element.71), channel_id=1, source_target_pairs={{0,2},{1,3},{2,0},{3,1},{4,6},{5,7},{6,4},{7,5},{8,10},{9,11},{10,... | collective-permute-start | bytes 491528 | tf_op jit(solution)/shard_map/ppermute | solution.py:468
  36.8 19.2 %collective-permute-start.13 = (bf16[160,768]{1,0:T(8,128)(2,1)}, bf16[160,768]{1,0:T(8,128)(2,1)}, u32[]{:S(2)}, u32[]{:S(2)}) collective-permute-start(bf16[160,768]{1,0:T(8,128)(2,1)} %get-tuple-element.58.refs_2_), channel_id=1, source_target_pairs={{0,24},{8,16},{16,8},{24,0},{1,25},{9,17},{17,9},{25,1},{2,26},{10... | collective-permute-start | bytes 737288 | tf_op jit(solution)/shard_map/ppermute | solution.py:476
  39.3 16.8 %collective-permute-start.12 = (bf16[160,768]{1,0:T(8,128)(2,1)}, bf16[160,768]{1,0:T(8,128)(2,1)}, u32[]{:S(2)}, u32[]{:S(2)}) collective-permute-start(bf16[160,768]{1,0:T(8,128)(2,1)} %get-tuple-element.58.refs_2_), channel_id=1, source_target_pairs={{0,16},{8,24},{16,0},{24,8},{1,17},{9,25},{17,1},{25,9},{2,18},{10... | collective-permute-start | bytes 737288 | tf_op jit(solution)/shard_map/ppermute | solution.py:476
  39.8 16.3 %collective-permute-start.11 = (bf16[160,768]{1,0:T(8,128)(2,1)}, bf16[160,768]{1,0:T(8,128)(2,1)}, u32[]{:S(2)}, u32[]{:S(2)}) collective-permute-start(bf16[160,768]{1,0:T(8,128)(2,1)} %get-tuple-element.58.refs_2_), channel_id=1, source_target_pairs={{0,8},{8,0},{16,24},{24,16},{1,9},{9,1},{17,25},{25,17},{2,10},{10... | collective-permute-start | bytes 737288 | tf_op jit(solution)/shard_map/ppermute | solution.py:476
  40.3 15.7 %collective-permute-start.21 = (bf16[2,40,1024]{2,1,0:T(8,128)(2,1)}, bf16[2,40,1024]{2,1,0:T(8,128)(2,1)}, u32[]{:S(2)}, u32[]{:S(2)}) collective-permute-start(bf16[2,40,1024]{2,1,0:T(8,128)(2,1)} %get-tuple-element.72), channel_id=1, source_target_pairs={{0,4},{1,5},{2,6},{3,7},{4,0},{5,1},{6,2},{7,3},{8,12},{9,13},{10,... | collective-permute-start | bytes 491528 | tf_op jit(solution)/shard_map/ppermute | solution.py:468
  42.7 13.3 %collective-permute-start.22 = (bf16[2,40,1024]{2,1,0:T(8,128)(2,1)}, bf16[2,40,1024]{2,1,0:T(8,128)(2,1)}, u32[]{:S(2)}, u32[]{:S(2)}) collective-permute-start(bf16[2,40,1024]{2,1,0:T(8,128)(2,1)} %get-tuple-element.73), channel_id=1, source_target_pairs={{0,6},{1,7},{2,4},{3,5},{4,2},{5,3},{6,0},{7,1},{8,14},{9,15},{10,... | collective-permute-start | bytes 491528 | tf_op jit(solution)/shard_map/ppermute | solution.py:468
  56.1 22.4 %all-to-all-start = ((bf16[8,40,1024]{2,1,0:T(8,128)(2,1)}), bf16[8,40,1024]{2,1,0:T(8,128)(2,1)}, u32[]{:S(2)}, u32[]{:S(2)}) async-start(bf16[8,40,1024]{2,1,0:T(8,128)(2,1)} %get-tuple-element.78), calls=%async_computation | async-start | bytes 1310720 | tf_op jit(solution)/shard_map/all_to_all | solution.py:464
  60.5 8.1 %collective-permute-start.17 = (bf16[160,512]{1,0:T(8,128)(2,1)}, bf16[160,512]{1,0:T(8,128)(2,1)}, u32[]{:S(2)}, u32[]{:S(2)}) collective-permute-start(bf16[160,512]{1,0:T(8,128)(2,1)} %get-tuple-element.66), channel_id=1, source_target_pairs={{0,8},{8,0},{16,24},{24,16},{1,9},{9,1},{17,25},{25,17},{2,10},{10... | collective-permute-start | bytes 491528 | tf_op jit(solution)/shard_map/ppermute | solution.py:476
  62.0 9.8 %collective-permute-start.18 = (bf16[160,512]{1,0:T(8,128)(2,1)}, bf16[160,512]{1,0:T(8,128)(2,1)}, u32[]{:S(2)}, u32[]{:S(2)}) collective-permute-start(bf16[160,512]{1,0:T(8,128)(2,1)} %get-tuple-element.67), channel_id=1, source_target_pairs={{0,16},{8,24},{16,0},{24,8},{1,17},{9,25},{17,1},{25,9},{2,18},{10... | collective-permute-start | bytes 491528 | tf_op jit(solution)/shard_map/ppermute | solution.py:476
  63.5 8.3 %collective-permute-start.19 = (bf16[160,512]{1,0:T(8,128)(2,1)}, bf16[160,512]{1,0:T(8,128)(2,1)}, u32[]{:S(2)}, u32[]{:S(2)}) collective-permute-start(bf16[160,512]{1,0:T(8,128)(2,1)} %get-tuple-element.68), channel_id=1, source_target_pairs={{0,24},{8,16},{16,8},{24,0},{1,25},{9,17},{17,9},{25,1},{2,26},{10... | collective-permute-start | bytes 491528 | tf_op jit(solution)/shard_map/ppermute | solution.py:476
  71.8 3.5 %collective-permute-start.23 = (bf16[128,2048]{1,0:T(8,128)(2,1)}, bf16[128,2048]{1,0:T(8,128)(2,1)}, u32[]{:S(2)}, u32[]{:S(2)}) collective-permute-start(bf16[128,2048]{1,0:T(8,128)(2,1)} %shard_map.127), channel_id=1, source_target_pairs={{0,1},{1,0},{2,3},{3,2},{4,5},{5,4},{6,7},{7,6},{8,9},{9,8},{10,11... | collective-permute-start | bytes 1572872 | tf_op jit(solution)/shard_map/ppermute | solution.py:472

commit v5 on v4

--- a/solution.py
+++ b/solution.py
@@ -14,15 +14,15 @@
 CHUNK = 8
 FF_TILE = 256
 VMEM_LIMIT = 64 * 1024 * 1024 - 65536
-AHEAD = 6
+EARLY = 1
 SLOPE = jnp.bfloat16
 TURN = 1
 JOIN = True
 TIE_O = ()
 TIE_S = True
 TIE_L = True
-TIE_P = (4,5)
-NEAR = (1,)
+TIE_P = (4,)
+NEAR = (2,)
 ORDER_C = ()
 MATE_FIRST = ()
 CHEAP = 1000000
@@ -269,10 +269,6 @@
             def step(f, carry):
                 s = e * self.per + f
 
-                @pl.when(s + AHEAD < self.steps)
-                def _():
-                    self.start(s + AHEAD)
-
                 for copy in self.copies(s):
                     copy.wait()
                 cols = pl.ds(pl.multiple_of(f * FF_TILE, FF_TILE), FF_TILE)
@@ -280,6 +276,13 @@
                 return carry
 
             lax.fori_loop(0, self.per, step, 0)
+
+
+def start_weights(refs):
+    first = next(i for i, ref in enumerate(refs) if ref.shape == refs[-4].shape)
+    weights = Weights(refs[first : first + 3], refs[-4:-1], refs[-1])
+    for s in range(EARLY):
+        weights.start(s)
 
 
 def unpack_all(x_ref, blocks, n):
@@ -298,7 +301,7 @@
     blocks, outs = Blocks(refs[:n_in], n, group), Blocks(refs[n_in : n_in + n_out], n, group)
     hidden_ref, slope_ref, silu_ref, x_ref, acc_ref, wg_ref, wu_ref, wd_ref, sems = refs[n_in + n_out :]
     weights = Weights((wg_hbm, wu_hbm, wd_hbm), (wg_ref, wu_ref, wd_ref), sems)
-    for s in range(AHEAD):
+    for s in range(EARLY, weights.steps):
         weights.start(s)
     unpack_all(x_ref, blocks, n)
     hidden_ref[...] = jnp.zeros_like(hidden_ref)
@@ -334,7 +337,7 @@
     refs = refs[n_in + n_out :]
     shares, (pull_ref, turned_ref, acc_ref, wg_ref, wu_ref, wd_ref, sems) = refs[:parts], refs[parts:]
     weights = Weights((wg_hbm, wu_hbm, wd_hbm), (wg_ref, wu_ref, wd_ref), sems)
-    for s in range(AHEAD):
+    for s in range(EARLY, weights.steps):
         weights.start(s)
     unpack_all(pull_ref, blocks, n)
     for e, (start, stop) in enumerate(windows(n)):
@@ -391,7 +394,7 @@
 HBM = pl.BlockSpec(memory_space=pltpu.HBM)
 
 
-def call(kernel, ins, outs, flops, nbytes, scratch=(), lazy=False, out_spec=VMEM):
+def call(kernel, ins, outs, flops, nbytes, scratch=(), lazy=False, early=None, out_spec=VMEM):
     arrays, specs, buffers = [], [], []
     for x, way in ins:
         if way in ("copy", "scalars", "stay"):
@@ -412,6 +415,8 @@
         copies = {i: pltpu.make_async_copy(refs[i], given[k], sems.at[k]) for k, i in enumerate(copied)}
         for copy in copies.values():
             copy.start()
+        if early is not None:
+            early(refs)
         for k, i in enumerate(copied):
             refs[i] = given[k]
         if lazy:
@@ -538,6 +543,7 @@
         expert_flops,
         weight_bytes,
         [pltpu.VMEM((rows, width), BF16), pltpu.VMEM((local, most, width), F32)] + stream,
+        early=start_weights,
     )
     mix = jax.ShapeDtypeStruct((HALVES * tok_count, total), BF16)
     mix_pair = jax.ShapeDtypeStruct((HALVES * tok_count, total // 2), BF16)
@@ -567,6 +573,7 @@
             pltpu.VMEM((local, width, most), F32),
         ]
         + stream,
+        early=start_weights,
     )
     sent_b, shares = results[: len(out_b)], results[len(out_b) :]
     all_shares = exchange_dp(shares)

time: 81.8 us -> 80.1 us (0.979)
  starting transfers between devices: 35.3 us -> 30.7 us
  waiting for transfers between devices: 4.83 us -> 8.24 us
    ppermute x13, starting transfers between devices: 22.7 us -> 18.1 us  [exchange(): lax.ppermute(values[d], 'expert', [(i, i ^ step * d) for i in range(n)])]
    ppermute x13, waiting for transfers between devices: 0.03 us -> 3.44 us  [exchange(): lax.ppermute(values[d], 'expert', [(i, i ^ step * d) for i in range(n)])]
  transfers between devices with their start and end apart: 25 -> 25, of which waited for: 3 -> 7; matrix products, arithmetic and copies ran while one was open for 0% -> 0% of each run, Pallas kernels for 43% -> 44%
where the time goes in v5:
time: 80.1 us; the launch traced here: 79.7 us
  Pallas kernels  39.8 us (50%)
  starting transfers between devices  30.7 us (38%)
  waiting for transfers between devices  8.24 us (10%)
  between operations  0.96 us (1%)
    pallas_call x9, Pallas kernels, call(): pl.pallas_call(body, out_shape=outs, in_specs=specs, out_specs=jax.tree.m...  39.8 us
    ppermute x13, starting transfers between devices, exchange(): lax.ppermute(values[d], 'expert', [(i, i ^ step * d) for i in range(n)])  18.1 us
    ppermute x6, starting transfers between devices, exchange_dp(): lax.ppermute(values[k], 'dp', [(i, i ^ k) for i in range(parts)])  7.04 us
    all_to_all x1, starting transfers between devices, exchange(): lax.all_to_all(values[0], 'expert', split_axis=0, concat_axis=0, tiled=True)  4.4 us
    ppermute x13, waiting for transfers between devices, exchange(): lax.ppermute(values[d], 'expert', [(i, i ^ step * d) for i in range(n)])  3.44 us
    ppermute x6, waiting for transfers between devices, exchange_dp(): lax.ppermute(values[k], 'dp', [(i, i ^ k) for i in range(parts)])  3.29 us
  transfers between devices with their start and end apart: 25, of which 7 were waited for; matrix products, arithmetic and copies ran while one was open for 0% of the time, Pallas kernels for 44%

profile of v5, /device:TPU:0, one launch (start us, length us, event | category | flops | bytes accessed | tf_op | source)
XLA Modules:
  0.0 79.7 jit_solution(1028140108625755122)
XLA Ops:
  0.6 2.4 %shard_map.121 = (bf16[40,1024]{1,0:T(8,128)(2,1)}, bf16[40,1024]{1,0:T(8,128)(2,1)}, bf16[40,1024]{1,0:T(8,128)(2,1)}, bf16[40,1024]{1,0:T(8,128)(2,1)}, bf16[4...) custom-call(s32[1]{0:T(128)} %bitcast.refs_0_.refs_1_, ...), custom_call_target="tpu_custom_call" | custom-call | flops 167772160 | bytes 655360 | tf_op jit(solution)/shard_map/pallas_call | solution.py:429
  3.0 0.5 collective-permute-start.4
  3.6 4.0 %collective-permute-start.7 = (bf16[40,1024]{1,0:T(8,128)(2,1)}, bf16[40,1024]{1,0:T(8,128)(2,1)}, u32[]{:S(2)}, u32[]{:S(2)}) collective-permute-start(bf16[40,1024]{1,0:T(8,128)(2,1)} %get-tuple-element.51), channel_id=1, source_target_pairs={{0,4},{1,5},{2,6},{3,7},{4,0},{5,1},{6,2},{7,3},{8,12},{9,13},{10,... | collective-permute-start | bytes 245768 | tf_op jit(solution)/shard_map/ppermute | solution.py:473
  8.1 1.0 %collective-permute-done.1 = s32[128,8]{0,1:T(8,128)} collective-permute-done((s32[128,8]{0,1:T(8,128)}, s32[128,8]{0,1:T(8,128)}, u32[]{:S(2)}, u32[]{:S(2)}) %collective-permute-start.1) | collective-permute-done | bytes 4128 | tf_op jit(solution)/shard_map/ppermute | solution.py:477
  9.3 1.5 %collective-permute-start.6 = (bf16[40,1024]{1,0:T(8,128)(2,1)}, bf16[40,1024]{1,0:T(8,128)(2,1)}, u32[]{:S(2)}, u32[]{:S(2)}) collective-permute-start(bf16[40,1024]{1,0:T(8,128)(2,1)} %get-tuple-element.50), channel_id=1, source_target_pairs={{0,3},{1,2},{2,1},{3,0},{4,7},{5,6},{6,5},{7,4},{8,11},{9,10},{10,... | collective-permute-start | bytes 245768 | tf_op jit(solution)/shard_map/ppermute | solution.py:473
  11.0 3.4 %collective-permute-start.9 = (bf16[40,1024]{1,0:T(8,128)(2,1)}, bf16[40,1024]{1,0:T(8,128)(2,1)}, u32[]{:S(2)}, u32[]{:S(2)}) collective-permute-start(bf16[40,1024]{1,0:T(8,128)(2,1)} %get-tuple-element.53), channel_id=1, source_target_pairs={{0,6},{1,7},{2,4},{3,5},{4,2},{5,3},{6,0},{7,1},{8,14},{9,15},{10,... | collective-permute-start | bytes 245768 | tf_op jit(solution)/shard_map/ppermute | solution.py:473
  14.4 2.7 %shard_map.122 = (bf16[2,40,1024]{2,1,0:T(8,128)(2,1)}, bf16[2,40,1024]{2,1,0:T(8,128)(2,1)}, bf16[2,40,1024]{2,1,0:T(8,128)(2,1)}, bf16[2,40,1024]{2,1,0:T(8,128)(2,1)}) custom-call(s32[1]{0:T(128)} %bitcast.refs_0_.refs_1_, s32[16]{0:T(128)} %refs_0_.7, s32[8,128]{1,0:T(8,128)} %bitcast.9, s32[8,128]{1,0:T(8,128)} %bitcast.19, f32[8,128]{1,0:T(8,128)} %bitcast.14, ...), custom_call_target="tpu_custom_call" | custom-call | flops 167772160 | bytes 655360 | tf_op jit(solution)/shard_map/pallas_call | solution.py:429
  17.2 2.0 %collective-permute-start.14 = (bf16[2,40,1024]{2,1,0:T(8,128)(2,1)}, bf16[2,40,1024]{2,1,0:T(8,128)(2,1)}, u32[]{:S(2)}, u32[]{:S(2)}) collective-permute-start(bf16[2,40,1024]{2,1,0:T(8,128)(2,1)} %get-tuple-element.62), channel_id=1, source_target_pairs={{0,2},{1,3},{2,0},{3,1},{4,6},{5,7},{6,4},{7,5},{8,10},{9,11},{10,... | collective-permute-start | bytes 491528 | tf_op jit(solution)/shard_map/ppermute | solution.py:473
  19.2 0.8 %collective-permute-done.8.refs_11_ = bf16[40,1024]{1,0:T(8,128)(2,1)} collective-permute-done((bf16[40,1024]{1,0:T(8,128)(2,1)}, bf16[40,1024]{1,0:T(8,128)(2,1)}, u32[]{:S(2)}, u32[]{:S(2)}) %collective-permute-start.8) | collective-permute-done | bytes 81952 | tf_op jit(solution)/shard_map/ppermute | solution.py:473
  20.0 1.2 %collective-permute-start.15 = (bf16[2,40,1024]{2,1,0:T(8,128)(2,1)}, bf16[2,40,1024]{2,1,0:T(8,128)(2,1)}, u32[]{:S(2)}, u32[]{:S(2)}) collective-permute-start(bf16[2,40,1024]{2,1,0:T(8,128)(2,1)} %get-tuple-element.63), channel_id=1, source_target_pairs={{0,4},{1,5},{2,6},{3,7},{4,0},{5,1},{6,2},{7,3},{8,12},{9,13},{10,... | collective-permute-start | bytes 491528 | tf_op jit(solution)/shard_map/ppermute | solution.py:473
  21.3 1.4 %collective-permute-start.16 = (bf16[2,40,1024]{2,1,0:T(8,128)(2,1)}, bf16[2,40,1024]{2,1,0:T(8,128)(2,1)}, u32[]{:S(2)}, u32[]{:S(2)}) collective-permute-start(bf16[2,40,1024]{2,1,0:T(8,128)(2,1)} %get-tuple-element.64), channel_id=1, source_target_pairs={{0,6},{1,7},{2,4},{3,5},{4,2},{5,3},{6,0},{7,1},{8,14},{9,15},{10,... | collective-permute-start | bytes 491528 | tf_op jit(solution)/shard_map/ppermute | solution.py:473
  22.7 1.2 %collective-permute-done.10.refs_13_ = bf16[40,1024]{1,0:T(8,128)(2,1)} collective-permute-done((bf16[40,1024]{1,0:T(8,128)(2,1)}, bf16[40,1024]{1,0:T(8,128)(2,1)}, u32[]{:S(2)}, u32[]{:S(2)}) %collective-permute-start.10) | collective-permute-done | bytes 81952 | tf_op jit(solution)/shard_map/ppermute | solution.py:473
  23.9 0.7 collective-permute-done.5.refs_8_
  24.5 9.6 %shard_map.123 = (bf16[2,40,1024]{2,1,0:T(8,128)(2,1)}, bf16[2,40,1024]{2,1,0:T(8,128)(2,1)}, bf16[2,40,1024]{2,1,0:T(8,128)(2,1)}, bf16[2,40,1024]{2,1,0:T(8,12...) custom-call(s32[16]{0:T(128)} %refs_0_.7, s32[1]{0:T(128)} %bitcast.refs_0_.refs_1_, ...), custom_call_target="tpu_custom_call" | custom-call | flops 3019898880 | bytes 18874368 | tf_op jit(solution)/shard_map/pallas_call | solution.py:429
  34.2 1.4 %collective-permute-start.20 = (bf16[2,40,1024]{2,1,0:T(8,128)(2,1)}, bf16[2,40,1024]{2,1,0:T(8,128)(2,1)}, u32[]{:S(2)}, u32[]{:S(2)}) collective-permute-start(bf16[2,40,1024]{2,1,0:T(8,128)(2,1)} %get-tuple-element.71), channel_id=1, source_target_pairs={{0,2},{1,3},{2,0},{3,1},{4,6},{5,7},{6,4},{7,5},{8,10},{9,11},{10,... | collective-permute-start | bytes 491528 | tf_op jit(solution)/shard_map/ppermute | solution.py:473
  35.6 2.4 %collective-permute-start.13 = (bf16[160,768]{1,0:T(8,128)(2,1)}, bf16[160,768]{1,0:T(8,128)(2,1)}, u32[]{:S(2)}, u32[]{:S(2)}) collective-permute-start(bf16[160,768]{1,0:T(8,128)(2,1)} %get-tuple-element.58.refs_2_), channel_id=1, source_target_pairs={{0,24},{8,16},{16,8},{24,0},{1,25},{9,17},{17,9},{25,1},{2,26},{10... | collective-permute-start | bytes 737288 | tf_op jit(solution)/shard_map/ppermute | solution.py:481
  38.0 0.5 collective-permute-start.12
  38.6 0.5 collective-permute-start.11
  39.1 1.0 %collective-permute-start.21 = (bf16[2,40,1024]{2,1,0:T(8,128)(2,1)}, bf16[2,40,1024]{2,1,0:T(8,128)(2,1)}, u32[]{:S(2)}, u32[]{:S(2)}) collective-permute-start(bf16[2,40,1024]{2,1,0:T(8,128)(2,1)} %get-tuple-element.72), channel_id=1, source_target_pairs={{0,4},{1,5},{2,6},{3,7},{4,0},{5,1},{6,2},{7,3},{8,12},{9,13},{10,... | collective-permute-start | bytes 491528 | tf_op jit(solution)/shard_map/ppermute | solution.py:473
  40.1 0.8 collective-permute-done.20.refs_3_.refs_8_
  40.9 1.7 %collective-permute-start.22 = (bf16[2,40,1024]{2,1,0:T(8,128)(2,1)}, bf16[2,40,1024]{2,1,0:T(8,128)(2,1)}, u32[]{:S(2)}, u32[]{:S(2)}) collective-permute-start(bf16[2,40,1024]{2,1,0:T(8,128)(2,1)} %get-tuple-element.73), channel_id=1, source_target_pairs={{0,6},{1,7},{2,4},{3,5},{4,2},{5,3},{6,0},{7,1},{8,14},{9,15},{10,... | collective-permute-start | bytes 491528 | tf_op jit(solution)/shard_map/ppermute | solution.py:473
  42.6 11.8 %shard_map.125 = (bf16[8,40,1024]{2,1,0:T(8,128)(2,1)}, bf16[160,512]{1,0:T(8,128)(2,1)}, bf16[160,512]{1,0:T(8,128)(2,1)}, bf16[160,512]{1,0:T(8,128)(2,1)}, bf16[160,512]{1,0:T(8,128)(2,1)}) custom-call(s32[16]{0:T(128)} %refs_0_.7, s32[1]{0:T(128)} %bitcast.refs_0_.refs_1_, s32[1]{0:T(128)} %bitcast.7.refs_2_, bf16[16,2048]{1,0:T(8,128)(2,1)} %refs_3_.7, ...), custom_call_target="tpu_custom_call" | custom-call | flops 3019898880 | bytes 18874368 | tf_op jit(solution)/shard_map/pallas_call | solution.py:429
  54.5 4.4 %all-to-all-start = ((bf16[8,40,1024]{2,1,0:T(8,128)(2,1)}), bf16[8,40,1024]{2,1,0:T(8,128)(2,1)}, u32[]{:S(2)}, u32[]{:S(2)}) async-start(bf16[8,40,1024]{2,1,0:T(8,128)(2,1)} %get-tuple-element.78), calls=%async_computation | async-start | bytes 1310720 | tf_op jit(solution)/shard_map/all_to_all | solution.py:469
  58.9 1.6 %collective-permute-start.17 = (bf16[160,512]{1,0:T(8,128)(2,1)}, bf16[160,512]{1,0:T(8,128)(2,1)}, u32[]{:S(2)}, u32[]{:S(2)}) collective-permute-start(bf16[160,512]{1,0:T(8,128)(2,1)} %get-tuple-element.66), channel_id=1, source_target_pairs={{0,8},{8,0},{16,24},{24,16},{1,9},{9,1},{17,25},{25,17},{2,10},{10... | collective-permute-start | bytes 491528 | tf_op jit(solution)/shard_map/ppermute | solution.py:481
  60.4 1.5 %collective-permute-start.18 = (bf16[160,512]{1,0:T(8,128)(2,1)}, bf16[160,512]{1,0:T(8,128)(2,1)}, u32[]{:S(2)}, u32[]{:S(2)}) collective-permute-start(bf16[160,512]{1,0:T(8,128)(2,1)} %get-tuple-element.67), channel_id=1, source_target_pairs={{0,16},{8,24},{16,0},{24,8},{1,17},{9,25},{17,1},{25,9},{2,18},{10... | collective-permute-start | bytes 491528 | tf_op jit(solution)/shard_map/ppermute | solution.py:481
  62.4 2.1 %shard_map.124 = (bf16[256,320]{1,0:T(8,128)(2,1)}, bf16[256,160]{1,0:T(8,128)(2,1)}, bf16[256,160]{1,0:T(8,128)(2,1)}) custom-call(s32[16]{0:T(128)} %refs_0_.7, s32[1]{0:T(128)} %bitcast.refs_0_.refs_1_, s32[8,128]{1,0:T(8,128)} %bitcast.10, s32[8,128]{1,0:T(8,128)} %bitcast.20, f32[8,128]{1,0:T(8,128)} %bitcast.15, s32[8,128]{1,0:T(8,128)} %bitcast.4.refs_6_.refs_5_, ...), custom_call_target="tpu_custom_call" | custom-call | tf_op jit(solution)/shard_map/pallas_call | solution.py:429
  64.6 2.3 %shard_map.127 = bf16[128,2048]{1,0:T(8,128)(2,1)} custom-call(s32[1]{0:T(128)} %bitcast.refs_0_.refs_1_, bf16[256,160]{1,0:T(8,128)(2,1)} %get-tuple-element.70.refs_1_, bf16[2,40,1024]{2,1,0:T(8,128)(2,1)} %get-tuple-element.55.refs_2_.refs_7_, bf16[2,40,1024]{2,1,0:T(8,128)(2,1)} %collective-permute-done.20.refs_3_.refs_8_, ...), custom_call_target="tpu_custom_call" | custom-call | flops 83 | tf_op jit(solution)/shard_map/pallas_call | solution.py:429
  67.0 3.3 %collective-permute-done.18.refs_8_ = bf16[160,512]{1,0:T(8,128)(2,1)} collective-permute-done((bf16[160,512]{1,0:T(8,128)(2,1)}, bf16[160,512]{1,0:T(8,128)(2,1)}, u32[]{:S(2)}, u32[]{:S(2)}) %collective-permute-start.18) | collective-permute-done | bytes 163872 | tf_op jit(solution)/shard_map/ppermute | solution.py:481
  70.2 3.5 %shard_map.126 = bf16[2,768,512]{2,1,0:T(8,128)(2,1)} custom-call(s32[16]{0:T(128)} %refs_0_.7, s32[1]{0:T(128)} %bitcast.refs_0_.refs_1_, bf16[160,768]{1,0:T(8,128)(2,1)} %get-tuple-element.58.refs_2_, bf16[160,768]{1,0:T(8,128)(2,1)} %collective-permute-done.11.refs_3_, bf16[160,768]{1,0:T(8,128)(2,1)} %collective-permute-done.12.refs_4_, ...), custom_call_target="tpu_custom_call" | custom-call | flops 1006632960 | bytes 1638400 | tf_op jit(solution)/shard_map/pallas_call | solution.py:429
  73.7 2.6 %shard_map.128 = bf16[128,2048]{1,0:T(8,128)(2,1)} custom-call(s32[1]{0:T(128)} %bitcast.refs_0_.refs_1_, s32[8,128]{1,0:T(8,128)} %bitcast.11, f32[8,128]{1,0:T(8,128)} %bitcast.16, bf16[16,2048]{1,0:T(8,128)(2,1)} %refs_3_.7, bf16[128,2048]{1,0:T(8,128)(2,1)} %refs_4_.6, bf16[256,160]{1,0:T(8,128)(2,1)} %get-tuple-element.69.refs_5_, ...), custom_call_target="tpu_custom_call" | custom-call | flops 167 | tf_op jit(solution)/shard_map/pallas_call | solution.py:429
  76.4 0.5 all-to-all-done.refs_6_
  76.9 2.7 %shard_map.129 = bf16[128,2048]{1,0:T(8,128)(2,1)} custom-call(s32[1]{0:T(128)} %bitcast.refs_0_.refs_1_, s32[8,128]{1,0:T(8,128)} %bitcast.12, f32[8,128]{1,0:T(8,128)} %bitcast.17, bf16[16,2048]{1,0:T(8,128)(2,1)} %refs_3_.7, bf16[128,2048]{1,0:T(8,128)(2,1)} %refs_4_.7, bf16[256,320]{1,0:T(8,128)(2,1)} %get-tuple-element.76.refs_5_, ...), custom_call_target="tpu_custom_call" | custom-call | flops 167 | tf_op jit(solution)/shard_map/pallas_call | solution.py:429
  (27 shorter events, 1.6 us)
Async XLA Ops:
  3.0 8.0 %collective-permute-start.4 = (bf16[128,2048]{1,0:T(8,128)(2,1)}, bf16[128,2048]{1,0:T(8,128)(2,1)}, u32[]{:S(2)}, u32[]{:S(2)}) collective-permute-start(bf16[128,2048]{1,0:T(8,128)(2,1)} %refs_4_.7), channel_id=1, source_target_pairs={{0,1},{1,0},{2,3},{3,2},{4,5},{5,4},{6,7},{7,6},{8,9},{9,8},{10,11... | collective-permute-start | bytes 1572872 | tf_op jit(solution)/shard_map/ppermute | solution.py:477
  3.5 13.5 %collective-permute-start = (bf16[40,1024]{1,0:T(8,128)(2,1)}, bf16[40,1024]{1,0:T(8,128)(2,1)}, u32[]{:S(2)}, u32[]{:S(2)}) collective-permute-start(bf16[40,1024]{1,0:T(8,128)(2,1)} %get-tuple-element.42), channel_id=1, source_target_pairs={{0,1},{1,0},{2,3},{3,2},{4,5},{5,4},{6,7},{7,6},{8,9},{9,8},{10,11... | collective-permute-start | bytes 245768 | tf_op jit(solution)/shard_map/ppermute | solution.py:473
  3.6 13.6 %collective-permute-start.7 = (bf16[40,1024]{1,0:T(8,128)(2,1)}, bf16[40,1024]{1,0:T(8,128)(2,1)}, u32[]{:S(2)}, u32[]{:S(2)}) collective-permute-start(bf16[40,1024]{1,0:T(8,128)(2,1)} %get-tuple-element.51), channel_id=1, source_target_pairs={{0,4},{1,5},{2,6},{3,7},{4,0},{5,1},{6,2},{7,3},{8,12},{9,13},{10,... | collective-permute-start | bytes 245768 | tf_op jit(solution)/shard_map/ppermute | solution.py:473
  7.6 1.5 %collective-permute-start.1 = (s32[128,8]{0,1:T(8,128)}, s32[128,8]{0,1:T(8,128)}, u32[]{:S(2)}, u32[]{:S(2)}) collective-permute-start(s32[128,8]{0,1:T(8,128)} %param.11), channel_id=1, source_target_pairs={{0,1},{1,0},{2,3},{3,2},{4,5},{5,4},{6,7},{7,6},{8,9},{9,8},{10,11... | collective-permute-start | bytes 12296 | tf_op jit(solution)/shard_map/ppermute | solution.py:477
  7.6 1.7 %collective-permute-start.2 = (s32[128,8]{0,1:T(8,128)}, s32[128,8]{0,1:T(8,128)}, u32[]{:S(2)}, u32[]{:S(2)}) collective-permute-start(s32[128,8]{0,1:T(8,128)} %param.12), channel_id=1, source_target_pairs={{0,1},{1,0},{2,3},{3,2},{4,5},{5,4},{6,7},{7,6},{8,9},{9,8},{10,11... | collective-permute-start | bytes 12296 | tf_op jit(solution)/shard_map/ppermute | solution.py:477
  9.1 1.7 %collective-permute-start.3 = (f32[128,8]{0,1:T(8,128)}, f32[128,8]{0,1:T(8,128)}, u32[]{:S(2)}, u32[]{:S(2)}) collective-permute-start(f32[128,8]{0,1:T(8,128)} %param.13), channel_id=1, source_target_pairs={{0,1},{1,0},{2,3},{3,2},{4,5},{5,4},{6,7},{7,6},{8,9},{9,8},{10,11... | collective-permute-start | bytes 12296 | tf_op jit(solution)/shard_map/ppermute | solution.py:477
  9.3 7.9 %collective-permute-start.6 = (bf16[40,1024]{1,0:T(8,128)(2,1)}, bf16[40,1024]{1,0:T(8,128)(2,1)}, u32[]{:S(2)}, u32[]{:S(2)}) collective-permute-start(bf16[40,1024]{1,0:T(8,128)(2,1)} %get-tuple-element.50), channel_id=1, source_target_pairs={{0,3},{1,2},{2,1},{3,0},{4,7},{5,6},{6,5},{7,4},{8,11},{9,10},{10,... | collective-permute-start | bytes 245768 | tf_op jit(solution)/shard_map/ppermute | solution.py:473
  10.8 9.2 %collective-permute-start.8 = (bf16[40,1024]{1,0:T(8,128)(2,1)}, bf16[40,1024]{1,0:T(8,128)(2,1)}, u32[]{:S(2)}, u32[]{:S(2)}) collective-permute-start(bf16[40,1024]{1,0:T(8,128)(2,1)} %get-tuple-element.52), channel_id=1, source_target_pairs={{0,5},{1,4},{2,7},{3,6},{4,1},{5,0},{6,3},{7,2},{8,13},{9,12},{10,... | collective-permute-start | bytes 245768 | tf_op jit(solution)/shard_map/ppermute | solution.py:473
  11.0 10.3 %collective-permute-start.9 = (bf16[40,1024]{1,0:T(8,128)(2,1)}, bf16[40,1024]{1,0:T(8,128)(2,1)}, u32[]{:S(2)}, u32[]{:S(2)}) collective-permute-start(bf16[40,1024]{1,0:T(8,128)(2,1)} %get-tuple-element.53), channel_id=1, source_target_pairs={{0,6},{1,7},{2,4},{3,5},{4,2},{5,3},{6,0},{7,1},{8,14},{9,15},{10,... | collective-permute-start | bytes 245768 | tf_op jit(solution)/shard_map/ppermute | solution.py:473
  17.0 6.8 %collective-permute-start.10 = (bf16[40,1024]{1,0:T(8,128)(2,1)}, bf16[40,1024]{1,0:T(8,128)(2,1)}, u32[]{:S(2)}, u32[]{:S(2)}) collective-permute-start(bf16[40,1024]{1,0:T(8,128)(2,1)} %get-tuple-element.54), channel_id=1, source_target_pairs={{0,7},{1,6},{2,5},{3,4},{4,3},{5,2},{6,1},{7,0},{8,15},{9,14},{10,... | collective-permute-start | bytes 245768 | tf_op jit(solution)/shard_map/ppermute | solution.py:473
  17.2 7.3 %collective-permute-start.5 = (bf16[40,1024]{1,0:T(8,128)(2,1)}, bf16[40,1024]{1,0:T(8,128)(2,1)}, u32[]{:S(2)}, u32[]{:S(2)}) collective-permute-start(bf16[40,1024]{1,0:T(8,128)(2,1)} %get-tuple-element.49), channel_id=1, source_target_pairs={{0,2},{1,3},{2,0},{3,1},{4,6},{5,7},{6,4},{7,5},{8,10},{9,11},{10,... | collective-permute-start | bytes 245768 | tf_op jit(solution)/shard_map/ppermute | solution.py:473
  17.2 20.8 %collective-permute-start.14 = (bf16[2,40,1024]{2,1,0:T(8,128)(2,1)}, bf16[2,40,1024]{2,1,0:T(8,128)(2,1)}, u32[]{:S(2)}, u32[]{:S(2)}) collective-permute-start(bf16[2,40,1024]{2,1,0:T(8,128)(2,1)} %get-tuple-element.62), channel_id=1, source_target_pairs={{0,2},{1,3},{2,0},{3,1},{4,6},{5,7},{6,4},{7,5},{8,10},{9,11},{10,... | collective-permute-start | bytes 491528 | tf_op jit(solution)/shard_map/ppermute | solution.py:473
  20.0 18.5 %collective-permute-start.15 = (bf16[2,40,1024]{2,1,0:T(8,128)(2,1)}, bf16[2,40,1024]{2,1,0:T(8,128)(2,1)}, u32[]{:S(2)}, u32[]{:S(2)}) collective-permute-start(bf16[2,40,1024]{2,1,0:T(8,128)(2,1)} %get-tuple-element.63), channel_id=1, source_target_pairs={{0,4},{1,5},{2,6},{3,7},{4,0},{5,1},{6,2},{7,3},{8,12},{9,13},{10,... | collective-permute-start | bytes 491528 | tf_op jit(solution)/shard_map/ppermute | solution.py:473
  21.3 17.8 %collective-permute-start.16 = (bf16[2,40,1024]{2,1,0:T(8,128)(2,1)}, bf16[2,40,1024]{2,1,0:T(8,128)(2,1)}, u32[]{:S(2)}, u32[]{:S(2)}) collective-permute-start(bf16[2,40,1024]{2,1,0:T(8,128)(2,1)} %get-tuple-element.64), channel_id=1, source_target_pairs={{0,6},{1,7},{2,4},{3,5},{4,2},{5,3},{6,0},{7,1},{8,14},{9,15},{10,... | collective-permute-start | bytes 491528 | tf_op jit(solution)/shard_map/ppermute | solution.py:473
  34.2 6.7 %collective-permute-start.20 = (bf16[2,40,1024]{2,1,0:T(8,128)(2,1)}, bf16[2,40,1024]{2,1,0:T(8,128)(2,1)}, u32[]{:S(2)}, u32[]{:S(2)}) collective-permute-start(bf16[2,40,1024]{2,1,0:T(8,128)(2,1)} %get-tuple-element.71), channel_id=1, source_target_pairs={{0,2},{1,3},{2,0},{3,1},{4,6},{5,7},{6,4},{7,5},{8,10},{9,11},{10,... | collective-permute-start | bytes 491528 | tf_op jit(solution)/shard_map/ppermute | solution.py:473
  35.6 18.9 %collective-permute-start.13 = (bf16[160,768]{1,0:T(8,128)(2,1)}, bf16[160,768]{1,0:T(8,128)(2,1)}, u32[]{:S(2)}, u32[]{:S(2)}) collective-permute-start(bf16[160,768]{1,0:T(8,128)(2,1)} %get-tuple-element.58.refs_2_), channel_id=1, source_target_pairs={{0,24},{8,16},{16,8},{24,0},{1,25},{9,17},{17,9},{25,1},{2,26},{10... | collective-permute-start | bytes 737288 | tf_op jit(solution)/shard_map/ppermute | solution.py:481
  38.0 16.4 %collective-permute-start.12 = (bf16[160,768]{1,0:T(8,128)(2,1)}, bf16[160,768]{1,0:T(8,128)(2,1)}, u32[]{:S(2)}, u32[]{:S(2)}) collective-permute-start(bf16[160,768]{1,0:T(8,128)(2,1)} %get-tuple-element.58.refs_2_), channel_id=1, source_target_pairs={{0,16},{8,24},{16,0},{24,8},{1,17},{9,25},{17,1},{25,9},{2,18},{10... | collective-permute-start | bytes 737288 | tf_op jit(solution)/shard_map/ppermute | solution.py:481
  38.6 15.9 %collective-permute-start.11 = (bf16[160,768]{1,0:T(8,128)(2,1)}, bf16[160,768]{1,0:T(8,128)(2,1)}, u32[]{:S(2)}, u32[]{:S(2)}) collective-permute-start(bf16[160,768]{1,0:T(8,128)(2,1)} %get-tuple-element.58.refs_2_), channel_id=1, source_target_pairs={{0,8},{8,0},{16,24},{24,16},{1,9},{9,1},{17,25},{25,17},{2,10},{10... | collective-permute-start | bytes 737288 | tf_op jit(solution)/shard_map/ppermute | solution.py:481
  39.1 15.3 %collective-permute-start.21 = (bf16[2,40,1024]{2,1,0:T(8,128)(2,1)}, bf16[2,40,1024]{2,1,0:T(8,128)(2,1)}, u32[]{:S(2)}, u32[]{:S(2)}) collective-permute-start(bf16[2,40,1024]{2,1,0:T(8,128)(2,1)} %get-tuple-element.72), channel_id=1, source_target_pairs={{0,4},{1,5},{2,6},{3,7},{4,0},{5,1},{6,2},{7,3},{8,12},{9,13},{10,... | collective-permute-start | bytes 491528 | tf_op jit(solution)/shard_map/ppermute | solution.py:473
  40.9 13.5 %collective-permute-start.22 = (bf16[2,40,1024]{2,1,0:T(8,128)(2,1)}, bf16[2,40,1024]{2,1,0:T(8,128)(2,1)}, u32[]{:S(2)}, u32[]{:S(2)}) collective-permute-start(bf16[2,40,1024]{2,1,0:T(8,128)(2,1)} %get-tuple-element.73), channel_id=1, source_target_pairs={{0,6},{1,7},{2,4},{3,5},{4,2},{5,3},{6,0},{7,1},{8,14},{9,15},{10,... | collective-permute-start | bytes 491528 | tf_op jit(solution)/shard_map/ppermute | solution.py:473
  54.5 22.4 %all-to-all-start = ((bf16[8,40,1024]{2,1,0:T(8,128)(2,1)}), bf16[8,40,1024]{2,1,0:T(8,128)(2,1)}, u32[]{:S(2)}, u32[]{:S(2)}) async-start(bf16[8,40,1024]{2,1,0:T(8,128)(2,1)} %get-tuple-element.78), calls=%async_computation | async-start | bytes 1310720 | tf_op jit(solution)/shard_map/all_to_all | solution.py:469
  58.9 8.1 %collective-permute-start.17 = (bf16[160,512]{1,0:T(8,128)(2,1)}, bf16[160,512]{1,0:T(8,128)(2,1)}, u32[]{:S(2)}, u32[]{:S(2)}) collective-permute-start(bf16[160,512]{1,0:T(8,128)(2,1)} %get-tuple-element.66), channel_id=1, source_target_pairs={{0,8},{8,0},{16,24},{24,16},{1,9},{9,1},{17,25},{25,17},{2,10},{10... | collective-permute-start | bytes 491528 | tf_op jit(solution)/shard_map/ppermute | solution.py:481
  60.4 9.8 %collective-permute-start.18 = (bf16[160,512]{1,0:T(8,128)(2,1)}, bf16[160,512]{1,0:T(8,128)(2,1)}, u32[]{:S(2)}, u32[]{:S(2)}) collective-permute-start(bf16[160,512]{1,0:T(8,128)(2,1)} %get-tuple-element.67), channel_id=1, source_target_pairs={{0,16},{8,24},{16,0},{24,8},{1,17},{9,25},{17,1},{25,9},{2,18},{10... | collective-permute-start | bytes 491528 | tf_op jit(solution)/shard_map/ppermute | solution.py:481
  62.0 8.3 %collective-permute-start.19 = (bf16[160,512]{1,0:T(8,128)(2,1)}, bf16[160,512]{1,0:T(8,128)(2,1)}, u32[]{:S(2)}, u32[]{:S(2)}) collective-permute-start(bf16[160,512]{1,0:T(8,128)(2,1)} %get-tuple-element.68), channel_id=1, source_target_pairs={{0,24},{8,16},{16,8},{24,0},{1,25},{9,17},{17,9},{25,1},{2,26},{10... | collective-permute-start | bytes 491528 | tf_op jit(solution)/shard_map/ppermute | solution.py:481
  70.2 3.5 %collective-permute-start.23 = (bf16[128,2048]{1,0:T(8,128)(2,1)}, bf16[128,2048]{1,0:T(8,128)(2,1)}, u32[]{:S(2)}, u32[]{:S(2)}) collective-permute-start(bf16[128,2048]{1,0:T(8,128)(2,1)} %shard_map.127), channel_id=1, source_target_pairs={{0,1},{1,0},{2,3},{3,2},{4,5},{5,4},{6,7},{7,6},{8,9},{9,8},{10,11... | collective-permute-start | bytes 1572872 | tf_op jit(solution)/shard_map/ppermute | solution.py:477

commit v6 on v5

--- a/solution.py
+++ b/solution.py
@@ -335,9 +335,9 @@
     group = group_ref[0]
     blocks, outs = Blocks(refs[:n_in], n, group), Blocks(refs[n_in : n_in + n_out], n, group)
     refs = refs[n_in + n_out :]
-    shares, (pull_ref, turned_ref, acc_ref, wg_ref, wu_ref, wd_ref, sems) = refs[:parts], refs[parts:]
+    shares, (pull_ref, turned_ref, acc_ref, share_sems, wg_ref, wu_ref, wd_ref, sems) = refs[:parts], refs[parts:]
     weights = Weights((wg_hbm, wu_hbm, wd_hbm), (wg_ref, wu_ref, wd_ref), sems)
-    for s in range(EARLY, weights.steps):
+    for s in range(weights.steps):
         weights.start(s)
     unpack_all(pull_ref, blocks, n)
     for e, (start, stop) in enumerate(windows(n)):
@@ -350,9 +350,11 @@
             turned_ref[e] = pull.T.astype(BF16)
             acc_ref[e] = -(own_scale(scale_ref, group, e) * pull).T
     width = pull_ref.shape[1] // parts
+    sends = []
     for k, share in enumerate(shares):
         start = pl.multiple_of((dp_ref[0] ^ k) * width, width)
-        share[...] = pull_ref[:, pl.ds(start, width)]
+        sends.append(pltpu.make_async_copy(pull_ref.at[:, pl.ds(start, width)], share, share_sems.at[k]))
+        sends[-1].start()
 
     def body(e, cols, wg, wu, wd):
         d_hidden = mm(wd[...], turned_ref[e])
@@ -369,6 +371,8 @@
     sums = [acc_ref[e].astype(BF16) for e in range(2)]
     for c in range(0, n, size):
         outs.store(c, pack_windows(sums, n, c, size, counts_ref, group, NT))
+    for send in sends:
+        send.wait()
 
 
 def grad_kernel(n, parts, counts_ref, group_ref, *refs):
@@ -430,7 +434,7 @@
         body,
         out_shape=outs,
         in_specs=specs,
-        out_specs=jax.tree.map(lambda _: out_spec, outs),
+        out_specs=out_spec if isinstance(out_spec, list) else jax.tree.map(lambda _: out_spec, outs),
         scratch_shapes=list(scratch) + buffers,
         compiler_params=pltpu.CompilerParams(vmem_limit_bytes=VMEM_LIMIT),
         cost_estimate=pl.CostEstimate(flops=flops, bytes_accessed=nbytes, transcendentals=0),
@@ -571,9 +575,10 @@
             pltpu.VMEM((rows, width), BF16),
             pltpu.VMEM((local, width, most), BF16),
             pltpu.VMEM((local, width, most), F32),
+            pltpu.SemaphoreType.DMA((parts,)),
         ]
         + stream,
-        early=start_weights,
+        out_spec=[VMEM] * len(out_b) + [HBM] * parts,
     )
     sent_b, shares = results[: len(out_b)], results[len(out_b) :]
     all_shares = exchange_dp(shares)

time: 80.1 us -> 80.1 us (level)
  no operation moved by 1% of the time
where the time goes in v6:
time: 80.1 us; the launch traced here: 79.7 us
  Pallas kernels  39.7 us (50%)
  starting transfers between devices  30.7 us (38%)
  waiting for transfers between devices  8.24 us (10%)
  between operations  0.96 us (1%)
    pallas_call x9, Pallas kernels, call(): pl.pallas_call(body, out_shape=outs, in_specs=specs, out_specs=out_spec i...  39.7 us
    ppermute x13, starting transfers between devices, exchange(): lax.ppermute(values[d], 'expert', [(i, i ^ step * d) for i in range(n)])  18.1 us
    ppermute x6, starting transfers between devices, exchange_dp(): lax.ppermute(values[k], 'dp', [(i, i ^ k) for i in range(parts)])  7.04 us
    all_to_all x1, starting transfers between devices, exchange(): lax.all_to_all(values[0], 'expert', split_axis=0, concat_axis=0, tiled=True)  4.4 us
    ppermute x13, waiting for transfers between devices, exchange(): lax.ppermute(values[d], 'expert', [(i, i ^ step * d) for i in range(n)])  3.44 us
    ppermute x6, waiting for transfers between devices, exchange_dp(): lax.ppermute(values[k], 'dp', [(i, i ^ k) for i in range(parts)])  3.28 us
  transfers between devices with their start and end apart: 25, of which 7 were waited for; matrix products, arithmetic and copies ran while one was open for 0% of the time, Pallas kernels for 44%

profile of v6, /device:TPU:0, one launch (start us, length us, event | category | flops | bytes accessed | tf_op | source)
XLA Modules:
  0.0 79.7 jit_solution(498088818764255741)
XLA Ops:
  0.6 2.4 %shard_map.121 = (bf16[40,1024]{1,0:T(8,128)(2,1)}, bf16[40,1024]{1,0:T(8,128)(2,1)}, bf16[40,1024]{1,0:T(8,128)(2,1)}, bf16[40,1024]{1,0:T(8,128)(2,1)}, bf16[4...) custom-call(s32[1]{0:T(128)} %bitcast.refs_0_.refs_1_, ...), custom_call_target="tpu_custom_call" | custom-call | flops 167772160 | bytes 655360 | tf_op jit(solution)/shard_map/pallas_call | solution.py:433
  3.0 0.5 collective-permute-start.4
  3.6 4.0 %collective-permute-start.7 = (bf16[40,1024]{1,0:T(8,128)(2,1)}, bf16[40,1024]{1,0:T(8,128)(2,1)}, u32[]{:S(2)}, u32[]{:S(2)}) collective-permute-start(bf16[40,1024]{1,0:T(8,128)(2,1)} %get-tuple-element.51), channel_id=1, source_target_pairs={{0,4},{1,5},{2,6},{3,7},{4,0},{5,1},{6,2},{7,3},{8,12},{9,13},{10,... | collective-permute-start | bytes 245768 | tf_op jit(solution)/shard_map/ppermute | solution.py:477
  8.1 1.0 %collective-permute-done.1 = s32[128,8]{0,1:T(8,128)} collective-permute-done((s32[128,8]{0,1:T(8,128)}, s32[128,8]{0,1:T(8,128)}, u32[]{:S(2)}, u32[]{:S(2)}) %collective-permute-start.1) | collective-permute-done | bytes 4128 | tf_op jit(solution)/shard_map/ppermute | solution.py:481
  9.3 1.5 %collective-permute-start.6 = (bf16[40,1024]{1,0:T(8,128)(2,1)}, bf16[40,1024]{1,0:T(8,128)(2,1)}, u32[]{:S(2)}, u32[]{:S(2)}) collective-permute-start(bf16[40,1024]{1,0:T(8,128)(2,1)} %get-tuple-element.50), channel_id=1, source_target_pairs={{0,3},{1,2},{2,1},{3,0},{4,7},{5,6},{6,5},{7,4},{8,11},{9,10},{10,... | collective-permute-start | bytes 245768 | tf_op jit(solution)/shard_map/ppermute | solution.py:477
  11.0 3.4 %collective-permute-start.9 = (bf16[40,1024]{1,0:T(8,128)(2,1)}, bf16[40,1024]{1,0:T(8,128)(2,1)}, u32[]{:S(2)}, u32[]{:S(2)}) collective-permute-start(bf16[40,1024]{1,0:T(8,128)(2,1)} %get-tuple-element.53), channel_id=1, source_target_pairs={{0,6},{1,7},{2,4},{3,5},{4,2},{5,3},{6,0},{7,1},{8,14},{9,15},{10,... | collective-permute-start | bytes 245768 | tf_op jit(solution)/shard_map/ppermute | solution.py:477
  14.4 2.7 %shard_map.122 = (bf16[2,40,1024]{2,1,0:T(8,128)(2,1)}, bf16[2,40,1024]{2,1,0:T(8,128)(2,1)}, bf16[2,40,1024]{2,1,0:T(8,128)(2,1)}, bf16[2,40,1024]{2,1,0:T(8,128)(2,1)}) custom-call(s32[1]{0:T(128)} %bitcast.refs_0_.refs_1_, s32[16]{0:T(128)} %refs_0_.7, s32[8,128]{1,0:T(8,128)} %bitcast.9, s32[8,128]{1,0:T(8,128)} %bitcast.19, f32[8,128]{1,0:T(8,128)} %bitcast.14, ...), custom_call_target="tpu_custom_call" | custom-call | flops 167772160 | bytes 655360 | tf_op jit(solution)/shard_map/pallas_call | solution.py:433
  17.2 2.0 %collective-permute-start.14 = (bf16[2,40,1024]{2,1,0:T(8,128)(2,1)}, bf16[2,40,1024]{2,1,0:T(8,128)(2,1)}, u32[]{:S(2)}, u32[]{:S(2)}) collective-permute-start(bf16[2,40,1024]{2,1,0:T(8,128)(2,1)} %get-tuple-element.62), channel_id=1, source_target_pairs={{0,2},{1,3},{2,0},{3,1},{4,6},{5,7},{6,4},{7,5},{8,10},{9,11},{10,... | collective-permute-start | bytes 491528 | tf_op jit(solution)/shard_map/ppermute | solution.py:477
  19.2 0.8 %collective-permute-done.8.refs_11_ = bf16[40,1024]{1,0:T(8,128)(2,1)} collective-permute-done((bf16[40,1024]{1,0:T(8,128)(2,1)}, bf16[40,1024]{1,0:T(8,128)(2,1)}, u32[]{:S(2)}, u32[]{:S(2)}) %collective-permute-start.8) | collective-permute-done | bytes 81952 | tf_op jit(solution)/shard_map/ppermute | solution.py:477
  20.0 1.2 %collective-permute-start.15 = (bf16[2,40,1024]{2,1,0:T(8,128)(2,1)}, bf16[2,40,1024]{2,1,0:T(8,128)(2,1)}, u32[]{:S(2)}, u32[]{:S(2)}) collective-permute-start(bf16[2,40,1024]{2,1,0:T(8,128)(2,1)} %get-tuple-element.63), channel_id=1, source_target_pairs={{0,4},{1,5},{2,6},{3,7},{4,0},{5,1},{6,2},{7,3},{8,12},{9,13},{10,... | collective-permute-start | bytes 491528 | tf_op jit(solution)/shard_map/ppermute | solution.py:477
  21.3 1.4 %collective-permute-start.16 = (bf16[2,40,1024]{2,1,0:T(8,128)(2,1)}, bf16[2,40,1024]{2,1,0:T(8,128)(2,1)}, u32[]{:S(2)}, u32[]{:S(2)}) collective-permute-start(bf16[2,40,1024]{2,1,0:T(8,128)(2,1)} %get-tuple-element.64), channel_id=1, source_target_pairs={{0,6},{1,7},{2,4},{3,5},{4,2},{5,3},{6,0},{7,1},{8,14},{9,15},{10,... | collective-permute-start | bytes 491528 | tf_op jit(solution)/shard_map/ppermute | solution.py:477
  22.7 1.2 %collective-permute-done.10.refs_13_ = bf16[40,1024]{1,0:T(8,128)(2,1)} collective-permute-done((bf16[40,1024]{1,0:T(8,128)(2,1)}, bf16[40,1024]{1,0:T(8,128)(2,1)}, u32[]{:S(2)}, u32[]{:S(2)}) %collective-permute-start.10) | collective-permute-done | bytes 81952 | tf_op jit(solution)/shard_map/ppermute | solution.py:477
  23.9 0.7 collective-permute-done.5.refs_8_
  24.5 9.6 %shard_map.123 = (bf16[2,40,1024]{2,1,0:T(8,128)(2,1)}, bf16[2,40,1024]{2,1,0:T(8,128)(2,1)}, bf16[2,40,1024]{2,1,0:T(8,128)(2,1)}, bf16[2,40,1024]{2,1,0:T(8,12...) custom-call(s32[16]{0:T(128)} %refs_0_.7, s32[1]{0:T(128)} %bitcast.refs_0_.refs_1_, ...), custom_call_target="tpu_custom_call" | custom-call | flops 3019898880 | bytes 18874368 | tf_op jit(solution)/shard_map/pallas_call | solution.py:433
  34.2 1.4 %collective-permute-start.20 = (bf16[2,40,1024]{2,1,0:T(8,128)(2,1)}, bf16[2,40,1024]{2,1,0:T(8,128)(2,1)}, u32[]{:S(2)}, u32[]{:S(2)}) collective-permute-start(bf16[2,40,1024]{2,1,0:T(8,128)(2,1)} %get-tuple-element.71), channel_id=1, source_target_pairs={{0,2},{1,3},{2,0},{3,1},{4,6},{5,7},{6,4},{7,5},{8,10},{9,11},{10,... | collective-permute-start | bytes 491528 | tf_op jit(solution)/shard_map/ppermute | solution.py:477
  35.6 2.4 %collective-permute-start.13 = (bf16[160,768]{1,0:T(8,128)(2,1)}, bf16[160,768]{1,0:T(8,128)(2,1)}, u32[]{:S(2)}, u32[]{:S(2)}) collective-permute-start(bf16[160,768]{1,0:T(8,128)(2,1)} %get-tuple-element.58.refs_2_), channel_id=1, source_target_pairs={{0,24},{8,16},{16,8},{24,0},{1,25},{9,17},{17,9},{25,1},{2,26},{10... | collective-permute-start | bytes 737288 | tf_op jit(solution)/shard_map/ppermute | solution.py:485
  38.0 0.5 collective-permute-start.12
  38.6 0.5 collective-permute-start.11
  39.1 1.0 %collective-permute-start.21 = (bf16[2,40,1024]{2,1,0:T(8,128)(2,1)}, bf16[2,40,1024]{2,1,0:T(8,128)(2,1)}, u32[]{:S(2)}, u32[]{:S(2)}) collective-permute-start(bf16[2,40,1024]{2,1,0:T(8,128)(2,1)} %get-tuple-element.72), channel_id=1, source_target_pairs={{0,4},{1,5},{2,6},{3,7},{4,0},{5,1},{6,2},{7,3},{8,12},{9,13},{10,... | collective-permute-start | bytes 491528 | tf_op jit(solution)/shard_map/ppermute | solution.py:477
  40.1 0.8 collective-permute-done.20.refs_3_.refs_8_
  40.9 1.7 %collective-permute-start.22 = (bf16[2,40,1024]{2,1,0:T(8,128)(2,1)}, bf16[2,40,1024]{2,1,0:T(8,128)(2,1)}, u32[]{:S(2)}, u32[]{:S(2)}) collective-permute-start(bf16[2,40,1024]{2,1,0:T(8,128)(2,1)} %get-tuple-element.73), channel_id=1, source_target_pairs={{0,6},{1,7},{2,4},{3,5},{4,2},{5,3},{6,0},{7,1},{8,14},{9,15},{10,... | collective-permute-start | bytes 491528 | tf_op jit(solution)/shard_map/ppermute | solution.py:477
  42.6 11.8 %shard_map.125 = (bf16[8,40,1024]{2,1,0:T(8,128)(2,1)}, bf16[160,512]{1,0:T(8,128)(2,1)}, bf16[160,512]{1,0:T(8,128)(2,1)}, bf16[160,512]{1,0:T(8,128)(2,1)}, bf16[160,512]{1,0:T(8,128)(2,1)}) custom-call(s32[16]{0:T(128)} %refs_0_.7, s32[1]{0:T(128)} %bitcast.refs_0_.refs_1_, s32[1]{0:T(128)} %bitcast.7.refs_2_, bf16[16,2048]{1,0:T(8,128)(2,1)} %refs_3_.7, ...), custom_call_target="tpu_custom_call" | custom-call | flops 3019898880 | bytes 18874368 | tf_op jit(solution)/shard_map/pallas_call | solution.py:433
  54.4 4.4 %all-to-all-start = ((bf16[8,40,1024]{2,1,0:T(8,128)(2,1)}), bf16[8,40,1024]{2,1,0:T(8,128)(2,1)}, u32[]{:S(2)}, u32[]{:S(2)}) async-start(bf16[8,40,1024]{2,1,0:T(8,128)(2,1)} %get-tuple-element.78), calls=%async_computation | async-start | bytes 1310720 | tf_op jit(solution)/shard_map/all_to_all | solution.py:473
  58.8 1.6 %collective-permute-start.17 = (bf16[160,512]{1,0:T(8,128)(2,1)}, bf16[160,512]{1,0:T(8,128)(2,1)}, u32[]{:S(2)}, u32[]{:S(2)}) collective-permute-start(bf16[160,512]{1,0:T(8,128)(2,1)} %get-tuple-element.66), channel_id=1, source_target_pairs={{0,8},{8,0},{16,24},{24,16},{1,9},{9,1},{17,25},{25,17},{2,10},{10... | collective-permute-start | bytes 491528 | tf_op jit(solution)/shard_map/ppermute | solution.py:485
  60.4 1.5 %collective-permute-start.18 = (bf16[160,512]{1,0:T(8,128)(2,1)}, bf16[160,512]{1,0:T(8,128)(2,1)}, u32[]{:S(2)}, u32[]{:S(2)}) collective-permute-start(bf16[160,512]{1,0:T(8,128)(2,1)} %get-tuple-element.67), channel_id=1, source_target_pairs={{0,16},{8,24},{16,0},{24,8},{1,17},{9,25},{17,1},{25,9},{2,18},{10... | collective-permute-start | bytes 491528 | tf_op jit(solution)/shard_map/ppermute | solution.py:485
  62.4 2.1 %shard_map.124 = (bf16[256,320]{1,0:T(8,128)(2,1)}, bf16[256,160]{1,0:T(8,128)(2,1)}, bf16[256,160]{1,0:T(8,128)(2,1)}) custom-call(s32[16]{0:T(128)} %refs_0_.7, s32[1]{0:T(128)} %bitcast.refs_0_.refs_1_, s32[8,128]{1,0:T(8,128)} %bitcast.10, s32[8,128]{1,0:T(8,128)} %bitcast.20, f32[8,128]{1,0:T(8,128)} %bitcast.15, s32[8,128]{1,0:T(8,128)} %bitcast.4.refs_6_.refs_5_, ...), custom_call_target="tpu_custom_call" | custom-call | tf_op jit(solution)/shard_map/pallas_call | solution.py:433
  64.5 2.3 %shard_map.127 = bf16[128,2048]{1,0:T(8,128)(2,1)} custom-call(s32[1]{0:T(128)} %bitcast.refs_0_.refs_1_, bf16[256,160]{1,0:T(8,128)(2,1)} %get-tuple-element.70.refs_1_, bf16[2,40,1024]{2,1,0:T(8,128)(2,1)} %get-tuple-element.55.refs_2_.refs_7_, bf16[2,40,1024]{2,1,0:T(8,128)(2,1)} %collective-permute-done.20.refs_3_.refs_8_, ...), custom_call_target="tpu_custom_call" | custom-call | flops 83 | tf_op jit(solution)/shard_map/pallas_call | solution.py:433
  66.9 3.3 %collective-permute-done.18.refs_8_ = bf16[160,512]{1,0:T(8,128)(2,1)} collective-permute-done((bf16[160,512]{1,0:T(8,128)(2,1)}, bf16[160,512]{1,0:T(8,128)(2,1)}, u32[]{:S(2)}, u32[]{:S(2)}) %collective-permute-start.18) | collective-permute-done | bytes 163872 | tf_op jit(solution)/shard_map/ppermute | solution.py:485
  70.2 3.5 %shard_map.126 = bf16[2,768,512]{2,1,0:T(8,128)(2,1)} custom-call(s32[16]{0:T(128)} %refs_0_.7, s32[1]{0:T(128)} %bitcast.refs_0_.refs_1_, bf16[160,768]{1,0:T(8,128)(2,1)} %get-tuple-element.58.refs_2_, bf16[160,768]{1,0:T(8,128)(2,1)} %collective-permute-done.11.refs_3_, bf16[160,768]{1,0:T(8,128)(2,1)} %collective-permute-done.12.refs_4_, ...), custom_call_target="tpu_custom_call" | custom-call | flops 1006632960 | bytes 1638400 | tf_op jit(solution)/shard_map/pallas_call | solution.py:433
  73.7 2.6 %shard_map.128 = bf16[128,2048]{1,0:T(8,128)(2,1)} custom-call(s32[1]{0:T(128)} %bitcast.refs_0_.refs_1_, s32[8,128]{1,0:T(8,128)} %bitcast.11, f32[8,128]{1,0:T(8,128)} %bitcast.16, bf16[16,2048]{1,0:T(8,128)(2,1)} %refs_3_.7, bf16[128,2048]{1,0:T(8,128)(2,1)} %refs_4_.6, bf16[256,160]{1,0:T(8,128)(2,1)} %get-tuple-element.69.refs_5_, ...), custom_call_target="tpu_custom_call" | custom-call | flops 167 | tf_op jit(solution)/shard_map/pallas_call | solution.py:433
  76.3 0.5 all-to-all-done.refs_6_
  76.8 2.7 %shard_map.129 = bf16[128,2048]{1,0:T(8,128)(2,1)} custom-call(s32[1]{0:T(128)} %bitcast.refs_0_.refs_1_, s32[8,128]{1,0:T(8,128)} %bitcast.12, f32[8,128]{1,0:T(8,128)} %bitcast.17, bf16[16,2048]{1,0:T(8,128)(2,1)} %refs_3_.7, bf16[128,2048]{1,0:T(8,128)(2,1)} %refs_4_.7, bf16[256,320]{1,0:T(8,128)(2,1)} %get-tuple-element.76.refs_5_, ...), custom_call_target="tpu_custom_call" | custom-call | flops 167 | tf_op jit(solution)/shard_map/pallas_call | solution.py:433
  (27 shorter events, 1.6 us)
Async XLA Ops:
  3.0 8.0 %collective-permute-start.4 = (bf16[128,2048]{1,0:T(8,128)(2,1)}, bf16[128,2048]{1,0:T(8,128)(2,1)}, u32[]{:S(2)}, u32[]{:S(2)}) collective-permute-start(bf16[128,2048]{1,0:T(8,128)(2,1)} %refs_4_.7), channel_id=1, source_target_pairs={{0,1},{1,0},{2,3},{3,2},{4,5},{5,4},{6,7},{7,6},{8,9},{9,8},{10,11... | collective-permute-start | bytes 1572872 | tf_op jit(solution)/shard_map/ppermute | solution.py:481
  3.5 13.5 %collective-permute-start = (bf16[40,1024]{1,0:T(8,128)(2,1)}, bf16[40,1024]{1,0:T(8,128)(2,1)}, u32[]{:S(2)}, u32[]{:S(2)}) collective-permute-start(bf16[40,1024]{1,0:T(8,128)(2,1)} %get-tuple-element.42), channel_id=1, source_target_pairs={{0,1},{1,0},{2,3},{3,2},{4,5},{5,4},{6,7},{7,6},{8,9},{9,8},{10,11... | collective-permute-start | bytes 245768 | tf_op jit(solution)/shard_map/ppermute | solution.py:477
  3.6 13.6 %collective-permute-start.7 = (bf16[40,1024]{1,0:T(8,128)(2,1)}, bf16[40,1024]{1,0:T(8,128)(2,1)}, u32[]{:S(2)}, u32[]{:S(2)}) collective-permute-start(bf16[40,1024]{1,0:T(8,128)(2,1)} %get-tuple-element.51), channel_id=1, source_target_pairs={{0,4},{1,5},{2,6},{3,7},{4,0},{5,1},{6,2},{7,3},{8,12},{9,13},{10,... | collective-permute-start | bytes 245768 | tf_op jit(solution)/shard_map/ppermute | solution.py:477
  7.6 1.5 %collective-permute-start.1 = (s32[128,8]{0,1:T(8,128)}, s32[128,8]{0,1:T(8,128)}, u32[]{:S(2)}, u32[]{:S(2)}) collective-permute-start(s32[128,8]{0,1:T(8,128)} %param.11), channel_id=1, source_target_pairs={{0,1},{1,0},{2,3},{3,2},{4,5},{5,4},{6,7},{7,6},{8,9},{9,8},{10,11... | collective-permute-start | bytes 12296 | tf_op jit(solution)/shard_map/ppermute | solution.py:481
  7.6 1.7 %collective-permute-start.2 = (s32[128,8]{0,1:T(8,128)}, s32[128,8]{0,1:T(8,128)}, u32[]{:S(2)}, u32[]{:S(2)}) collective-permute-start(s32[128,8]{0,1:T(8,128)} %param.12), channel_id=1, source_target_pairs={{0,1},{1,0},{2,3},{3,2},{4,5},{5,4},{6,7},{7,6},{8,9},{9,8},{10,11... | collective-permute-start | bytes 12296 | tf_op jit(solution)/shard_map/ppermute | solution.py:481
  9.1 1.7 %collective-permute-start.3 = (f32[128,8]{0,1:T(8,128)}, f32[128,8]{0,1:T(8,128)}, u32[]{:S(2)}, u32[]{:S(2)}) collective-permute-start(f32[128,8]{0,1:T(8,128)} %param.13), channel_id=1, source_target_pairs={{0,1},{1,0},{2,3},{3,2},{4,5},{5,4},{6,7},{7,6},{8,9},{9,8},{10,11... | collective-permute-start | bytes 12296 | tf_op jit(solution)/shard_map/ppermute | solution.py:481
  9.3 7.9 %collective-permute-start.6 = (bf16[40,1024]{1,0:T(8,128)(2,1)}, bf16[40,1024]{1,0:T(8,128)(2,1)}, u32[]{:S(2)}, u32[]{:S(2)}) collective-permute-start(bf16[40,1024]{1,0:T(8,128)(2,1)} %get-tuple-element.50), channel_id=1, source_target_pairs={{0,3},{1,2},{2,1},{3,0},{4,7},{5,6},{6,5},{7,4},{8,11},{9,10},{10,... | collective-permute-start | bytes 245768 | tf_op jit(solution)/shard_map/ppermute | solution.py:477
  10.8 9.2 %collective-permute-start.8 = (bf16[40,1024]{1,0:T(8,128)(2,1)}, bf16[40,1024]{1,0:T(8,128)(2,1)}, u32[]{:S(2)}, u32[]{:S(2)}) collective-permute-start(bf16[40,1024]{1,0:T(8,128)(2,1)} %get-tuple-element.52), channel_id=1, source_target_pairs={{0,5},{1,4},{2,7},{3,6},{4,1},{5,0},{6,3},{7,2},{8,13},{9,12},{10,... | collective-permute-start | bytes 245768 | tf_op jit(solution)/shard_map/ppermute | solution.py:477
  11.0 10.3 %collective-permute-start.9 = (bf16[40,1024]{1,0:T(8,128)(2,1)}, bf16[40,1024]{1,0:T(8,128)(2,1)}, u32[]{:S(2)}, u32[]{:S(2)}) collective-permute-start(bf16[40,1024]{1,0:T(8,128)(2,1)} %get-tuple-element.53), channel_id=1, source_target_pairs={{0,6},{1,7},{2,4},{3,5},{4,2},{5,3},{6,0},{7,1},{8,14},{9,15},{10,... | collective-permute-start | bytes 245768 | tf_op jit(solution)/shard_map/ppermute | solution.py:477
  17.0 6.8 %collective-permute-start.10 = (bf16[40,1024]{1,0:T(8,128)(2,1)}, bf16[40,1024]{1,0:T(8,128)(2,1)}, u32[]{:S(2)}, u32[]{:S(2)}) collective-permute-start(bf16[40,1024]{1,0:T(8,128)(2,1)} %get-tuple-element.54), channel_id=1, source_target_pairs={{0,7},{1,6},{2,5},{3,4},{4,3},{5,2},{6,1},{7,0},{8,15},{9,14},{10,... | collective-permute-start | bytes 245768 | tf_op jit(solution)/shard_map/ppermute | solution.py:477
  17.2 7.3 %collective-permute-start.5 = (bf16[40,1024]{1,0:T(8,128)(2,1)}, bf16[40,1024]{1,0:T(8,128)(2,1)}, u32[]{:S(2)}, u32[]{:S(2)}) collective-permute-start(bf16[40,1024]{1,0:T(8,128)(2,1)} %get-tuple-element.49), channel_id=1, source_target_pairs={{0,2},{1,3},{2,0},{3,1},{4,6},{5,7},{6,4},{7,5},{8,10},{9,11},{10,... | collective-permute-start | bytes 245768 | tf_op jit(solution)/shard_map/ppermute | solution.py:477
  17.2 20.8 %collective-permute-start.14 = (bf16[2,40,1024]{2,1,0:T(8,128)(2,1)}, bf16[2,40,1024]{2,1,0:T(8,128)(2,1)}, u32[]{:S(2)}, u32[]{:S(2)}) collective-permute-start(bf16[2,40,1024]{2,1,0:T(8,128)(2,1)} %get-tuple-element.62), channel_id=1, source_target_pairs={{0,2},{1,3},{2,0},{3,1},{4,6},{5,7},{6,4},{7,5},{8,10},{9,11},{10,... | collective-permute-start | bytes 491528 | tf_op jit(solution)/shard_map/ppermute | solution.py:477
  20.0 18.5 %collective-permute-start.15 = (bf16[2,40,1024]{2,1,0:T(8,128)(2,1)}, bf16[2,40,1024]{2,1,0:T(8,128)(2,1)}, u32[]{:S(2)}, u32[]{:S(2)}) collective-permute-start(bf16[2,40,1024]{2,1,0:T(8,128)(2,1)} %get-tuple-element.63), channel_id=1, source_target_pairs={{0,4},{1,5},{2,6},{3,7},{4,0},{5,1},{6,2},{7,3},{8,12},{9,13},{10,... | collective-permute-start | bytes 491528 | tf_op jit(solution)/shard_map/ppermute | solution.py:477
  21.3 17.8 %collective-permute-start.16 = (bf16[2,40,1024]{2,1,0:T(8,128)(2,1)}, bf16[2,40,1024]{2,1,0:T(8,128)(2,1)}, u32[]{:S(2)}, u32[]{:S(2)}) collective-permute-start(bf16[2,40,1024]{2,1,0:T(8,128)(2,1)} %get-tuple-element.64), channel_id=1, source_target_pairs={{0,6},{1,7},{2,4},{3,5},{4,2},{5,3},{6,0},{7,1},{8,14},{9,15},{10,... | collective-permute-start | bytes 491528 | tf_op jit(solution)/shard_map/ppermute | solution.py:477
  34.2 6.7 %collective-permute-start.20 = (bf16[2,40,1024]{2,1,0:T(8,128)(2,1)}, bf16[2,40,1024]{2,1,0:T(8,128)(2,1)}, u32[]{:S(2)}, u32[]{:S(2)}) collective-permute-start(bf16[2,40,1024]{2,1,0:T(8,128)(2,1)} %get-tuple-element.71), channel_id=1, source_target_pairs={{0,2},{1,3},{2,0},{3,1},{4,6},{5,7},{6,4},{7,5},{8,10},{9,11},{10,... | collective-permute-start | bytes 491528 | tf_op jit(solution)/shard_map/ppermute | solution.py:477
  35.6 18.8 %collective-permute-start.13 = (bf16[160,768]{1,0:T(8,128)(2,1)}, bf16[160,768]{1,0:T(8,128)(2,1)}, u32[]{:S(2)}, u32[]{:S(2)}) collective-permute-start(bf16[160,768]{1,0:T(8,128)(2,1)} %get-tuple-element.58.refs_2_), channel_id=1, source_target_pairs={{0,24},{8,16},{16,8},{24,0},{1,25},{9,17},{17,9},{25,1},{2,26},{10... | collective-permute-start | bytes 737288 | tf_op jit(solution)/shard_map/ppermute | solution.py:485
  38.0 16.4 %collective-permute-start.12 = (bf16[160,768]{1,0:T(8,128)(2,1)}, bf16[160,768]{1,0:T(8,128)(2,1)}, u32[]{:S(2)}, u32[]{:S(2)}) collective-permute-start(bf16[160,768]{1,0:T(8,128)(2,1)} %get-tuple-element.58.refs_2_), channel_id=1, source_target_pairs={{0,16},{8,24},{16,0},{24,8},{1,17},{9,25},{17,1},{25,9},{2,18},{10... | collective-permute-start | bytes 737288 | tf_op jit(solution)/shard_map/ppermute | solution.py:485
  38.6 15.9 %collective-permute-start.11 = (bf16[160,768]{1,0:T(8,128)(2,1)}, bf16[160,768]{1,0:T(8,128)(2,1)}, u32[]{:S(2)}, u32[]{:S(2)}) collective-permute-start(bf16[160,768]{1,0:T(8,128)(2,1)} %get-tuple-element.58.refs_2_), channel_id=1, source_target_pairs={{0,8},{8,0},{16,24},{24,16},{1,9},{9,1},{17,25},{25,17},{2,10},{10... | collective-permute-start | bytes 737288 | tf_op jit(solution)/shard_map/ppermute | solution.py:485
  39.1 15.3 %collective-permute-start.21 = (bf16[2,40,1024]{2,1,0:T(8,128)(2,1)}, bf16[2,40,1024]{2,1,0:T(8,128)(2,1)}, u32[]{:S(2)}, u32[]{:S(2)}) collective-permute-start(bf16[2,40,1024]{2,1,0:T(8,128)(2,1)} %get-tuple-element.72), channel_id=1, source_target_pairs={{0,4},{1,5},{2,6},{3,7},{4,0},{5,1},{6,2},{7,3},{8,12},{9,13},{10,... | collective-permute-start | bytes 491528 | tf_op jit(solution)/shard_map/ppermute | solution.py:477
  40.9 13.5 %collective-permute-start.22 = (bf16[2,40,1024]{2,1,0:T(8,128)(2,1)}, bf16[2,40,1024]{2,1,0:T(8,128)(2,1)}, u32[]{:S(2)}, u32[]{:S(2)}) collective-permute-start(bf16[2,40,1024]{2,1,0:T(8,128)(2,1)} %get-tuple-element.73), channel_id=1, source_target_pairs={{0,6},{1,7},{2,4},{3,5},{4,2},{5,3},{6,0},{7,1},{8,14},{9,15},{10,... | collective-permute-start | bytes 491528 | tf_op jit(solution)/shard_map/ppermute | solution.py:477
  54.4 22.4 %all-to-all-start = ((bf16[8,40,1024]{2,1,0:T(8,128)(2,1)}), bf16[8,40,1024]{2,1,0:T(8,128)(2,1)}, u32[]{:S(2)}, u32[]{:S(2)}) async-start(bf16[8,40,1024]{2,1,0:T(8,128)(2,1)} %get-tuple-element.78), calls=%async_computation | async-start | bytes 1310720 | tf_op jit(solution)/shard_map/all_to_all | solution.py:473
  58.8 8.1 %collective-permute-start.17 = (bf16[160,512]{1,0:T(8,128)(2,1)}, bf16[160,512]{1,0:T(8,128)(2,1)}, u32[]{:S(2)}, u32[]{:S(2)}) collective-permute-start(bf16[160,512]{1,0:T(8,128)(2,1)} %get-tuple-element.66), channel_id=1, source_target_pairs={{0,8},{8,0},{16,24},{24,16},{1,9},{9,1},{17,25},{25,17},{2,10},{10... | collective-permute-start | bytes 491528 | tf_op jit(solution)/shard_map/ppermute | solution.py:485
  60.4 9.8 %collective-permute-start.18 = (bf16[160,512]{1,0:T(8,128)(2,1)}, bf16[160,512]{1,0:T(8,128)(2,1)}, u32[]{:S(2)}, u32[]{:S(2)}) collective-permute-start(bf16[160,512]{1,0:T(8,128)(2,1)} %get-tuple-element.67), channel_id=1, source_target_pairs={{0,16},{8,24},{16,0},{24,8},{1,17},{9,25},{17,1},{25,9},{2,18},{10... | collective-permute-start | bytes 491528 | tf_op jit(solution)/shard_map/ppermute | solution.py:485
  61.9 8.3 %collective-permute-start.19 = (bf16[160,512]{1,0:T(8,128)(2,1)}, bf16[160,512]{1,0:T(8,128)(2,1)}, u32[]{:S(2)}, u32[]{:S(2)}) collective-permute-start(bf16[160,512]{1,0:T(8,128)(2,1)} %get-tuple-element.68), channel_id=1, source_target_pairs={{0,24},{8,16},{16,8},{24,0},{1,25},{9,17},{17,9},{25,1},{2,26},{10... | collective-permute-start | bytes 491528 | tf_op jit(solution)/shard_map/ppermute | solution.py:485
  70.2 3.5 %collective-permute-start.23 = (bf16[128,2048]{1,0:T(8,128)(2,1)}, bf16[128,2048]{1,0:T(8,128)(2,1)}, u32[]{:S(2)}, u32[]{:S(2)}) collective-permute-start(bf16[128,2048]{1,0:T(8,128)(2,1)} %shard_map.127), channel_id=1, source_target_pairs={{0,1},{1,0},{2,3},{3,2},{4,5},{5,4},{6,7},{7,6},{8,9},{9,8},{10,11... | collective-permute-start | bytes 1572872 | tf_op jit(solution)/shard_map/ppermute | solution.py:481
